TPU v7x, 32 devices: a whole 2x2x4 slice. The times are simulated.
32 devices in a mesh: dp: 8 (over z, y), fsdp: 4 (over x, core).
Axes of the slice: x: 2, y: 2, z: 4, core: 2. Of those that a mesh axis runs over, the one named last changes fastest.
Arguments:
- tokens: bfloat16 [512, 128, 768], P(('dp', 'fsdp')), may hold values from -6 to 6
- input_weight: bfloat16 [768, 2304], P(('dp', 'fsdp')), may hold values from -0.21875 to 0.21875
- query_bias: bfloat16 [768], P(('dp', 'fsdp')), may hold values from -1.75 to 1.75
- value_bias: bfloat16 [768], P(('dp', 'fsdp')), may hold values from -1.75 to 1.75
- output_weight: bfloat16 [768, 768], P(('dp', 'fsdp')), may hold values from -0.875 to 0.875
- output_bias: bfloat16 [768], P(('dp', 'fsdp')), may hold values from -1.75 to 1.75
- first_gain: bfloat16 [768], P(('dp', 'fsdp')), may hold values from 0.5 to 1.5
- first_shift: bfloat16 [768], P(('dp', 'fsdp')), may hold values from -1.75 to 1.75
- up_weight: bfloat16 [768, 3072], P(('dp', 'fsdp')), may hold values from -0.21875 to 0.21875
- up_bias: bfloat16 [3072], P(('dp', 'fsdp')), may hold values from -1.75 to 1.75
- down_weight: bfloat16 [3072, 768], P(('dp', 'fsdp')), may hold values from -0.109375 to 0.109375
- down_bias: bfloat16 [768], P(('dp', 'fsdp')), may hold values from -1.75 to 1.75
- second_gain: bfloat16 [768], P(('dp', 'fsdp')), may hold values from 0.5 to 1.5
- second_shift: bfloat16 [768], P(('dp', 'fsdp')), may hold values from -1.75 to 1.75
- student_weight: bfloat16 [768, 128], P(('dp', 'fsdp')), may hold values from -0.21875 to 0.21875
- student_bias: bfloat16 [128], P(('dp', 'fsdp')), may hold values from -1.75 to 1.75
- pool_query: bfloat16 [128], P(('dp', 'fsdp')), may hold values from -12 to 12
- pool_weight: bfloat16 [128, 128], P(('dp', 'fsdp')), may hold values from -0.5 to 0.5
- pool_bias: bfloat16 [128], P(('dp', 'fsdp')), may hold values from -1.75 to 1.75
- class_weight: bfloat16 [128, 14], P(('dp', 'fsdp')), may hold values from -0.5 to 0.5
- class_bias: bfloat16 [14], replicated, may hold values from -3 to 3
- lengths: int32 [512], P(('dp', 'fsdp')), may hold values from 1 to 128, 40960 in all
- exit_layer: int32 [512], P(('dp', 'fsdp')), may hold values from 6 to 9
- destination: int32 [512], replicated, may hold values from 0 to 511, as said below
- repacked_grad: bfloat16 [512, 128, 768], P(('dp', 'fsdp')), may hold values from -6 to 6
- logits_grad: bfloat16 [512, 14], P(('dp', 'fsdp')), may hold values from -6 to 6
Outputs:
- repacked: bfloat16 [512, 128, 768], P(('dp', 'fsdp'))
- student_logits: float32 [512, 14], P(('dp', 'fsdp'))
- tokens_grad: float32 [512, 128, 768], P(('dp', 'fsdp'))
- input_weight_grad: float32 [768, 2304], P(('dp', 'fsdp'))
- query_bias_grad: float32 [768], P(('dp', 'fsdp'))
- value_bias_grad: float32 [768], P(('dp', 'fsdp'))
- output_weight_grad: float32 [768, 768], P(('dp', 'fsdp'))
- output_bias_grad: float32 [768], P(('dp', 'fsdp'))
- first_gain_grad: float32 [768], P(('dp', 'fsdp'))
- first_shift_grad: float32 [768], P(('dp', 'fsdp'))
- up_weight_grad: float32 [768, 3072], P(('dp', 'fsdp'))
- up_bias_grad: float32 [3072], P(('dp', 'fsdp'))
- down_weight_grad: float32 [3072, 768], P(('dp', 'fsdp'))
- down_bias_grad: float32 [768], P(('dp', 'fsdp'))
- second_gain_grad: float32 [768], P(('dp', 'fsdp'))
- second_shift_grad: float32 [768], P(('dp', 'fsdp'))
- student_weight_grad: float32 [768, 128], P(('dp', 'fsdp'))
- student_bias_grad: float32 [128], P(('dp', 'fsdp'))
- pool_query_grad: float32 [128], P(('dp', 'fsdp'))
- pool_weight_grad: float32 [128, 128], P(('dp', 'fsdp'))
- pool_bias_grad: float32 [128], P(('dp', 'fsdp'))
- class_weight_grad: float32 [128, 14], P(('dp', 'fsdp'))
- class_bias_grad: float32 [14], replicated
Inputs may be any that keep to these rules, and one draw needn't show every extreme that they name: destination is a permutation of 0 to 511 that keeps every sample inside its aligned block of 16 times (devices along fsdp) samples; of the 16 samples of one device at most 6 go to any one device, and in every draw some device sends exactly 6 to some device.
All inputs are finite; a program needn't handle non-finite values. No bound on the sum of `lengths` on one device may be relied on, other than what follows from the above.
Results may differ from a plain program's by a relative error of at most 0.025.
Values may be sent and summed in bfloat16 or wider, within the bound.
No kernel may reach another device: no remote copies, remote signals or barrier semaphores. Data moves between devices by JAX's collectives and lax.ppermute only.
A program may use at most 320 MiB of HBM per device.

v0:
```python
import math

import jax
import jax.numpy as jnp
from jax import lax
from jax.sharding import PartitionSpec as P

HEADS = 12
HEAD_DIM = 64
STU_HEADS = 2
MICRO = 2
LAYER = 6


EPS = 1e-06
MASKED = -1e30
EXACT = lax.Precision.HIGHEST


def matmul(left, right):
    return jnp.dot(left, right, preferred_element_type=jnp.float32)


def matmul_left(left, right):
    return lax.dot_general(
        left, right, (((0,), (0,)), ((), ())), preferred_element_type=jnp.float32
    )


def matmul_right(left, right):
    return lax.dot_general(
        left, right, (((1,), (1,)), ((), ())), preferred_element_type=jnp.float32
    )


def column_sum(matrix):
    return jnp.sum(matrix.astype(jnp.float32), axis=0)


def rounded(values):
    return lax.optimization_barrier(values.astype(jnp.bfloat16)).astype(jnp.float32)


def normalize(total, gain, shift):
    mean = jnp.mean(total, axis=-1, keepdims=True)
    centered = total - mean
    scaling = lax.rsqrt(jnp.mean(centered * centered, axis=-1, keepdims=True) + EPS)
    normed = centered * scaling
    return (normed * gain + shift, normed, scaling)


def normalize_back(cotangent, normed, scaling, gain):
    scaled = cotangent * gain
    inner = (
        scaled
        - jnp.mean(scaled, axis=-1, keepdims=True)
        - normed * jnp.mean(scaled * normed, axis=-1, keepdims=True)
    )
    return (scaling * inner, jnp.sum(cotangent * normed, axis=0), jnp.sum(cotangent, axis=0))


def head_view(matrix, count, positions):
    return matrix.reshape(count, positions, HEADS, HEAD_DIM)


def masked_scores(query, key, valid):
    scores = jnp.einsum("bqhd,bkhd->bhqk", query, key, preferred_element_type=jnp.float32) * (
        1.0 / math.sqrt(HEAD_DIM)
    )
    return jnp.where(valid[:, None, None, :], scores, MASKED)


def forward_batch(tokens_part, length_part, weights):
    (
        input_weight,
        query_bias,
        value_bias,
        output_weight,
        output_bias,
        first_gain,
        first_shift,
        up_weight,
        up_bias,
        down_weight,
        down_bias,
        second_gain,
        second_shift,
        student_weight,
        student_bias,
        pool_query,
        pool_weight,
        pool_bias,
        class_weight,
    ) = weights
    count, positions, width = tokens_part.shape
    rows = tokens_part.reshape(count * positions, width)
    projected = matmul(rows, input_weight)
    query = (projected[:, :width] + query_bias.astype(jnp.float32)).astype(jnp.bfloat16)
    key = projected[:, width : 2 * width].astype(jnp.bfloat16)
    value = (projected[:, 2 * width :] + value_bias.astype(jnp.float32)).astype(jnp.bfloat16)
    valid = jnp.arange(positions, dtype=jnp.int32)[None, :] < length_part[:, None]
    scores = masked_scores(
        head_view(query, count, positions), head_view(key, count, positions), valid
    )
    peak = jnp.max(scores, axis=-1, keepdims=True)
    log_total = peak + jnp.log(jnp.sum(jnp.exp(scores - peak), axis=-1, keepdims=True))
    softened = jnp.exp(scores - log_total).astype(jnp.bfloat16)
    mixed = jnp.einsum(
        "bhqk,bkhd->bqhd",
        softened,
        head_view(value, count, positions),
        preferred_element_type=jnp.float32,
    )
    mixed = mixed.reshape(count * positions, width).astype(jnp.bfloat16)
    attended = matmul(mixed, output_weight) + output_bias.astype(jnp.float32)
    first, normed_one, scaling_one = normalize(
        rows.astype(jnp.float32) + attended,
        first_gain.astype(jnp.float32),
        first_shift.astype(jnp.float32),
    )
    first_low = first.astype(jnp.bfloat16)
    up = matmul(first_low, up_weight) + up_bias.astype(jnp.float32)
    activated = jax.nn.gelu(up, approximate=False).astype(jnp.bfloat16)
    down = matmul(activated, down_weight) + down_bias.astype(jnp.float32)
    second, normed_two, scaling_two = normalize(
        first + down, second_gain.astype(jnp.float32), second_shift.astype(jnp.float32)
    )
    second_low = second.astype(jnp.bfloat16)
    reduced = (matmul(second_low, student_weight) + student_bias.astype(jnp.float32)).astype(
        jnp.bfloat16
    )
    reduced_wide = reduced.astype(jnp.float32).reshape(count, positions, STU_HEADS, -1)
    query_pool = pool_query.astype(jnp.float32).reshape(STU_HEADS, -1)
    pool_scale = 1.0 / math.sqrt(query_pool.shape[-1])
    pool_scores = jnp.einsum("bshd,hd->bhs", reduced_wide, query_pool, precision=EXACT) * pool_scale
    pool_share = jax.nn.softmax(jnp.where(valid[:, None, :], pool_scores, MASKED), axis=-1)
    pooled = (
        jnp.einsum("bhs,bshd->bhd", pool_share, reduced_wide, precision=EXACT)
        .reshape(count, -1)
        .astype(jnp.bfloat16)
    )
    hidden = matmul(pooled, pool_weight) + pool_bias.astype(jnp.float32)
    squashed = jnp.tanh(hidden)
    squashed_low = squashed.astype(jnp.bfloat16)
    logits_part = matmul(squashed_low, class_weight)
    saved = (
        rows,
        query,
        key,
        value,
        valid,
        log_total,
        mixed,
        normed_one,
        scaling_one,
        first_low,
        up,
        activated,
        normed_two,
        scaling_two,
        second_low,
        reduced_wide,
        pool_share,
        pooled,
        squashed,
        squashed_low,
    )
    return (saved, second_low, logits_part)


def backward_batch(saved, second_cot, logits_part_grad, weights):
    (
        input_weight,
        query_bias,
        value_bias,
        output_weight,
        output_bias,
        first_gain,
        first_shift,
        up_weight,
        up_bias,
        down_weight,
        down_bias,
        second_gain,
        second_shift,
        student_weight,
        student_bias,
        pool_query,
        pool_weight,
        pool_bias,
        class_weight,
    ) = weights
    (
        rows,
        query,
        key,
        value,
        valid,
        log_total,
        mixed,
        normed_one,
        scaling_one,
        first_low,
        up,
        activated,
        normed_two,
        scaling_two,
        second_low,
        reduced_wide,
        pool_share,
        pooled,
        squashed,
        squashed_low,
    ) = saved
    count, positions = valid.shape
    width = rows.shape[1]
    class_weight_grad = matmul_left(squashed_low, logits_part_grad)
    hidden_cot = (
        matmul_right(logits_part_grad, class_weight) * (1.0 - squashed * squashed)
    ).astype(jnp.bfloat16)
    pool_weight_grad = matmul_left(pooled, hidden_cot)
    pool_bias_grad = column_sum(hidden_cot)
    pooled_cot = rounded(matmul_right(hidden_cot, pool_weight)).reshape(count, STU_HEADS, -1)
    query_pool = pool_query.astype(jnp.float32).reshape(STU_HEADS, -1)
    pool_scale = 1.0 / math.sqrt(query_pool.shape[-1])
    share_cot = jnp.einsum("bhd,bshd->bhs", pooled_cot, reduced_wide, precision=EXACT)
    score_cot = pool_share * (share_cot - jnp.sum(pool_share * share_cot, axis=-1, keepdims=True))
    reduced_cot = jnp.einsum("bhs,bhd->bshd", pool_share, pooled_cot, precision=EXACT)
    reduced_cot = (
        reduced_cot
        + jnp.einsum("bhs,hd->bshd", score_cot, query_pool, precision=EXACT) * pool_scale
    )
    pool_query_grad = (
        jnp.einsum("bhs,bshd->hd", score_cot, reduced_wide, precision=EXACT) * pool_scale
    ).reshape(-1)
    reduced_cot = reduced_cot.reshape(count * positions, -1).astype(jnp.bfloat16)
    student_weight_grad = matmul_left(second_low, reduced_cot)
    student_bias_grad = column_sum(reduced_cot)
    total_two = second_cot + matmul_right(reduced_cot, student_weight)
    sum_two_cot, second_gain_grad, second_shift_grad = normalize_back(
        total_two, normed_two, scaling_two, second_gain.astype(jnp.float32)
    )
    down_cot = sum_two_cot.astype(jnp.bfloat16)
    down_weight_grad = matmul_left(activated, down_cot)
    down_bias_grad = column_sum(down_cot)
    unused, gelu_back = jax.vjp(lambda inner: jax.nn.gelu(inner, approximate=False), up)
    up_cot = gelu_back(matmul_right(down_cot, down_weight))[0].astype(jnp.bfloat16)
    up_weight_grad = matmul_left(first_low, up_cot)
    up_bias_grad = column_sum(up_cot)
    first_cot = sum_two_cot + matmul_right(up_cot, up_weight)
    sum_one_cot, first_gain_grad, first_shift_grad = normalize_back(
        first_cot, normed_one, scaling_one, first_gain.astype(jnp.float32)
    )
    attended_cot = sum_one_cot.astype(jnp.bfloat16)
    output_weight_grad = matmul_left(mixed, attended_cot)
    output_bias_grad = column_sum(attended_cot)
    mixed_cot = head_view(
        matmul_right(attended_cot, output_weight).astype(jnp.bfloat16), count, positions
    )
    query_heads = head_view(query, count, positions)
    key_heads = head_view(key, count, positions)
    value_heads = head_view(value, count, positions)
    softened = jnp.exp(masked_scores(query_heads, key_heads, valid) - log_total)
    attention_cot = jnp.einsum(
        "bqhd,bkhd->bhqk", mixed_cot, value_heads, preferred_element_type=jnp.float32
    )
    value_cot = jnp.einsum(
        "bhqk,bqhd->bkhd",
        softened.astype(jnp.bfloat16),
        mixed_cot,
        preferred_element_type=jnp.float32,
    )
    scores_cot = softened * (
        attention_cot - jnp.sum(softened * attention_cot, axis=-1, keepdims=True)
    )
    scores_cot = scores_cot.astype(jnp.bfloat16)
    scale = 1.0 / math.sqrt(HEAD_DIM)
    query_cot = (
        jnp.einsum("bhqk,bkhd->bqhd", scores_cot, key_heads, preferred_element_type=jnp.float32)
        * scale
    )
    key_cot = (
        jnp.einsum("bhqk,bqhd->bkhd", scores_cot, query_heads, preferred_element_type=jnp.float32)
        * scale
    )
    projected_cot = jnp.concatenate(
        [
            query_cot.reshape(count * positions, width),
            key_cot.reshape(count * positions, width),
            value_cot.reshape(count * positions, width),
        ],
        axis=1,
    ).astype(jnp.bfloat16)
    input_weight_grad = matmul_left(rows, projected_cot)
    query_bias_grad = column_sum(projected_cot[:, :width])
    value_bias_grad = column_sum(projected_cot[:, 2 * width :])
    rows_cot = sum_one_cot + matmul_right(projected_cot, input_weight)
    gradients = (
        input_weight_grad,
        query_bias_grad,
        value_bias_grad,
        output_weight_grad,
        output_bias_grad,
        first_gain_grad,
        first_shift_grad,
        up_weight_grad,
        up_bias_grad,
        down_weight_grad,
        down_bias_grad,
        second_gain_grad,
        second_shift_grad,
        student_weight_grad,
        student_bias_grad,
        pool_query_grad,
        pool_weight_grad,
        pool_bias_grad,
        class_weight_grad,
    )
    return (gradients, rows_cot.reshape(count, positions, width))


def body(
    tokens,
    input_weight,
    query_bias,
    value_bias,
    output_weight,
    output_bias,
    first_gain,
    first_shift,
    up_weight,
    up_bias,
    down_weight,
    down_bias,
    second_gain,
    second_shift,
    student_weight,
    student_bias,
    pool_query,
    pool_weight,
    pool_bias,
    class_weight,
    class_bias,
    lengths,
    exit_layer,
    destination,
    repacked_grad,
    logits_grad,
):
    weights = (
        lax.all_gather(input_weight, ("dp", "fsdp"), axis=0, tiled=True),
        lax.all_gather(query_bias, ("dp", "fsdp"), axis=0, tiled=True),
        lax.all_gather(value_bias, ("dp", "fsdp"), axis=0, tiled=True),
        lax.all_gather(output_weight, ("dp", "fsdp"), axis=0, tiled=True),
        lax.all_gather(output_bias, ("dp", "fsdp"), axis=0, tiled=True),
        lax.all_gather(first_gain, ("dp", "fsdp"), axis=0, tiled=True),
        lax.all_gather(first_shift, ("dp", "fsdp"), axis=0, tiled=True),
        lax.all_gather(up_weight, ("dp", "fsdp"), axis=0, tiled=True),
        lax.all_gather(up_bias, ("dp", "fsdp"), axis=0, tiled=True),
        lax.all_gather(down_weight, ("dp", "fsdp"), axis=0, tiled=True),
        lax.all_gather(down_bias, ("dp", "fsdp"), axis=0, tiled=True),
        lax.all_gather(second_gain, ("dp", "fsdp"), axis=0, tiled=True),
        lax.all_gather(second_shift, ("dp", "fsdp"), axis=0, tiled=True),
        lax.all_gather(student_weight, ("dp", "fsdp"), axis=0, tiled=True),
        lax.all_gather(student_bias, ("dp", "fsdp"), axis=0, tiled=True),
        lax.all_gather(pool_query, ("dp", "fsdp"), axis=0, tiled=True),
        lax.all_gather(pool_weight, ("dp", "fsdp"), axis=0, tiled=True),
        lax.all_gather(pool_bias, ("dp", "fsdp"), axis=0, tiled=True),
        lax.all_gather(class_weight, ("dp", "fsdp"), axis=0, tiled=True),
    )
    samples, positions, width = tokens.shape
    part = samples // MICRO
    saved_list = []
    second_list = []
    logits_list = []
    for batch in range(MICRO):
        begin = batch * part
        saved, second_low, logits_part = forward_batch(
            tokens[begin : begin + part], lengths[begin : begin + part], weights
        )
        saved_list.append(saved)
        second_list.append(second_low)
        logits_list.append(logits_part)
    student_logits = jnp.concatenate(logits_list, axis=0) + class_bias.astype(jnp.float32)
    second_rows = jnp.concatenate(second_list, axis=0).reshape(samples, positions * width)
    fsdp_count = lax.axis_size("fsdp")
    group_index = lax.axis_index("dp")
    member = lax.axis_index("fsdp")
    capacity = 3 * samples // (2 * fsdp_count)
    span = fsdp_count * samples
    group_slots = lax.dynamic_slice_in_dim(destination, group_index * span, span).reshape(
        fsdp_count, samples
    )
    target = group_slots // samples - group_index * fsdp_count
    slot = group_slots % samples
    order = jnp.arange(samples, dtype=jnp.int32)
    before = order[None, :] < order[:, None]
    same = target[:, :, None] == target[:, None, :]
    rank = jnp.sum(jnp.where(same & before[None, :, :], 1, 0), axis=2).astype(jnp.int32)
    send_column = lax.dynamic_index_in_dim(target * capacity + rank, member, 0, keepdims=False)
    alive = exit_layer > LAYER
    buffer_slots = jnp.arange(fsdp_count * capacity, dtype=jnp.int32)
    send_table = ((buffer_slots[:, None] == send_column[None, :]) & alive[None, :]).astype(
        jnp.bfloat16
    )
    receive_column = (jnp.arange(fsdp_count, dtype=jnp.int32)[:, None] * capacity + rank).reshape(
        -1
    )
    arrives = (target == member).reshape(-1)
    place = jnp.where(arrives[:, None] & (slot.reshape(-1)[:, None] == order[None, :]), 1.0, 0.0)
    pick = jnp.where(receive_column[:, None] == buffer_slots[None, :], 1.0, 0.0)
    receive_table = matmul_left(place, pick).astype(jnp.bfloat16)
    outgoing = matmul(send_table, second_rows).astype(jnp.bfloat16)
    received = lax.all_to_all(outgoing, "fsdp", split_axis=0, concat_axis=0, tiled=True)
    repacked = (
        matmul(receive_table, received).astype(jnp.bfloat16).reshape(samples, positions, width)
    )
    back_buffer = matmul_left(
        receive_table, repacked_grad.reshape(samples, positions * width)
    ).astype(jnp.bfloat16)
    returned = lax.all_to_all(back_buffer, "fsdp", split_axis=0, concat_axis=0, tiled=True)
    second_cot_rows = matmul_left(send_table, returned).reshape(samples * positions, width)
    bias_grad = lax.psum(jnp.sum(logits_grad.astype(jnp.float32), axis=0), ("dp", "fsdp"))
    total = None
    shares = None
    token_parts = []
    for batch in range(MICRO):
        begin = batch * part
        gradients, token_part = backward_batch(
            saved_list[batch],
            second_cot_rows[begin * positions : (begin + part) * positions],
            logits_grad[begin : begin + part],
            weights,
        )
        token_parts.append(token_part)
        total = (
            gradients
            if batch == 0
            else tuple((older + newer for older, newer in zip(total, gradients)))
        )
    shares = (
        lax.psum_scatter(total[0], ("dp", "fsdp"), scatter_dimension=0, tiled=True),
        lax.psum_scatter(total[1], ("dp", "fsdp"), scatter_dimension=0, tiled=True),
        lax.psum_scatter(total[2], ("dp", "fsdp"), scatter_dimension=0, tiled=True),
        lax.psum_scatter(total[3], ("dp", "fsdp"), scatter_dimension=0, tiled=True),
        lax.psum_scatter(total[4], ("dp", "fsdp"), scatter_dimension=0, tiled=True),
        lax.psum_scatter(total[5], ("dp", "fsdp"), scatter_dimension=0, tiled=True),
        lax.psum_scatter(total[6], ("dp", "fsdp"), scatter_dimension=0, tiled=True),
        lax.psum_scatter(total[7], ("dp", "fsdp"), scatter_dimension=0, tiled=True),
        lax.psum_scatter(total[8], ("dp", "fsdp"), scatter_dimension=0, tiled=True),
        lax.psum_scatter(total[9], ("dp", "fsdp"), scatter_dimension=0, tiled=True),
        lax.psum_scatter(total[10], ("dp", "fsdp"), scatter_dimension=0, tiled=True),
        lax.psum_scatter(total[11], ("dp", "fsdp"), scatter_dimension=0, tiled=True),
        lax.psum_scatter(total[12], ("dp", "fsdp"), scatter_dimension=0, tiled=True),
        lax.psum_scatter(total[13], ("dp", "fsdp"), scatter_dimension=0, tiled=True),
        lax.psum_scatter(total[14], ("dp", "fsdp"), scatter_dimension=0, tiled=True),
        lax.psum_scatter(total[15], ("dp", "fsdp"), scatter_dimension=0, tiled=True),
        lax.psum_scatter(total[16], ("dp", "fsdp"), scatter_dimension=0, tiled=True),
        lax.psum_scatter(total[17], ("dp", "fsdp"), scatter_dimension=0, tiled=True),
        lax.psum_scatter(total[18], ("dp", "fsdp"), scatter_dimension=0, tiled=True),
    )
    tokens_grad = jnp.concatenate(token_parts, axis=0)
    return (repacked, student_logits, tokens_grad) + tuple(shares) + (bias_grad,)


def solution(mesh):
    placed = (
        P(("dp", "fsdp"), None, None),
        P(("dp", "fsdp"), None),
        P(("dp", "fsdp")),
        P(("dp", "fsdp")),
        P(("dp", "fsdp"), None),
        P(("dp", "fsdp")),
        P(("dp", "fsdp")),
        P(("dp", "fsdp")),
        P(("dp", "fsdp"), None),
        P(("dp", "fsdp")),
        P(("dp", "fsdp"), None),
        P(("dp", "fsdp")),
        P(("dp", "fsdp")),
        P(("dp", "fsdp")),
        P(("dp", "fsdp"), None),
        P(("dp", "fsdp")),
        P(("dp", "fsdp")),
        P(("dp", "fsdp"), None),
        P(("dp", "fsdp")),
        P(("dp", "fsdp"), None),
        P(),
        P(("dp", "fsdp")),
        P(("dp", "fsdp")),
        P(),
        P(("dp", "fsdp"), None, None),
        P(("dp", "fsdp"), None),
    )
    return jax.shard_map(
        body,
        mesh=mesh,
        in_specs=placed,
        out_specs=(
            P(("dp", "fsdp"), None, None),
            P(("dp", "fsdp"), None),
            P(("dp", "fsdp"), None, None),
            P(("dp", "fsdp"), None),
            P(("dp", "fsdp")),
            P(("dp", "fsdp")),
            P(("dp", "fsdp"), None),
            P(("dp", "fsdp")),
            P(("dp", "fsdp")),
            P(("dp", "fsdp")),
            P(("dp", "fsdp"), None),
            P(("dp", "fsdp")),
            P(("dp", "fsdp"), None),
            P(("dp", "fsdp")),
            P(("dp", "fsdp")),
            P(("dp", "fsdp")),
            P(("dp", "fsdp"), None),
            P(("dp", "fsdp")),
            P(("dp", "fsdp")),
            P(("dp", "fsdp"), None),
            P(("dp", "fsdp")),
            P(("dp", "fsdp"), None),
            P(),
        ),
        check_vma=False,
    )
```

profile of v0, /device:TPU:0, one launch (start us, length us, event | category | flops | bytes accessed | tf_op | source)
XLA Modules:
  0.0 1374.8 jit_solution(17532592138922852143)
XLA Ops:
  10.7 3.6 copy.253
  18.3 6.8 all_to_all.19
  25.2 5.6 all-to-all-start.1
  34.3 114.2 %all-reduce.28 = (bf16[768]{0:T(1024)(128)(2,1)S(1)}, bf16[768]{0:T(1024)(128)(2,1)S(1)}, bf16[768]{0:T(1024)(128)(2,1)S(1)}, bf16[768]{0:T(1024)(128)(2,1)S(1)}...) all-reduce(bf16[768]{0:T(1024)(128)(2,1)S(1)} %dynamic-update-slice, ...), channel_id=1, replica_groups=mesh['dp'=8,'fsdp'=4] {'dp','fsdp'}, use_global_device_ids=true, to_apply=%add.2 | all-reduce | flops 9600 | bytes 38400
  152.7 41.2 %all-gather.1 = bf16[32,4,14]{2,1,0:T(4,128)(2,1)} all-gather(bf16[1,4,14]{2,1,0:T(4,128)(2,1)S(1)} %bitcast.402), channel_id=1, replica_groups=mesh['dp'=8,'fsdp'=4] {'dp','fsdp'}, dimensions={0}, use_global_device_ids=true | all-gather | bytes 3696 | tf_op jit(solution)/shard_map/all_gather | solution.py:369
  193.9 38.5 %all-gather = bf16[32,4,128]{2,1,0:T(4,128)(2,1)} all-gather(bf16[1,4,128]{2,1,0:T(4,128)(2,1)S(1)} %bitcast.403), channel_id=1, replica_groups=mesh['dp'=8,'fsdp'=4] {'dp','fsdp'}, dimensions={0}, use_global_device_ids=true | all-gather | bytes 33792 | tf_op jit(solution)/shard_map/all_gather | solution.py:367
  232.4 41.8 %all_gather.70 = bf16[768,128]{1,0:T(8,128)(2,1)} all-gather(bf16[24,128]{1,0:T(8,128)(2,1)S(1)} %copy-done.122), channel_id=1, replica_groups=mesh['dp'=8,'fsdp'=4] {'dp','fsdp'}, dimensions={0}, use_global_device_ids=true | all-gather | bytes 202752 | tf_op jit(solution)/shard_map/all_gather | solution.py:364
  276.4 6.7 all_to_all.21
  288.2 4.0 slice.65
  294.3 6.3 fusion.195
  300.7 3.6 copy-done.24
  306.9 5.8 fusion.194
  312.7 3.6 copy-done.25
  318.8 6.9 fusion.18
  341.6 11.2 copy.169
  379.1 7.8 fusion.177
  387.0 4.5 copy-done.159
  391.5 63.5 %multiply_convert_fusion.1 = (bf16[1024,3072]{1,0:T(8,128)(2,1)}, f32[1024,3072]{1,0:T(8,128)}, bf16[1024,3072]{1,0:T(8,128)(2,1)}, f32[1024,3072]{1,0:T(8,128)}, f32[1024,3072]{1,0:T(8,128)}) fusion(f32[3072]{0:T(1024)S(1)} %convert_element_type.279, f32[1024,3072]{1,0:T(8,128)S(1)} %fusion.177, bf16[768,3072]{1,0:T(8,128)(2,1)S(1)} %copy-done.139, ...), kind=kOutput, calls=%fused_computation.26 | convolution fusion | flops 5251006464 | bytes 70805504 | tf_op jit(solution)/shard_map/dot_general | solution.py:21
  455.1 10.6 fusion.190
  468.8 5.4 fusion.191
  506.4 4.9 multiply_reduce_fusion.3
  511.4 5.3 convert_reduce_fusion.3
  516.7 19.5 %convert_reduce_fusion.1 = (f32[3072]{0:T(1024)}, bf16[1024,3072]{1,0:T(8,128)(2,1)}) fusion(f32[1024,3072]{1,0:T(8,128)} %get-tuple-element.168, bf16[3072,768]{1,0:T(8,128)(2,1)} %all-gather.13.cloned.1.call-done, f32[1024,768]{1,0:T(8,128)} %get-tuple-element.162, f32[1024,3072]{1,0:T(8,128)} %get-tuple-element.209, f32[3072]{0:T(1024)S(1)} %copy-done.120), kind=kOutput, calls=%fused_computation.10 | convolution fusion | flops 4886098944 | bytes 39346176 | tf_op jit(solution)/shard_map/dot_general | solution.py:31
  536.2 12.5 multiply_reduce_fusion.5
  551.6 18.8 %convert_reduce_fusion = (f32[3072]{0:T(1024)S(1)}, bf16[1024,3072]{1,0:T(8,128)(2,1)}) fusion(f32[1024,3072]{1,0:T(8,128)} %get-tuple-element.184, bf16[3072,768]{1,0:T(8,128)(2,1)} %all-gather.13.cloned.1.call-done, f32[1024,768]{1,0:T(8,128)} %get-tuple-element.160, f32[1024,3072]{1,0:T(8,128)} %copy-done.159, f32[3072]{0:T(1024)S(1)} %copy-done.120), kind=kOutput, calls=%fused_computation.9 | convolution fusion | flops 4886098944 | bytes 39346176 | tf_op jit(solution)/shard_map/dot_general | solution.py:31
  570.4 13.5 convert_reduce_fusion.5
  595.4 6.4 fusion.36
  607.5 3.4 fusion.40
  621.1 6.6 fusion.35
  669.4 6.1 fusion.196
  675.6 5.9 add_bitcast_fusion
  681.4 8.0 copy.240
  689.5 8.4 fusion.159
  697.9 10.6 convolution_add_fusion
  709.2 9.2 fusion.179
  718.4 11.0 convolution_add_fusion.1
  737.0 3.5 convolution_convert_fusion.1
  740.6 6.7 all_to_all.16
  747.4 5.5 all-to-all-start
  755.4 101.5 %all-reduce.27 = (f32[768]{0:T(1024)S(1)}, f32[768]{0:T(1024)S(1)}, f32[768]{0:T(1024)S(1)}, f32[768]{0:T(1024)S(1)}, f32[768]{0:T(1024)S(1)}, /*index=5*/f32[30...) all-reduce(f32[768]{0:T(1024)S(1)} %add.425, ...), channel_id=3, replica_groups=mesh['dp'=8,'fsdp'=4] {'dp','fsdp'}, use_global_device_ids=true, to_apply=%region_32.33.clone | all-reduce | flops 11406 | bytes 91248
  865.3 8.5 convolution_add_fusion.6
  873.9 4.0 convolution_add_fusion.7
  882.5 6.8 all_to_all.18
  889.4 3.5 convolution_convert_fusion.2
  895.2 64.8 %reduce-scatter.10.cloned.1.call-done = f32[24,768]{1,0:T(8,128)} async-done(((f32[768,768]{1,0:T(8,128)}), f32[24,768]{1,0:T(8,128)}) %reduce-scatter.10.cloned.1.call-update) | async-done | bytes 73744 | tf_op jit(solution)/shard_map/reduce_scatter | solution.py:445
  960.1 124.4 %reduce-scatter.16.cloned.1.call-done = f32[24,2304]{1,0:T(8,128)} async-done(((f32[768,2304]{1,0:T(8,128)}), f32[24,2304]{1,0:T(8,128)}) %reduce-scatter.16.cloned.1.call-update) | async-done | bytes 221200
  1084.4 142.4 %reduce-scatter.14.cloned.1.call-done = f32[96,768]{1,0:T(8,128)} async-done(((f32[3072,768]{1,0:T(8,128)}), f32[96,768]{1,0:T(8,128)}) %reduce-scatter.14.cloned.1.call-update) | async-done | bytes 294928 | tf_op jit(solution)/shard_map/reduce_scatter | solution.py:451
  1226.9 140.8 %reduce-scatter.12.cloned.1.call-done = f32[24,3072]{1,0:T(8,128)} async-done(((f32[768,3072]{1,0:T(8,128)}), f32[24,3072]{1,0:T(8,128)}) %reduce-scatter.12.cloned.1.call-update) | async-done | bytes 294928 | tf_op jit(solution)/shard_map/reduce_scatter | solution.py:449
  (595 shorter events, 203.9 us)
Async XLA Ops:
  7.2 287.2 %all-gather.7.cloned.1.call-start = ((), (), s32[]{:S(2)}) async-start(), calls=%async_computation.7 | async-start | bytes 3649536 | tf_op jit(solution)/shard_map/all_gather | solution.py:351
  7.9 354.1 %all-gather.9.cloned.1.call-start = ((), (), s32[]{:S(2)}) async-start(), calls=%async_computation.8 | async-start | bytes 1216512 | tf_op jit(solution)/shard_map/all_gather | solution.py:354
  8.7 370.4 %all-gather.11.cloned.1.call-start = ((), (), s32[]{:S(2)}) async-start(), calls=%async_computation.9 | async-start | bytes 4866048 | tf_op jit(solution)/shard_map/all_gather | solution.py:358
  25.1 8.7 copy-start.154
  25.1 8.9 copy-start.155
  25.2 127.5 %copy-start.135 = (bf16[4,14]{1,0:T(4,128)(2,1)S(1)}, bf16[4,14]{1,0:T(4,128)(2,1)}, u32[]{:S(2)}) copy-start(bf16[4,14]{1,0:T(4,128)(2,1)} %param.45) | copy-start | bytes 340
  25.2 168.7 %copy-start.136 = (bf16[4,128]{1,0:T(4,128)(2,1)S(1)}, bf16[4,128]{1,0:T(4,128)(2,1)}, u32[]{:S(2)}) copy-start(bf16[4,128]{1,0:T(4,128)(2,1)} %param.43) | copy-start | bytes 3076
  25.2 207.3 %copy-start.122 = (bf16[24,128]{1,0:T(8,128)(2,1)S(1)}, bf16[24,128]{1,0:T(8,128)(2,1)}, u32[]{:S(2)}) copy-start(bf16[24,128]{1,0:T(8,128)(2,1)} %param.40) | copy-start | bytes 18436
  25.2 249.1 %copy-start.156 = (s32[16]{0:T(128)S(1)}, s32[16]{0:T(128)}, u32[]{:S(2)}) copy-start(s32[16]{0:T(128)} %param.48) | copy-start | bytes 196
  25.2 249.1 %copy-start.134 = (s32[16]{0:T(128)S(1)}, s32[16]{0:T(128)}, u32[]{:S(2)}) copy-start(s32[16]{0:T(128)} %param.47) | copy-start | bytes 196
  25.2 249.3 %copy-start.46 = (bf16[16,128,768]{2,1,0:T(8,128)(2,1)S(1)}, bf16[16,128,768]{2,1,0:T(8,128)(2,1)}, u32[]{:S(2)}) copy-start(bf16[16,128,768]{2,1,0:T(8,128)(2,1)} %param.26) | copy-start | bytes 9437188
  25.2 251.2 %all-to-all-start.1 = ((bf16[4,6,98304]{2,1,0:T(8,128)(2,1)}), bf16[4,6,98304]{2,1,0:T(8,128)(2,1)}, u32[]{:S(2)}, u32[]{:S(2)}) async-start(bf16[4,6,98304]{2,1,0:T(8,128)(2,1)} %all_to_all.19), calls=%async_computation.1 | async-start | bytes 12582912 | tf_op jit(solution)/shard_map/all_to_all | solution.py:421
  30.8 424.3 %all-gather.13.cloned.1.call-start = ((), (), s32[]{:S(2)}) async-start(), calls=%async_computation.10 | async-start | bytes 4866048 | tf_op jit(solution)/shard_map/all_gather | solution.py:360
  31.4 849.9 %all-reduce.31.cloned.1.call-start = ((), (), s32[]{:S(2)}) async-start(), calls=%async_computation.15 | async-start | bytes 131072
  150.9 315.5 %copy-start.71 = (f32[768]{0:T(1024)}, f32[768]{0:T(1024)S(1)}, u32[]{:S(2)}) copy-start(f32[768]{0:T(1024)S(1)} %convert_element_type.277) | copy-start | bytes 9220
  152.7 234.3 %copy-start.119 = (f32[3072]{0:T(1024)}, f32[3072]{0:T(1024)S(1)}, u32[]{:S(2)}) copy-start(f32[3072]{0:T(1024)S(1)} %convert_element_type.279) | copy-start | bytes 36868
  274.3 8.8 copy-start.128
  274.3 8.8 copy-start.130
  274.5 83.3 %copy-start.100 = (pred[8,128]{1,0:T(8,128)(4,1)}, pred[8,128]{1,0:T(8,128)(4,1)S(1)}, u32[]{:S(2)}) copy-start(pred[8,128]{1,0:T(8,128)(4,1)S(1)} %get-tuple-element.235) | copy-start | bytes 3076
  274.5 97.7 %copy-start.103 = (pred[8,128]{1,0:T(8,128)(4,1)}, pred[8,128]{1,0:T(8,128)(4,1)S(1)}, u32[]{:S(2)}) copy-start(pred[8,128]{1,0:T(8,128)(4,1)S(1)} %get-tuple-element.234) | copy-start | bytes 3076
  366.1 89.0 %copy-start.80 = (f32[1024]{0:T(1024)}, f32[1024]{0:T(1024)S(1)}, u32[]{:S(2)}) copy-start(f32[1024]{0:T(1024)S(1)} %add_rsqrt_fusion.3) | copy-start | bytes 12292
  379.1 12.4 copy-start.13
  379.1 12.4 copy-start.139
  391.5 63.6 %copy-start.127 = (f32[768]{0:T(1024)S(1)}, f32[768]{0:T(1024)}, u32[]{:S(2)}) copy-start(f32[768]{0:T(1024)} %convert_element_type.281) | copy-start | bytes 9220
  455.1 11.3 slice-start.8
  455.1 11.3 slice-start.10
  455.1 11.2 slice-start.9
  455.1 11.2 slice-start.11
  465.7 9.0 copy-start.2
  465.8 9.0 copy-start.86
  480.0 11.8 copy-start.104
  516.7 19.5 %copy-start.81 = (f32[1024]{0:T(1024)S(1)}, f32[1024]{0:T(1024)}, u32[]{:S(2)}) copy-start(f32[1024]{0:T(1024)} %copy-done.80) | copy-start | bytes 12292
  536.2 12.5 copy-start.23
  551.6 18.8 %copy-start.6 = (f32[1024,768]{1,0:T(8,128)S(1)}, f32[1024,768]{1,0:T(8,128)}, u32[]{:S(2)}) copy-start(f32[1024,768]{1,0:T(8,128)} %copy-done.4) | copy-start | bytes 9437188
  590.8 11.1 slice-start.2
  616.4 11.2 slice-start
  639.6 255.6 %reduce-scatter.18.cloned.1.call-start = ((), (), s32[]{:S(2)}) async-start(), calls=%async_computation.16 | async-start | bytes 405504
  646.5 313.6 %reduce-scatter.10.cloned.1.call-start = ((), (), s32[]{:S(2)}) async-start(), calls=%async_computation.11 | async-start | bytes 2433024 | tf_op jit(solution)/shard_map/reduce_scatter | solution.py:445
  651.0 17.0 %copy-start.18 = (bf16[8,128,12,64]{1,0,3,2:T(8,128)(2,1)}, bf16[8,128,12,64]{1,0,3,2:T(8,128)(2,1)S(1)}, u32[]{:S(2)}) copy-start(bf16[8,128,12,64]{1,0,3,2:T(8,128)(2,1)S(1)} %copy.198) | copy-start | bytes 4718596
  661.2 423.3 %reduce-scatter.16.cloned.1.call-start = ((), (), s32[]{:S(2)}) async-start(), calls=%async_computation.14 | async-start | bytes 7299072
  689.5 537.4 %reduce-scatter.14.cloned.1.call-start = ((), (), s32[]{:S(2)}) async-start(), calls=%async_computation.13 | async-start | bytes 9732096 | tf_op jit(solution)/shard_map/reduce_scatter | solution.py:451
  708.5 9.9 copy-start.7
  708.5 659.2 %reduce-scatter.12.cloned.1.call-start = ((), (), s32[]{:S(2)}) async-start(), calls=%async_computation.12 | async-start | bytes 9732096 | tf_op jit(solution)/shard_map/reduce_scatter | solution.py:449
  747.4 135.2 %all-to-all-start = ((bf16[4,6,98304]{2,1,0:T(8,128)(2,1)}), bf16[4,6,98304]{2,1,0:T(8,128)(2,1)}, u32[]{:S(2)}, u32[]{:S(2)}) async-start(bf16[4,6,98304]{2,1,0:T(8,128)(2,1)} %all_to_all.16), calls=%async_computation | async-start | bytes 12582912 | tf_op jit(solution)/shard_map/all_to_all | solution.py:414
  753.1 111.3 %copy-start.65 = (bf16[32,4,14]{2,1,0:T(4,128)(2,1)S(1)}, bf16[32,4,14]{2,1,0:T(4,128)(2,1)}, u32[]{:S(2)}) copy-start(bf16[32,4,14]{2,1,0:T(4,128)(2,1)} %all-gather.1) | copy-start | bytes 10756
  754.3 119.5 %slice-start.6 = ((s8[4718592]{0:T(1024)(128)(4,1)}), s8[524288]{0:T(1024)(128)(4,1)S(1)}, s32[]{:S(2)}) async-start(s8[4718592]{0:T(1024)(128)(4,1)} %bitcast.384), calls=%async_computation.23 | async-start | bytes 1048576
  865.3 8.5 slice-start.7
  865.3 8.5 copy-start.140
  (136 other events, 566.0 us)
Sparse Core Ops, SparseCore 0:
  10.9 70.7 all-gather.6
  84.7 53.6 all-gather.8
  141.2 62.6 all-gather.10
  206.7 63.2 all-gather.12
  639.7 113.7 all-reduce.30
  758.9 96.2 reduce-scatter.17
  861.9 98.1 reduce-scatter.9
  966.3 118.0 reduce-scatter.15
  1091.9 134.9 reduce-scatter.13
  1233.2 134.4 reduce-scatter.11
where the time goes:
time: 1380 us; the launch traced here: 1370 us
  waiting for transfers between devices  475 us (34%)
  blocking collectives  337 us (24%)
  matrix products  322 us (23%)
  local copies, waits for them, and re-layouts  170 us (12%)
  other arithmetic  41 us (3%)
  between operations  16.5 us (1%)
    unnamed x2, blocking collectives  216 us
    reduce_scatter x1, waiting for transfers between devices, body(): lax.psum_scatter(total[9], ('dp', 'fsdp'), scatter_dimension=0, tiled=True)  142 us
    reduce_scatter x1, waiting for transfers between devices, body(): lax.psum_scatter(total[7], ('dp', 'fsdp'), scatter_dimension=0, tiled=True)  141 us
    unnamed x13, waiting for transfers between devices  127 us
    dot_general x16, matrix products, matmul(): return jnp.dot(left, right, preferred_element_type=jnp.float32)  116 us
    dot_general x14, matrix products, matmul_right(): lax.dot_general(left, right, (((1,), (1,)), ((), ())), preferred_element_...  93.9 us
    unnamed x399, local copies, waits for them, and re-layouts  80.5 us
    dot_general x17, matrix products, matmul_left(): lax.dot_general(left, right, (((0,), (0,)), ((), ())), preferred_element_...  69 us
  transfers between devices with their start and end apart: 12, of which 4 were waited for; matrix products, arithmetic and copies ran while one was open for 22% of the time, Pallas kernels for 0%

commit v1 on v0

v1 whole, which is shorter than its diff:
```python
import functools
import itertools
import math

import jax
import jax.numpy as jnp
from jax import lax
from jax.experimental import pallas as pl
from jax.experimental.pallas import tpu as pltpu
from jax.sharding import PartitionSpec as P

HEADS = 12
HEAD_DIM = 64
STU_HEADS = 2
LAYER = 6
EPS = 1e-06
MASKED = -1e30
AXES = ("dp", "fsdp")
F32 = jnp.float32
BF16 = jnp.bfloat16
VMEM_LIMIT = 60 * 1024 * 1024

QB, VB, OB, G1, S1, DB, G2, S2 = range(8)


def dot(left, right):
    return jnp.dot(left, right, preferred_element_type=F32)


def dot_nt(left, right):
    return lax.dot_general(left, right, (((1,), (1,)), ((), ())), preferred_element_type=F32)


def dot_tn(left, right):
    return lax.dot_general(left, right, (((0,), (0,)), ((), ())), preferred_element_type=F32)


def params(limit=VMEM_LIMIT):
    return pltpu.CompilerParams(vmem_limit_bytes=limit, dimension_semantics=("arbitrary",))


def cost(flops, nbytes):
    return pl.CostEstimate(flops=int(flops), bytes_accessed=int(nbytes), transcendentals=0)


def whole(shape, index=None):
    index = index or (0,) * len(shape)
    return pl.BlockSpec(shape, lambda i, *_: index, pipeline_mode=pl.Buffered(1))


def rows_spec(rows, width):
    return pl.BlockSpec((rows, width), lambda i, *_: (i, 0))


def kept(shape):
    return pl.BlockSpec(shape, lambda i, *_: (0,) * len(shape))


def layer_norm(total):
    mean = jnp.mean(total, axis=-1, keepdims=True)
    centered = total - mean
    factor = lax.rsqrt(jnp.mean(centered * centered, axis=-1, keepdims=True) + EPS)
    return centered * factor, factor


def layer_norm_back(cot, gain, normed, factor):
    scaled = cot * gain
    inner = (
        scaled
        - jnp.mean(scaled, axis=-1, keepdims=True)
        - normed * jnp.mean(scaled * normed, axis=-1, keepdims=True)
    )
    return factor * inner


def gelu_parts(up):
    size = jnp.abs(up) * (1.0 / math.sqrt(2.0))
    near = 1.0 / (1.0 + 0.3275911 * size)
    bell = jnp.exp(-(size * size))
    series = near * (
        0.5 * 0.254829592
        + near
        * (
            0.5 * -0.284496736
            + near * (0.5 * 1.421413741 + near * (0.5 * -1.453152027 + near * (0.5 * 1.061405429)))
        )
    )
    tail = series * bell
    phi = jnp.where(up >= 0.0, 1.0 - tail, tail)
    slope = phi + up * (bell * (1.0 / math.sqrt(2.0 * math.pi)))
    return up * phi, slope


def column_sum(matrix):
    return jnp.sum(matrix, axis=0, keepdims=True)


def stack_rows(rows, count):
    width = rows[0].shape[1]
    pad = count - len(rows)
    if pad:
        rows = list(rows) + [jnp.zeros((pad, width), F32)]
    return jnp.concatenate(rows, axis=0)


def one_hot_rows(count, width, group, stride, skip):
    row = lax.broadcasted_iota(jnp.int32, (count, width), 0)
    column = lax.broadcasted_iota(jnp.int32, (count, width), 1)
    shift = group.bit_length() - 1
    wanted = (row >> shift) * stride + skip + (row & (group - 1))
    return jnp.where(column == wanted, 1.0, 0.0).astype(BF16)


def turn_lanes(matrix):
    return pltpu.roll(matrix, 64, 1)


def read_small(block, vec_ref, sv_ref, pw_ref, cw_ref, ub_ref, stu, classes, devices):
    width = block.shape[0]
    shard = width // devices
    group = stu // devices
    lane = lax.broadcasted_iota(jnp.int32, (stu, 128), 1)
    left, right, rest = (
        dot(one_hot_rows(stu, width, group, shard, n * group), block) for n in range(3)
    )
    pw_ref[...] = jnp.where(lane < 64, turn_lanes(left), right).astype(BF16)
    rest = turn_lanes(rest)
    cw_ref[...] = jnp.where(lane < classes, rest, 0.0).astype(BF16)
    sv_ref[...] = rest.T[classes : classes + 8]
    low, high = (
        dot(one_hot_rows(devices, width, 1, shard, 3 * group + n), block) for n in range(2)
    )
    lane = lax.broadcasted_iota(jnp.int32, (devices, 128), 1)
    ub_ref[...] = jnp.where(lane < 64, turn_lanes(low), high)
    vec_ref[...] = block.astype(F32).T[:8]


def pack_small(vectors, up_bias, pool_weight, class_weight, columns):
    shard = vectors[0].shape[0]
    group = pool_weight.shape[0]
    rest = jnp.concatenate([class_weight] + [c[:, None] for c in columns], axis=1)
    up = jnp.pad(up_bias, (0, -up_bias.shape[0] % 64)).reshape(-1, 64)
    right = jnp.concatenate(
        [
            pool_weight[:, :64],
            pool_weight[:, 64:],
            jnp.pad(rest, ((0, 0), (0, 64 - rest.shape[1]))),
            up,
        ],
        axis=0,
    )
    right = jnp.pad(right, ((0, shard - right.shape[0]), (0, 0)))
    left = jnp.stack(vectors + (jnp.zeros_like(vectors[0]),) * (64 - len(vectors)), axis=1)
    return jnp.concatenate([left, right], axis=1)


def attend_kernel(lens, table, *refs, seq, width, stu, classes, devices):
    x_ref = refs[0]
    pieces = refs[1:-11]
    qkv_ref, prob_ref, mixed_ref, vec_ref, sv_ref, pw_ref, cw_ref, ub_ref, ws_ref, w_ref, sem = refs[-11:]
    step = pl.program_id(0)
    half = w_ref.shape[1] // 2
    cut = half - 128

    @pl.when(step == 0)
    def _():
        fetch_pieces(table, pieces, w_ref, sem, True, True)
        ws_ref[...] = w_ref[:, cut:half]
        read_small(
            w_ref[:, half + cut :], vec_ref, sv_ref, pw_ref, cw_ref, ub_ref, stu, classes, devices
        )

    rows = x_ref.shape[0]
    x = x_ref[...]
    vec = vec_ref[...]
    query = dot(x, w_ref[:, :width]) + vec[QB : QB + 1]
    qkv_ref[:, :width] = query.astype(BF16)
    split = 2 * width - cut
    qkv_ref[:, width:cut] = dot(x, w_ref[:, width:cut]).astype(BF16)
    qkv_ref[:, cut : 2 * width] = dot(x, w_ref[:, half : half + split]).astype(BF16)
    value = dot(x, w_ref[:, half + split : half + cut]) + vec[VB : VB + 1]
    qkv_ref[:, 2 * width :] = value.astype(BF16)
    lane = lax.broadcasted_iota(jnp.int32, (seq, 128), 1)
    first_head = lane < HEAD_DIM
    place = lax.broadcasted_iota(jnp.int32, (seq, 2 * seq), 0)
    scale = jnp.asarray(1.0 / math.sqrt(HEAD_DIM), BF16)
    for s in range(rows // seq):
        valid = place < lens[step * (rows // seq) + s]
        at = slice(s * seq, (s + 1) * seq)
        for pair in range(width // 128):
            low = pair * 128
            q = qkv_ref[at, low : low + 128] * scale
            k = qkv_ref[at, width + low : width + low + 128]
            v = qkv_ref[at, 2 * width + low : 2 * width + low + 128]
            zero = jnp.zeros_like(q)
            both = jnp.concatenate(
                [jnp.where(first_head, q, zero), jnp.where(first_head, zero, q)], axis=0
            )
            scores = jnp.where(valid, dot_nt(k, both), MASKED)
            raised = jnp.exp(scores - jnp.max(scores, axis=0, keepdims=True))
            share = raised * (1.0 / jnp.sum(raised, axis=0, keepdims=True))
            share = share.astype(BF16)
            prob_ref[s, pair] = share
            out = dot_tn(share, v)
            mixed_ref[at, low : low + 128] = jnp.where(first_head, out[:seq], out[seq:]).astype(BF16)


def attend(lens, table, rows, pieces, seq, block, stu, classes, devices):
    count, width = rows.shape
    pairs = width // 128
    samples = block // seq
    columns = 2 * pieces[0].shape[1]
    small = [
        jax.ShapeDtypeStruct((8, width), F32),
        jax.ShapeDtypeStruct((8, stu), F32),
        jax.ShapeDtypeStruct((stu, stu), BF16),
        jax.ShapeDtypeStruct((stu, 128), BF16),
        jax.ShapeDtypeStruct((devices, 128), F32),
        jax.ShapeDtypeStruct((width, stu), BF16),
    ]
    return pl.pallas_call(
        functools.partial(
            attend_kernel, seq=seq, width=width, stu=stu, classes=classes, devices=devices
        ),
        grid_spec=pltpu.PrefetchScalarGridSpec(
            num_scalar_prefetch=2,
            grid=(count // block,),
            in_specs=[rows_spec(block, width)] + [pl.BlockSpec(memory_space=pl.ANY)] * len(pieces),
            out_specs=[
                rows_spec(block, 3 * width),
                pl.BlockSpec((samples, pairs, seq, 2 * seq), lambda i, *_: (i, 0, 0, 0)),
                rows_spec(block, width),
            ]
            + [kept(s.shape) for s in small],
            scratch_shapes=[
                pltpu.VMEM((width, columns), BF16),
                pltpu.SemaphoreType.DMA((2 * len(pieces),)),
            ],
        ),
        out_shape=[
            jax.ShapeDtypeStruct((count, 3 * width), BF16),
            jax.ShapeDtypeStruct((count // seq, pairs, seq, 2 * seq), BF16),
            jax.ShapeDtypeStruct((count, width), BF16),
        ]
        + small,
        compiler_params=params(),
        cost_estimate=cost(2 * count * width * 3 * width * 2, 30e6),
        name="attend",
    )(lens, table, rows, *pieces)


def up_kernel(
    mixed_ref, x_ref, w_ref, vec_ref, ub_ref, norm_ref, factor_ref, low_ref, act_ref, slope_ref, *, chunk
):
    width = x_ref.shape[1]
    vec = vec_ref[...]
    total = dot(mixed_ref[...], w_ref[:, :width]) + vec[OB : OB + 1] + x_ref[...].astype(F32)
    normed, factor = layer_norm(total)
    norm_ref[...] = normed
    factor_ref[...] = jnp.broadcast_to(factor, factor_ref.shape)
    low_ref[...] = (normed * vec[G1 : G1 + 1] + vec[S1 : S1 + 1]).astype(BF16)
    low = low_ref[...]
    for begin in range(0, act_ref.shape[1], chunk):
        at = slice(begin, begin + chunk)
        up = dot(low, w_ref[:, width + begin : width + begin + chunk]) + ub_ref[0:1, at]
        act, slope = gelu_parts(up)
        act_ref[:, at] = act.astype(BF16)
        slope_ref[:, at] = slope.astype(BF16)


def up_part(mixed, rows, large, vec, ub, block):
    count, width = rows.shape
    ff = large.shape[1] - width
    return pl.pallas_call(
        functools.partial(up_kernel, chunk=256),
        grid_spec=pltpu.PrefetchScalarGridSpec(
            num_scalar_prefetch=0,
            grid=(count // block,),
            in_specs=[
                rows_spec(block, width),
                rows_spec(block, width),
                pl.BlockSpec(large.shape, lambda i: (0, 0), pipeline_mode=pl.Buffered(1)),
                whole(vec.shape),
                whole(ub.shape),
            ],
            out_specs=[
                rows_spec(block, width),
                rows_spec(block, 128),
                rows_spec(block, width),
                rows_spec(block, ff),
                rows_spec(block, ff),
            ],
        ),
        out_shape=[
            jax.ShapeDtypeStruct((count, width), F32),
            jax.ShapeDtypeStruct((count, 128), F32),
            jax.ShapeDtypeStruct((count, width), BF16),
            jax.ShapeDtypeStruct((count, ff), BF16),
            jax.ShapeDtypeStruct((count, ff), BF16),
        ],
        compiler_params=params(),
        cost_estimate=cost(2 * count * width * (ff + width) * 2, 50e6),
        name="up_part",
    )(mixed, rows, large, vec, ub)


def down_kernel(lens, alive, table, *refs, seq):
    act_ref, norm_ref, cot_ref, lg_ref, vec_ref, ws_ref, sv_ref, pw_ref, cw_ref = refs[:9]
    pieces = refs[9:-11]
    second_ref, sum_ref, dcot_ref, logits_ref, vgrad_ref, sgrad_ref = refs[-11:-5]
    wsgrad_ref, pwgrad_ref, cwgrad_ref, wd_ref, sem = refs[-5:]
    step = pl.program_id(0)
    rows = act_ref.shape[0]
    samples = rows // seq
    vec = vec_ref[...]
    sv = sv_ref[...]
    stu = sv.shape[1]
    pool_width = stu // STU_HEADS
    pool_scale = 1.0 / math.sqrt(pool_width)

    @pl.when(step == 0)
    def _():
        fetch_pieces(table, pieces, wd_ref, sem, True, True)
        vgrad_ref[...] = jnp.zeros_like(vgrad_ref)
        sgrad_ref[...] = jnp.zeros_like(sgrad_ref)
        wsgrad_ref[...] = jnp.zeros_like(wsgrad_ref)
        pwgrad_ref[...] = jnp.zeros_like(pwgrad_ref)
        cwgrad_ref[...] = jnp.zeros_like(cwgrad_ref)

    first = norm_ref[...] * vec[G1 : G1 + 1] + vec[S1 : S1 + 1]
    down = dot(act_ref[...], wd_ref[...]) + vec[DB : DB + 1]
    normed, factor = layer_norm(first + down)
    second = (normed * vec[G2 : G2 + 1] + vec[S2 : S2 + 1]).astype(BF16)
    reduced = (dot(second, ws_ref[...]) + sv[0:1]).astype(BF16)
    head_of = lax.broadcasted_iota(jnp.int32, (stu, stu), 0) // pool_width
    same = head_of == lax.broadcasted_iota(jnp.int32, (stu, stu), 1) // pool_width
    pool_query = sv[1:2]
    query_table = jnp.where(same, jnp.broadcast_to(pool_query, (stu, stu)), 0.0).astype(BF16)
    scores = dot_nt(reduced, query_table) * pool_scale
    place = lax.broadcasted_iota(jnp.int32, (seq, stu), 0)
    shares = []
    pooled_rows = []
    for s in range(samples):
        at = slice(s * seq, (s + 1) * seq)
        part = jnp.where(place < lens[step * samples + s], scores[at], MASKED)
        raised = jnp.exp(part - jnp.max(part, axis=0, keepdims=True))
        share = raised / jnp.sum(raised, axis=0, keepdims=True)
        shares.append(share)
        pooled_rows.append(column_sum(share * reduced[at].astype(F32)))
    pooled = stack_rows(pooled_rows, 8).astype(BF16)
    squashed = jnp.tanh(dot(pooled, pw_ref[...]) + sv[2:3])
    squashed_low = squashed.astype(BF16)
    logits_ref[...] = dot(squashed_low, cw_ref[...])
    lg = lg_ref[...]
    cwgrad_ref[...] += dot_tn(squashed_low, lg)
    hidden_cot = (dot_nt(lg, cw_ref[...]) * (1.0 - squashed * squashed)).astype(BF16)
    pwgrad_ref[...] += dot_tn(pooled, hidden_cot)
    pooled_cot = dot_nt(hidden_cot, pw_ref[...]).astype(BF16).astype(F32)
    query_grad = jnp.zeros((1, stu), F32)
    cots = []
    for s in range(samples):
        at = slice(s * seq, (s + 1) * seq)
        row = pooled_cot[s : s + 1]
        table = jnp.where(same, jnp.broadcast_to(row, (stu, stu)), 0.0).astype(BF16)
        share_cot = dot_nt(reduced[at], table)
        share = shares[s]
        score_cot = share * (share_cot - column_sum(share * share_cot))
        query_grad += column_sum(score_cot * reduced[at].astype(F32)) * pool_scale
        cots.append((share * row + score_cot * (pool_query * pool_scale)).astype(BF16))
    reduced_cot = jnp.concatenate(cots, axis=0)
    sgrad_ref[...] += stack_rows(
        [
            column_sum(reduced_cot.astype(F32)),
            query_grad,
            column_sum(hidden_cot.astype(F32)),
        ],
        8,
    )
    wsgrad_ref[...] += dot_tn(reduced_cot, second)
    back = dot_nt(reduced_cot, ws_ref[...])
    parts = []
    for s in range(samples):
        at = slice(s * seq, (s + 1) * seq)
        live = alive[step * samples + s] > 0
        parts.append(back[at] + jnp.where(live, cot_ref[at].astype(F32), 0.0))
        second_ref[at] = jnp.where(live, second[at], jnp.zeros_like(second[at]))
    total = jnp.concatenate(parts, axis=0)
    sum_cot = layer_norm_back(total, vec[G2 : G2 + 1], normed, factor)
    sum_ref[...] = sum_cot
    down_cot = sum_cot.astype(BF16)
    dcot_ref[...] = down_cot
    vgrad_ref[...] += stack_rows(
        [column_sum(total * normed), column_sum(total), column_sum(down_cot.astype(F32))], 8
    )


def down_part(lens, alive, table, act, normed, cot, lg, pieces, vec, ws, sv, pw, cw, seq, block):
    count, ff = act.shape
    width = normed.shape[1]
    stu = ws.shape[1]
    steps = count // block
    return pl.pallas_call(
        functools.partial(down_kernel, seq=seq),
        grid_spec=pltpu.PrefetchScalarGridSpec(
            num_scalar_prefetch=3,
            grid=(steps,),
            in_specs=[
                rows_spec(block, ff),
                rows_spec(block, width),
                rows_spec(block, width),
                rows_spec(8, 128),
                whole(vec.shape),
                whole(ws.shape),
                whole(sv.shape),
                whole(pw.shape),
                whole(cw.shape),
            ]
            + [pl.BlockSpec(memory_space=pl.ANY)] * len(pieces),
            out_specs=[
                rows_spec(block, width),
                rows_spec(block, width),
                rows_spec(block, width),
                rows_spec(8, 128),
                kept((8, width)),
                kept((8, stu)),
                kept((stu, width)),
                kept((stu, stu)),
                kept((stu, 128)),
            ],
            scratch_shapes=[
                pltpu.VMEM((ff, width), BF16),
                pltpu.SemaphoreType.DMA((2 * len(pieces),)),
            ],
        ),
        out_shape=[
            jax.ShapeDtypeStruct((count, width), BF16),
            jax.ShapeDtypeStruct((count, width), F32),
            jax.ShapeDtypeStruct((count, width), BF16),
            jax.ShapeDtypeStruct((steps * 8, 128), F32),
            jax.ShapeDtypeStruct((8, width), F32),
            jax.ShapeDtypeStruct((8, stu), F32),
            jax.ShapeDtypeStruct((stu, width), F32),
            jax.ShapeDtypeStruct((stu, stu), F32),
            jax.ShapeDtypeStruct((stu, 128), F32),
        ],
        compiler_params=params(),
        cost_estimate=cost(2 * count * width * ff * 2, 40e6),
        name="down_part",
    )(lens, alive, table, act, normed, cot, lg, vec, ws, sv, pw, cw, *pieces)


def up_back_kernel(table, *refs, chunk):
    dcot_ref, slope_ref, sum_ref, norm_ref, factor_ref, w_ref, vec_ref = refs[:7]
    pieces = refs[7:-8]
    ucot_ref, one_ref, acot_ref, mcot_ref, vgrad_ref, ugrad_ref, wd_ref, sem = refs[-8:]
    step = pl.program_id(0)
    width = dcot_ref.shape[1]
    vec = vec_ref[...]

    @pl.when(step == 0)
    def _():
        fetch_pieces(table, pieces, wd_ref, sem, True, True)
        vgrad_ref[...] = jnp.zeros_like(vgrad_ref)
        ugrad_ref[...] = jnp.zeros_like(ugrad_ref)

    down_cot = dcot_ref[...]
    for begin in range(0, slope_ref.shape[1], chunk):
        at = slice(begin, begin + chunk)
        up_cot = dot_nt(down_cot, wd_ref[at, :]) * slope_ref[:, at].astype(F32)
        up_cot = up_cot.astype(BF16)
        ucot_ref[:, at] = up_cot
        ugrad_ref[0:1, at] += column_sum(up_cot.astype(F32))
    cot = sum_ref[...] + dot_nt(ucot_ref[...], w_ref[:, width:])
    normed = norm_ref[...]
    one_cot = layer_norm_back(cot, vec[G1 : G1 + 1], normed, factor_ref[:, 0:1])
    one_ref[...] = one_cot
    low = one_cot.astype(BF16)
    acot_ref[...] = low
    mcot_ref[...] = dot_nt(low, w_ref[:, :width]).astype(BF16)
    vgrad_ref[...] += stack_rows(
        [column_sum(cot * normed), column_sum(cot), column_sum(low.astype(F32))], 8
    )


def up_back(table, dcot, slope, sum_two, normed, factor, pieces, large, vec, block):
    count, width = dcot.shape
    ff = slope.shape[1]
    return pl.pallas_call(
        functools.partial(up_back_kernel, chunk=512),
        grid_spec=pltpu.PrefetchScalarGridSpec(
            num_scalar_prefetch=1,
            grid=(count // block,),
            in_specs=[
                rows_spec(block, width),
                rows_spec(block, ff),
                rows_spec(block, width),
                rows_spec(block, width),
                rows_spec(block, 128),
                whole(large.shape),
                whole(vec.shape),
            ]
            + [pl.BlockSpec(memory_space=pl.ANY)] * len(pieces),
            out_specs=[
                rows_spec(block, ff),
                rows_spec(block, width),
                rows_spec(block, width),
                rows_spec(block, width),
                kept((8, width)),
                kept((8, ff)),
            ],
            scratch_shapes=[
                pltpu.VMEM((ff, width), BF16),
                pltpu.SemaphoreType.DMA((2 * len(pieces),)),
            ],
        ),
        out_shape=[
            jax.ShapeDtypeStruct((count, ff), BF16),
            jax.ShapeDtypeStruct((count, width), F32),
            jax.ShapeDtypeStruct((count, width), BF16),
            jax.ShapeDtypeStruct((count, width), BF16),
            jax.ShapeDtypeStruct((8, width), F32),
            jax.ShapeDtypeStruct((8, ff), F32),
        ],
        compiler_params=params(),
        cost_estimate=cost(2 * count * width * ff * 2.5, 60e6),
        name="up_back",
    )(table, dcot, slope, sum_two, normed, factor, large, vec, *pieces)


def attend_back_kernel(mcot_ref, qkv_ref, prob_ref, pcot_ref, vgrad_ref, *, seq, width):
    step = pl.program_id(0)
    rows = mcot_ref.shape[0]

    @pl.when(step == 0)
    def _():
        vgrad_ref[...] = jnp.zeros_like(vgrad_ref)

    lane = lax.broadcasted_iota(jnp.int32, (seq, 128), 1)
    first_head = lane < HEAD_DIM
    scale = 1.0 / math.sqrt(HEAD_DIM)

    def split(part):
        zero = jnp.zeros_like(part)
        return jnp.concatenate(
            [jnp.where(first_head, part, zero), jnp.where(first_head, zero, part)], axis=0
        )

    for s in range(rows // seq):
        at = slice(s * seq, (s + 1) * seq)
        for pair in range(width // 128):
            low = pair * 128
            q = split(qkv_ref[at, low : low + 128])
            k = qkv_ref[at, width + low : width + low + 128]
            v = qkv_ref[at, 2 * width + low : 2 * width + low + 128]
            cot = split(mcot_ref[at, low : low + 128])
            share = prob_ref[s, pair]
            share_cot = dot_nt(v, cot)
            pcot_ref[at, 2 * width + low : 2 * width + low + 128] = dot(share, cot).astype(BF16)
            wide = share.astype(F32)
            product = wide * share_cot
            score_cot = (product - wide * column_sum(product)).astype(BF16)
            pcot_ref[at, width + low : width + low + 128] = (dot(score_cot, q) * scale).astype(BF16)
            query_cot = dot_tn(score_cot, k) * scale
            pcot_ref[at, low : low + 128] = jnp.where(
                first_head, query_cot[:seq], query_cot[seq:]
            ).astype(BF16)
    vgrad_ref[...] += stack_rows(
        [
            column_sum(pcot_ref[:, :width].astype(F32)),
            column_sum(pcot_ref[:, 2 * width :].astype(F32)),
        ],
        8,
    )


def attend_back(mcot, qkv, prob, seq, block):
    count, width = mcot.shape
    pairs = width // 128
    return pl.pallas_call(
        functools.partial(attend_back_kernel, seq=seq, width=width),
        grid_spec=pltpu.PrefetchScalarGridSpec(
            num_scalar_prefetch=0,
            grid=(count // block,),
            in_specs=[
                rows_spec(block, width),
                rows_spec(block, 3 * width),
                pl.BlockSpec((block // seq, pairs, seq, 2 * seq), lambda i, *_: (i, 0, 0, 0)),
            ],
            out_specs=[rows_spec(block, 3 * width), kept((8, width))],
        ),
        out_shape=[
            jax.ShapeDtypeStruct((count, 3 * width), BF16),
            jax.ShapeDtypeStruct((8, width), F32),
        ],
        compiler_params=params(),
        cost_estimate=cost(2 * count * width * 3 * width * 2, 30e6),
        name="attend_back",
    )(mcot, qkv, prob)


def token_kernel(table, *refs):
    pcot_ref, one_ref = refs[:2]
    pieces = refs[2:-3]
    out_ref, w_ref, sem = refs[-3:]

    @pl.when(pl.program_id(0) == 0)
    def _():
        fetch_pieces(table, pieces, w_ref, sem, True, True)

    half = w_ref.shape[1] // 2
    cut = half - 128
    out_ref[...] = (
        one_ref[...]
        + dot_nt(pcot_ref[:, :cut], w_ref[:, :cut])
        + dot_nt(pcot_ref[:, cut:], w_ref[:, half : half + cut])
    )


def token_part(table, pcot, one_cot, pieces, block):
    count, width = one_cot.shape
    return pl.pallas_call(
        token_kernel,
        grid_spec=pltpu.PrefetchScalarGridSpec(
            num_scalar_prefetch=1,
            grid=(count // block,),
            in_specs=[rows_spec(block, 3 * width), rows_spec(block, width)]
            + [pl.BlockSpec(memory_space=pl.ANY)] * len(pieces),
            out_specs=rows_spec(block, width),
            scratch_shapes=[
                pltpu.VMEM((width, 2 * pieces[0].shape[1]), BF16),
                pltpu.SemaphoreType.DMA((2 * len(pieces),)),
            ],
        ),
        out_shape=jax.ShapeDtypeStruct((count, width), F32),
        compiler_params=params(),
        cost_estimate=cost(2 * count * width * 3 * width, 25e6),
        name="token_part",
    )(table, pcot, one_cot, *pieces)


def weight_kernel(left_ref, right_ref, out_ref, turned):
    @pl.when(pl.program_id(0) == 0)
    def _():
        turned[...] = left_ref[...].T

    out_ref[...] = dot(turned[...], right_ref[...]).astype(out_ref.dtype)


def weight_part(left, right, tile, name):
    count, height = left.shape
    width = right.shape[1]
    return pl.pallas_call(
        weight_kernel,
        grid_spec=pltpu.PrefetchScalarGridSpec(
            num_scalar_prefetch=0,
            grid=(width // tile,),
            in_specs=[
                whole((count, height)),
                pl.BlockSpec((count, tile), lambda i, *_: (0, i)),
            ],
            out_specs=pl.BlockSpec((height, tile), lambda i, *_: (0, i)),
            scratch_shapes=[pltpu.VMEM((height, count), BF16)],
        ),
        out_shape=jax.ShapeDtypeStruct((height, width), BF16),
        compiler_params=params(),
        cost_estimate=cost(2 * count * width * height, 2 * (count + height) * width),
        name=name,
    )(left, right)


def weight_pieces_kernel(table, left_ref, right_ref, *refs, steps):
    other_ref, planes, flat, turned = refs[0], refs[1:-2], refs[-2], refs[-1]
    step = pl.program_id(0)
    lines = table.shape[0] - 1
    rows = turned.shape[0] // lines

    @pl.when(step == 0)
    def _():
        flat[...] = left_ref[...].T
        for n in range(lines):
            at = pl.ds(pl.multiple_of(table[n], 16), rows)
            turned[n * rows : (n + 1) * rows] = flat[at]

    out = dot(turned[...], right_ref[...]).astype(BF16)

    @pl.when(step < steps)
    def _():
        other_ref[...] = out

    @pl.when(step >= steps)
    def _():
        for n, plane in enumerate(planes):
            height = plane.shape[0]
            plane[...] = out[n * height : (n + 1) * height]


def weight_pieces(table, left, right, tile, planes, name):
    count, height = left.shape
    half = right.shape[1] // 2
    steps = half // tile
    core_at = table.shape[0] - 1

    def columns(i, t):
        core = t[core_at]
        return (0, jnp.where(i < steps, (1 - core) * steps + i, core * steps + i - steps))

    last = steps - 1
    return pl.pallas_call(
        functools.partial(weight_pieces_kernel, steps=steps),
        grid_spec=pltpu.PrefetchScalarGridSpec(
            num_scalar_prefetch=1,
            grid=(2 * steps,),
            in_specs=[whole((count, height)), pl.BlockSpec((count, tile), columns)],
            out_specs=[pl.BlockSpec((height, tile), lambda i, t: (0, jnp.minimum(i, last)))]
            + [
                pl.BlockSpec((height // planes, tile), lambda i, t: (0, jnp.maximum(i - steps, 0)))
            ]
            * planes,
            scratch_shapes=[pltpu.VMEM((height, count), BF16)] * 2,
        ),
        out_shape=[jax.ShapeDtypeStruct((height, half), BF16)]
        + [jax.ShapeDtypeStruct((height // planes, half), BF16)] * planes,
        compiler_params=params(),
        cost_estimate=cost(2 * count * 2 * half * height, 4 * (count + height) * half),
        name=name,
    )(table, left, right)


def small_kernel(table, *refs, classes, devices):
    vin_ref, vone_ref, vtwo_ref, ugrad_ref, sgrad_ref, wsgrad_ref, pwgrad_ref, cwgrad_ref = refs[:8]
    other_ref, planes, halves = refs[8], refs[9:-1], refs[-1]
    width = vin_ref.shape[1]
    stu = sgrad_ref.shape[1]
    shard = width // devices
    group = stu // devices
    halves[0] = wsgrad_ref[...].T
    vin, vone, vtwo = vin_ref[...], vone_ref[...], vtwo_ref[...]
    rows = [vin[0:1], vin[1:2], vone[2:3], vone[0:1], vone[1:2], vtwo[2:3], vtwo[0:1], vtwo[1:2]]
    block = stack_rows(rows, 128).T
    lane = lax.broadcasted_iota(jnp.int32, (stu, 128), 1)
    high = lane >= 64
    pwgrad = pwgrad_ref[...]
    spare = jnp.zeros((classes, stu), F32)
    rest = jnp.concatenate(
        [spare, sgrad_ref[0:3], jnp.zeros((128 - classes - 3, stu), F32)], axis=0
    ).T
    rest = rest + jnp.where(lane < classes, cwgrad_ref[...], 0.0)
    for n, part in enumerate((turn_lanes(pwgrad), pwgrad, turn_lanes(rest))):
        part = jnp.where(high, part, 0.0).astype(BF16)
        block = block + dot_tn(one_hot_rows(stu, width, group, shard, n * group), part)
    ugrad = ugrad_ref[...]
    high = lax.broadcasted_iota(jnp.int32, ugrad.shape, 1) >= 64
    for n, part in enumerate((turn_lanes(ugrad), ugrad)):
        part = jnp.where(high, part, 0.0).astype(BF16)
        block = block + dot_tn(one_hot_rows(devices, width, 1, shard, 3 * group + n), part)
    halves[1] = block
    lines = table.shape[0] - 1
    core = table[lines]
    rows = width // lines
    per = lines // len(planes)
    for n in range(lines):
        at = pl.ds(pl.multiple_of(table[n], 16), rows)
        other_ref[n * rows : (n + 1) * rows] = halves[1 - core, at].astype(BF16)
        begin = (n % per) * rows
        planes[n // per][begin : begin + rows] = halves[core, at].astype(BF16)


def small_pieces(table, grads, planes, classes, devices):
    width = grads[0].shape[1]
    return pl.pallas_call(
        functools.partial(small_kernel, classes=classes, devices=devices),
        grid_spec=pltpu.PrefetchScalarGridSpec(
            num_scalar_prefetch=1,
            grid=(1,),
            in_specs=[whole(g.shape) for g in grads],
            out_specs=[kept((width, 128))] + [kept((width // planes, 128))] * planes,
            scratch_shapes=[pltpu.VMEM((2, width, 128), F32)],
        ),
        out_shape=[jax.ShapeDtypeStruct((width, 128), BF16)]
        + [jax.ShapeDtypeStruct((width // planes, 128), BF16)] * planes,
        compiler_params=params(),
        cost_estimate=cost(1e8, 2e6),
        name="small_pieces",
    )(table, *grads)


def finish_kernel(block_ref, *outs, group, classes, up_size):
    block = block_ref[...]
    shard = block.shape[0]
    columns = jnp.concatenate([block, jnp.zeros((128 - shard, 128), F32)], axis=0).T
    for n in range(8):
        outs[n][...] = columns[n : n + 1, :shard]
    outs[8][...] = block[:group, 64:]
    outs[9][...] = block[group : 2 * group, 64:]
    outs[10][...] = block[2 * group : 3 * group, 64 : 64 + classes]
    for n in range(3):
        row = columns[64 + classes + n : 64 + classes + n + 1]
        outs[11 + n][...] = row[:, 2 * group : 3 * group]
    first = min(64, up_size)
    outs[14][:, :first] = block[3 * group : 3 * group + 1, 64 : 64 + first]
    if up_size > first:
        outs[14][:, first:] = block[3 * group + 1 : 3 * group + 2, 64 : 64 + up_size - first]


def pick_kernel(table, source_ref, *refs, count):
    outs, held, sem_in, sem_out = refs[:-3], refs[-3], refs[-2], refs[-1]
    reads, writes = [], []
    for o, out in enumerate(outs):
        for j in range(count):
            n = o * count + j
            reads.append(pltpu.make_async_copy(source_ref.at[table[o, j]], held.at[n], sem_in.at[n]))
            writes.append(pltpu.make_async_copy(held.at[n], out.at[j], sem_out.at[n]))
    for copy in reads:
        copy.start()
    for read, write in zip(reads, writes):
        read.wait()
        write.start()
    for copy in writes:
        copy.wait()


def pick(table, source, outs, count):
    total = outs * count
    return pl.pallas_call(
        functools.partial(pick_kernel, count=count),
        grid_spec=pltpu.PrefetchScalarGridSpec(
            num_scalar_prefetch=1,
            grid=(1,),
            in_specs=[pl.BlockSpec(memory_space=pl.ANY)],
            out_specs=[pl.BlockSpec(memory_space=pl.ANY)] * outs,
            scratch_shapes=[
                pltpu.VMEM((total,) + source.shape[1:], source.dtype),
                pltpu.SemaphoreType.DMA((total,)),
                pltpu.SemaphoreType.DMA((total,)),
            ],
        ),
        out_shape=[jax.ShapeDtypeStruct((count,) + source.shape[1:], source.dtype)] * outs,
        compiler_params=params(),
        cost_estimate=cost(0, 2 * total * source[0].size * 2),
        name="pick",
    )(table, source)


def place_kernel(origin, position, *refs, samples):
    sources, out_ref, held, sem_in, sem_out = refs[:-4], refs[-4], refs[-3], refs[-2], refs[-1]
    for j in range(samples):
        for o, source in enumerate(sources):

            @pl.when(origin[j] == o)
            def _():
                pltpu.make_async_copy(source.at[position[j]], held.at[j], sem_in.at[j]).start()

    writes = []
    for j in range(samples):
        pltpu.make_async_copy(sources[0].at[0], held.at[j], sem_in.at[j]).wait()
        writes.append(pltpu.make_async_copy(held.at[j], out_ref.at[j], sem_out.at[j]))
        writes[-1].start()
    for copy in writes:
        copy.wait()


def place(origin, position, sources):
    samples = origin.shape[0]
    shape = sources[0].shape[1:]
    return pl.pallas_call(
        functools.partial(place_kernel, samples=samples),
        grid_spec=pltpu.PrefetchScalarGridSpec(
            num_scalar_prefetch=2,
            grid=(1,),
            in_specs=[pl.BlockSpec(memory_space=pl.ANY)] * len(sources),
            out_specs=pl.BlockSpec(memory_space=pl.ANY),
            scratch_shapes=[
                pltpu.VMEM((samples,) + shape, sources[0].dtype),
                pltpu.SemaphoreType.DMA((samples,)),
                pltpu.SemaphoreType.DMA((samples,)),
            ],
        ),
        out_shape=jax.ShapeDtypeStruct((samples,) + shape, sources[0].dtype),
        compiler_params=params(),
        cost_estimate=cost(0, 4 * samples * shape[0] * shape[1]),
        name="place",
    )(origin, position, *sources)


def routes(destination, samples, fsdp):
    group = lax.axis_index("dp")
    me = lax.axis_index("fsdp")
    capacity = 3 * samples // (2 * fsdp)
    span = fsdp * samples
    slots = lax.dynamic_slice_in_dim(destination, group * span, span).reshape(fsdp, samples)
    target = slots // samples - group * fsdp
    slot = slots % samples
    order = jnp.arange(samples, dtype=jnp.int32)
    before = order[None, :] < order[:, None]
    rank = jnp.sum(
        jnp.where((target[:, :, None] == target[:, None, :]) & before[None], 1, 0), axis=2
    ).astype(jnp.int32)
    offsets = (me + jnp.arange(1, fsdp, dtype=jnp.int32)) % fsdp
    places = jnp.arange(capacity, dtype=jnp.int32)

    def mine(table):
        return lax.dynamic_index_in_dim(table, me, 0, keepdims=False)

    my_target, my_slot, my_rank = mine(target), mine(slot), mine(rank)
    hit = (my_target[None, None, :] == offsets[:, None, None]) & (
        my_rank[None, None, :] == places[None, :, None]
    )
    out_pick = jnp.sum(jnp.where(hit, order[None, None, :], 0), axis=2).astype(jnp.int32)
    lands = (target == me)[:, :, None] & (slot[:, :, None] == order[None, None, :])
    origin_table = ((me - jnp.arange(fsdp, dtype=jnp.int32)) % fsdp)[:, None, None]
    in_origin = jnp.sum(jnp.where(lands, origin_table, 0), axis=(0, 1)).astype(jnp.int32)
    entry = jnp.where(origin_table == 0, order[None, :, None], rank[:, :, None])
    in_place = jnp.sum(jnp.where(lands, entry, 0), axis=(0, 1)).astype(jnp.int32)
    their_target = jnp.take(target, offsets, axis=0)
    their_slot = jnp.take(slot, offsets, axis=0)
    their_rank = jnp.take(rank, offsets, axis=0)
    hit = (their_target[:, None, :] == me) & (their_rank[:, None, :] == places[None, :, None])
    back_pick = jnp.sum(jnp.where(hit, their_slot[:, None, :], 0), axis=2).astype(jnp.int32)
    back_origin = ((me - my_target) % fsdp).astype(jnp.int32)
    back_place = jnp.where(back_origin == 0, my_slot, my_rank).astype(jnp.int32)
    return capacity, out_pick, in_origin, in_place, back_pick, back_origin, back_place


class Grid:
    def __init__(self, dp, fsdp):
        self.size = {"c": 2, "x": fsdp // 2}
        self.size["z"] = 4 if dp % 4 == 0 else dp
        self.size["y"] = dp // self.size["z"]
        d, f = lax.axis_index("dp"), lax.axis_index("fsdp")
        self.at = {"z": d // self.size["y"], "y": d % self.size["y"], "x": f // 2, "c": f % 2}

    def number(self, at):
        dp = at["z"] * self.size["y"] + at["y"]
        return (dp * self.size["x"] + at["x"]) * 2 + at["c"]

    def send(self, array, axis, offset):
        pairs = []
        spans = [range(self.size[a]) for a in "zyxc"]
        for place in itertools.product(*spans):
            here = dict(zip("zyxc", place))
            there = dict(here)
            there[axis] = (here[axis] + offset) % self.size[axis]
            pairs.append((self.number(here), self.number(there)))
        return lax.ppermute(array, AXES, pairs)

    def spread(self, array, axis):
        return [array] + [self.send(array, axis, o) for o in range(1, self.size[axis])]

    def ordered(self, parts, axis):
        n, at = self.size[axis], self.at[axis]
        out = []
        for j in range(n):
            pick = parts[0]
            for o in range(1, n):
                pick = jnp.where((at - o) % n == j, parts[o], pick)
            out.append(pick)
        return jnp.concatenate(out, axis=0)


def gather_pieces(grid, shard):
    half = shard.shape[1] // 2
    c = grid.at["c"]
    mine = lax.dynamic_slice_in_dim(shard, c * half, half, 1)
    other = lax.dynamic_slice_in_dim(shard, (1 - c) * half, half, 1)
    chip = grid.ordered([mine, grid.send(other, "c", 1)], "c")
    line = grid.ordered(grid.spread(chip, "x"), "x")
    columns = grid.spread(line, "z")
    planes = [[] for _ in range(grid.size["y"])]
    for part in columns:
        for o, got in enumerate(grid.spread(part, "y")):
            planes[o].append(got)
    own = [part for plane in planes for part in plane]
    far = [grid.send(jnp.concatenate(plane, axis=0), "c", 1) for plane in planes]
    return own, far


def piece_table(grid, rows, sign):
    oy, oz = jnp.meshgrid(jnp.arange(grid.size["y"]), jnp.arange(grid.size["z"]), indexing="ij")
    z = (grid.at["z"] + sign * oz.reshape(-1)) % grid.size["z"]
    y = (grid.at["y"] + sign * oy.reshape(-1)) % grid.size["y"]
    lines = (z * grid.size["y"] + y) * rows
    return jnp.concatenate([lines, jnp.reshape(grid.at["c"], (1,))]).astype(jnp.int32)


def fetch_pieces(table, pieces, w_ref, sem, begin, finish):
    own_count = sum(1 for p in pieces if p.shape[0] == pieces[0].shape[0])
    own, far = pieces[:own_count], pieces[own_count:]
    rows, half = own[0].shape
    per = own_count // len(far)
    core = table[own_count]
    copies = []
    for n in range(own_count):
        at = pl.ds(pl.multiple_of(table[n], 16), rows)
        near = pl.ds(pl.multiple_of(core * half, 128), half)
        away = pl.ds(pl.multiple_of((1 - core) * half, 128), half)
        copies.append(pltpu.make_async_copy(own[n], w_ref.at[at, near], sem.at[2 * n]))
        source = far[n // per].at[pl.ds((n % per) * rows, rows)]
        copies.append(pltpu.make_async_copy(source, w_ref.at[at, away], sem.at[2 * n + 1]))
    for copy in copies:
        if begin:
            copy.start()
    for copy in copies:
        if finish:
            copy.wait()


def add(*parts):
    total = parts[0].astype(F32)
    for part in parts[1:]:
        total = total + part.astype(F32)
    return total


def scatter_pieces(grid, other, planes):
    rows, half = planes[0].shape
    nz, nx = grid.size["z"], grid.size["x"]
    got = grid.send(other, "c", 1)
    came = []
    for o in range(1, grid.size["y"]):
        part = add(planes[o], got[o * rows : (o + 1) * rows]).astype(BF16)
        came.append(grid.send(part, "y", o))
    line = rows // nz
    terms = [planes[0], got[:rows]] + came
    cut = [add(*(t[o * line : (o + 1) * line] for t in terms)) for o in range(nz)]
    came = [grid.send(cut[o].astype(BF16), "z", o) for o in range(1, nz)]
    chip = line // nx
    line_sum = add(cut[0], *came)
    at = [(grid.at["x"] + o) % nx * chip for o in range(nx)]
    cut = [lax.dynamic_slice_in_dim(line_sum, a, chip, 0) for a in at]
    total = add(cut[0], *(grid.send(cut[o].astype(BF16), "x", o) for o in range(1, nx)))
    c = grid.at["c"]
    share = chip // 2
    mine = lax.dynamic_slice_in_dim(total, c * share, share, 0)
    far = lax.dynamic_slice_in_dim(total, (1 - c) * share, share, 0).astype(BF16)
    far = grid.send(far, "c", 1).astype(F32)
    return jnp.concatenate([jnp.where(c == 0, mine, far), jnp.where(c == 0, far, mine)], axis=1)


def exchange(parts, fsdp):
    out = []
    for o, part in enumerate(parts):
        pairs = [(m, (m + o + 1) % fsdp) for m in range(fsdp)]
        out.append(lax.ppermute(part, "fsdp", pairs))
    return out


def body(
    tokens,
    input_weight,
    query_bias,
    value_bias,
    output_weight,
    output_bias,
    first_gain,
    first_shift,
    up_weight,
    up_bias,
    down_weight,
    down_bias,
    second_gain,
    second_shift,
    student_weight,
    student_bias,
    pool_query,
    pool_weight,
    pool_bias,
    class_weight,
    class_bias,
    lengths,
    exit_layer,
    destination,
    repacked_grad,
    logits_grad,
):
    samples, seq, width = tokens.shape
    count = samples * seq
    devices = lax.axis_size("dp") * lax.axis_size("fsdp")
    fsdp = lax.axis_size("fsdp")
    ff = up_weight.shape[1]
    stu = student_weight.shape[1]
    classes = class_weight.shape[1]
    block = min(count, 256)
    wide_block = min(count, 512)
    shard = width // devices
    grid = Grid(lax.axis_size("dp"), fsdp)
    line = grid.size["x"] * 2 * shard
    table_in = piece_table(grid, line, -1)
    table_down = piece_table(grid, line * ff // width, -1)
    table_out = piece_table(grid, line, 1)
    planes = grid.size["y"]
    vectors = (
        query_bias,
        value_bias,
        output_bias,
        first_gain,
        first_shift,
        down_bias,
        second_gain,
        second_shift,
    )
    small = pack_small(vectors, up_bias, pool_weight, class_weight, (student_bias, pool_query, pool_bias))
    cut = 3 * width // 2
    own, far = gather_pieces(
        grid,
        jnp.concatenate([input_weight[:, :cut], student_weight, input_weight[:, cut:], small], axis=1),
    )
    pieces = own + far
    large = lax.all_gather(
        jnp.concatenate([output_weight, up_weight], axis=1), AXES, axis=0, tiled=True
    )
    own, far = gather_pieces(grid, down_weight)
    down_pieces = own + far

    capacity, out_pick, in_origin, in_place, back_pick, back_origin, back_place = routes(
        destination, samples, fsdp
    )
    alive = (exit_layer > LAYER).astype(jnp.int32)
    outgoing = pick(back_pick, repacked_grad, fsdp - 1, capacity)
    returned = exchange(outgoing, fsdp)
    second_cot = place(back_origin, back_place, [repacked_grad] + returned)

    rows = tokens.reshape(count, width)
    qkv, prob, mixed, vec, sv, pw, cw, ubm, ws = attend(
        lengths, table_in, rows, pieces, seq, block, stu, classes, devices
    )
    ub = jnp.broadcast_to(ubm[:, : ff // devices].reshape(1, ff), (8, ff))
    normed, factor, low, act, slope = up_part(mixed, rows, large, vec, ub, block)
    steps = count // wide_block
    lg = jnp.pad(
        logits_grad.reshape(steps, samples // steps, classes),
        ((0, 0), (0, 8 - samples // steps), (0, 128 - classes)),
    ).reshape(steps * 8, 128)
    second, sum_two, dcot, logits, vgrad_two, sgrad, wsgrad, pwgrad, cwgrad = down_part(
        lengths,
        alive,
        table_down,
        act,
        normed,
        second_cot.reshape(count, width),
        lg,
        down_pieces,
        vec,
        ws,
        sv,
        pw,
        cw,
        seq,
        wide_block,
    )
    student_logits = logits.reshape(steps, 8, 128)[:, : samples // steps, :classes].reshape(
        samples, classes
    ) + class_bias.astype(F32)
    second = second.reshape(samples, seq, width)
    leaving = pick(out_pick, second, fsdp - 1, capacity)
    arrived = exchange(leaving, fsdp)

    wd_grad = weight_part(act, dcot, 256, "down_grad")
    wd_share = lax.psum_scatter(wd_grad, AXES, scatter_dimension=0, tiled=True)
    ucot, one_cot, acot, mcot, vgrad_one, ugrad = up_back(
        table_down, dcot, slope, sum_two, normed, factor, down_pieces, large, vec, wide_block
    )
    wo_grad = weight_pieces(table_out, mixed, acot, 128, planes, "output_grad")
    wu_grad = weight_pieces(table_out, low, ucot, 512, planes, "up_grad")
    ff_grad = [jnp.concatenate(pair, axis=1) for pair in zip(wu_grad, wo_grad)]
    ff_share = scatter_pieces(grid, ff_grad[0], ff_grad[1:])
    pcot, vgrad_in = attend_back(mcot, qkv, prob, seq, block)
    ugm = jnp.pad(ugrad[0].reshape(devices, -1), ((0, 0), (0, 128 - ff // devices)))
    small_grad = small_pieces(
        table_out,
        (vgrad_in, vgrad_one, vgrad_two, ugm, sgrad, wsgrad, pwgrad, cwgrad),
        planes,
        classes,
        devices,
    )
    wi_grad = weight_pieces(table_out, rows, pcot, 384, planes, "input_grad")
    in_grad = [jnp.concatenate(pair, axis=1) for pair in zip(wi_grad, small_grad)]
    in_share = scatter_pieces(grid, in_grad[0], in_grad[1:])
    tokens_grad = token_part(table_in, pcot, one_cot, pieces, wide_block).reshape(samples, seq, width)
    repacked = place(in_origin, in_place, [second] + arrived)
    class_bias_grad = lax.psum(jnp.sum(logits_grad.astype(F32), axis=0), AXES)

    half = cut + 128
    input_share = jnp.concatenate([in_share[:, :cut], in_share[:, half : half + cut]], axis=1)
    flat = lambda size: jax.ShapeDtypeStruct((1, size), F32)
    group = stu // devices
    outs = pl.pallas_call(
        functools.partial(finish_kernel, group=group, classes=classes, up_size=ff // devices),
        out_shape=[flat(shard)] * 8
        + [
            jax.ShapeDtypeStruct((group, 64), F32),
            jax.ShapeDtypeStruct((group, 64), F32),
            jax.ShapeDtypeStruct((group, classes), F32),
        ]
        + [flat(group)] * 3
        + [flat(ff // devices)],
        name="finish",
    )(in_share[:, half + cut :])
    qb, vb, ob, g1, s1, db, g2, s2 = (o.reshape(-1) for o in outs[:8])
    up_half = ff // 2
    wu_share = jnp.concatenate(
        [ff_share[:, :up_half], ff_share[:, up_half + width // 2 : ff + width // 2]], axis=1
    )
    wo_share = jnp.concatenate(
        [ff_share[:, up_half : up_half + width // 2], ff_share[:, ff + width // 2 :]], axis=1
    )
    return (
        repacked,
        student_logits,
        tokens_grad,
        input_share,
        qb,
        vb,
        wo_share,
        ob,
        g1,
        s1,
        wu_share,
        outs[14].reshape(-1),
        wd_share.astype(F32),
        db,
        g2,
        s2,
        in_share[:, cut:half],
        outs[11].reshape(-1),
        outs[12].reshape(-1),
        jnp.concatenate(outs[8:10], axis=1),
        outs[13].reshape(-1),
        outs[10],
        class_bias_grad,
    )


def solution(mesh):
    both = P(AXES)
    matrix = P(AXES, None)
    cube = P(AXES, None, None)
    return jax.shard_map(
        body,
        mesh=mesh,
        in_specs=(
            cube,
            matrix,
            both,
            both,
            matrix,
            both,
            both,
            both,
            matrix,
            both,
            matrix,
            both,
            both,
            both,
            matrix,
            both,
            both,
            matrix,
            both,
            matrix,
            P(),
            both,
            both,
            P(),
            cube,
            matrix,
        ),
        out_specs=(
            cube,
            matrix,
            cube,
            matrix,
            both,
            both,
            matrix,
            both,
            both,
            both,
            matrix,
            both,
            matrix,
            both,
            both,
            both,
            matrix,
            both,
            both,
            matrix,
            both,
            matrix,
            P(),
        ),
        check_vma=False,
    )
```

time: 1380 us -> 620 us (0.45)
  waiting for transfers between devices: 475 us -> 138 us
  matrix products: 322 us -> 0 us
  Pallas kernels: 0 us -> 267 us
  blocking collectives: 337 us -> 71.3 us
  local copies, waits for them, and re-layouts: 170 us -> 29.8 us
  starting transfers between devices: 12.3 us -> 55 us
    reduce_scatter x3 -> x1, waiting for transfers between devices: 348 us -> 0.01 us  [body(): wd_share = lax.psum_scatter(wd_grad, AXES, scatter_dimension=0, tiled=True)]
    dot_general x67 -> x0, matrix products: 322 us -> none  [the longest x16 116 us: matmul(): return jnp.dot(left, right, preferred_element_type=jnp.float32)]
    pallas_call x0 -> x16, Pallas kernels: none -> 267 us  [the longest x3 44.9 us: weight_pieces(): pl.pallas_call(functools.partial(weight_pieces_kernel, steps=steps), grid...]
    unnamed x2 -> x0, blocking collectives: 216 us -> none
    ppermute x0 -> x42, waiting for transfers between devices: none -> 138 us  [the longest x36 138 us: send(): return lax.ppermute(array, AXES, pairs)]
    unnamed x13 -> x2, waiting for transfers between devices: 127 us -> 0.03 us
    all_gather x3 -> x0, blocking collectives: 122 us -> none  [the longest x1 41.8 us: body(): lax.all_gather(student_weight, ('dp', 'fsdp'), axis=0, tiled=True)]
    unnamed x399 -> x72, local copies, waits for them, and re-layouts: 80.5 us -> 7.16 us
  transfers between devices with their start and end apart: 12 -> 44, of which waited for: 4 -> 16; matrix products, arithmetic and copies ran while one was open for 22% -> 9% of each run, Pallas kernels for 0% -> 22%
where the time goes in v1:
time: 620 us; the launch traced here: 615 us
  Pallas kernels  267 us (43%)
  waiting for transfers between devices  138 us (22%)
  blocking collectives  71.3 us (12%)
  starting transfers between devices  55 us (9%)
  other arithmetic  39.2 us (6%)
  local copies, waits for them, and re-layouts  29.8 us (5%)
  between operations  15.3 us (2%)
    ppermute x36, waiting for transfers between devices, send(): return lax.ppermute(array, AXES, pairs)  138 us
    psum x1, blocking collectives, body(): class_bias_grad = lax.psum(jnp.sum(logits_grad.astype(F32), axis=0), AXES)  71.3 us
    ppermute x36, starting transfers between devices, send(): return lax.ppermute(array, AXES, pairs)  49.5 us
    pallas_call x3, Pallas kernels, weight_pieces(): pl.pallas_call(functools.partial(weight_pieces_kernel, steps=steps), grid...  44.9 us
    pallas_call x1, Pallas kernels, up_back(): pl.pallas_call(functools.partial(up_back_kernel, chunk=512), grid_spec=pl...  40.6 us
    pallas_call x1, Pallas kernels, up_part(): pl.pallas_call(functools.partial(up_kernel, chunk=256), grid_spec=pltpu.P...  39.6 us
    pallas_call x1, Pallas kernels, down_part(): pl.pallas_call(functools.partial(down_kernel, seq=seq), grid_spec=pltpu.P...  33.9 us
    pallas_call x1, Pallas kernels, attend(): pl.pallas_call(functools.partial(attend_kernel, seq=seq, width=width, stu...  25.5 us
  transfers between devices with their start and end apart: 44, of which 16 were waited for; matrix products, arithmetic and copies ran while one was open for 9% of the time, Pallas kernels for 22%

profile of v1, /device:TPU:0, one launch (start us, length us, event | category | flops | bytes accessed | tf_op | source)
XLA Modules:
  0.0 615.5 jit_solution(10592812347429064129)
XLA Ops:
  26.1 5.0 pick.2
  34.4 2.7 collective-permute-start.1
  37.3 5.0 collective-permute-done.1
  43.7 2.5 collective-permute-start.5
  46.2 2.7 collective-permute-start.4
  49.2 2.0 collective-permute-start.2
  52.9 2.3 collective-permute-start.18
  55.2 4.3 collective-permute-done.4.refs_4_.refs_5_
  59.4 9.3 %collective-permute-start.17 = (bf16[384,384]{1,0:T(8,128)(2,1)S(1)}, bf16[384,384]{1,0:T(8,128)(2,1)S(1)}, u32[]{:S(2)}, u32[]{:S(2)}) collective-permute-start(bf16[384,384]{1,0:T(8,128)(2,1)S(1)} %pad_maximum_fusion.4.refs_9_.refs_7_), channel_id=1, source_target_pairs={{0,16},{1,17},{2,18},{3,19},{4,20},{5,21},{6,22},{7,23},{8,24},{9,... | collective-permute-start | bytes 884744 | tf_op jit(solution)/shard_map/ppermute | solution.py:944
  69.3 24.0 %collective-permute-done.3.refs_3_.refs_4_ = bf16[96,1280]{1,0:T(8,128)(2,1)S(1)} collective-permute-done((bf16[96,1280]{1,0:T(8,128)(2,1)S(1)}, bf16[96,1280]{1,0:T(8,128)(2,1)S(1)}, u32[]{:S(2)}, u32[]{:S(2)}) %collective-permute-start.3) | collective-permute-done | bytes 245792 | tf_op jit(solution)/shard_map/ppermute | solution.py:944
  94.1 2.0 collective-permute-start.6
  96.2 17.5 %collective-permute-done.17.refs_11_.refs_9_ = bf16[384,384]{1,0:T(8,128)(2,1)S(1)} collective-permute-done((bf16[384,384]{1,0:T(8,128)(2,1)S(1)}, bf16[384,384]{1,0:T(8,128)(2,1)S(1)}, u32[]{:S(2)}, u32[]{:S(2)}) %collective-permute-start.17) | collective-permute-done | bytes 294944 | tf_op jit(solution)/shard_map/ppermute | solution.py:944
  119.8 3.9 collective-permute-done.22.refs_16_.refs_14_
  125.5 3.8 collective-permute-done.21.refs_15_.refs_13_
  129.3 3.1 collective-permute-done.20.refs_14_.refs_12_
  133.0 71.3 %psum.7 = f32[14]{0:T(128)} all-reduce(f32[14]{0:T(128)} %convert_reduce_fusion), channel_id=1, replica_groups=mesh['dp'=8,'fsdp'=4] {'dp','fsdp'}, use_global_device_ids=true, to_apply=%region_7.9 | all-reduce | flops 14 | bytes 112 | tf_op jit(solution)/shard_map/psum | solution.py:1180
  212.4 2.2 pad_maximum_fusion.2
  216.5 3.8 place.2
  220.4 25.5 %attend.1 = (bf16[2048,2304]{1,0:T(8,128)(2,1)}, bf16[16,6,128,256]{3,2,1,0:T(8,128)(2,1)}, bf16[2048,768]{1,0:T(8,128)(2,1)}, f32[8,768]{1,0:T(8,128)}, f32[8,1...) custom-call(s32[16]{0:T(128)} %lens.3, ...), custom_call_target="tpu_custom_call" | custom-call | flops 14495514624 | bytes 30000000 | tf_op jit(solution)/shard_map/attend/pallas_call | solution.py:221
  247.3 39.6 %up_part.1 = (f32[2048,768]{1,0:T(8,128)}, f32[2048,128]{1,0:T(8,128)}, bf16[2048,768]{1,0:T(8,128)(2,1)}, bf16[2048,3072]{1,0:T(8,128)(2,1)}, bf16[2048,3072]{1,0:T(8,128)(2,1)}) custom-call(bf16[2048,768]{1,0:T(8,128)(2,1)} %get-tuple-element.88.mixed_ref.left_ref, bf16[2048,768]{1,0:T(8,128)(2,1)} %bitcast.61, ...), custom_call_target="tpu_custom_call" | custom-call | flops 24159191040 | bytes 50000000 | tf_op jit(solution)/shard_map/up_part/pallas_call | solution.py:274
  286.9 33.9 %down_part.1 = (bf16[2048,768]{1,0:T(8,128)(2,1)}, f32[2048,768]{1,0:T(8,128)}, bf16[2048,768]{1,0:T(8,128)(2,1)}, f32[32,128]{1,0:T(8,128)}, f32[8,768]{1,0:T(8...) custom-call(s32[16]{0:T(128)} %lens.3, s32[16]{0:T(128)} %compare_convert_fusion.alive, ...), custom_call_target="tpu_custom_call" | custom-call | flops 19327352832 | bytes 40000000 | tf_op jit(solution)/shard_map/down_part/pallas_call | solution.py:402
  321.6 40.6 %up_back.1 = (bf16[2048,3072]{1,0:T(8,128)(2,1)}, f32[2048,768]{1,0:T(8,128)}, bf16[2048,768]{1,0:T(8,128)(2,1)}, bf16[2048,768]{1,0:T(8,128)(2,1)}, f32[8,768]{1,0:T(8,128)}, /*index=5*/f32[8,3072]{1,0:T(8,128)}) custom-call(s32[9]{0:T(128)} %pad_add_fusion.table, bf16[2048,768]{1,0:T(8,128)(2,1)} %get-tuple-element.105.refs_0_.right_ref, ...), custom_call_target="tpu_custom_call" | custom-call | flops 24159191040 | bytes 60000000 | tf_op jit(solution)/shard_map/up_back/pallas_call | solution.py:488
  363.2 11.2 %output_grad.1 = (bf16[768,384]{1,0:T(8,128)(2,1)}, bf16[384,384]{1,0:T(8,128)(2,1)}, bf16[384,384]{1,0:T(8,128)(2,1)}) custom-call(s32[9]{0:T(128)} %pad_add_fusion.2.table, bf16[2048,768]{1,0:T(8,128)(2,1)} %get-tuple-element.88.mixed_ref.left_ref, bf16[2048,768]{1,0:T(8,128)(2,1)} %get-tuple-element.133.right_ref), custom_call_target="tpu_custom_call" | custom-call | flops 2415919104 | bytes 4325376 | tf_op jit(solution)/shard_map/output_grad/pallas_call | solution.py:708
  374.4 23.6 %attend_back.1 = (bf16[2048,2304]{1,0:T(8,128)(2,1)}, f32[8,768]{1,0:T(8,128)}) custom-call(bf16[2048,768]{1,0:T(8,128)(2,1)} %get-tuple-element.109.mcot_ref, bf16[2048,2304]{1,0:T(8,128)(2,1)} %get-tuple-element.110.qkv_ref, bf16[16,6,128,256]{3,2,1,0:T(8,128)(2,1)} %get-tuple-element.111.prob_ref), custom_call_target="tpu_custom_call" | custom-call | flops 14495514624 | bytes 30000000 | tf_op jit(solution)/shard_map/attend_back/pallas_call | solution.py:579
  397.9 16.6 %input_grad.1 = (bf16[768,1152]{1,0:T(8,128)(2,1)}, bf16[384,1152]{1,0:T(8,128)(2,1)}, bf16[384,1152]{1,0:T(8,128)(2,1)}) custom-call(s32[9]{0:T(128)} %pad_add_fusion.2.table, bf16[2048,768]{1,0:T(8,128)(2,1)} %bitcast.62, bf16[2048,2304]{1,0:T(8,128)(2,1)} %get-tuple-element.112.refs_0_.right_ref), custom_call_target="tpu_custom_call" | custom-call | flops 7247757312 | bytes 12976128 | tf_op jit(solution)/shard_map/input_grad/pallas_call | solution.py:708
  415.1 3.2 small_pieces.1
  418.4 3.1 pad_maximum_fusion.1
  421.6 17.2 %up_grad.1 = (bf16[768,1536]{1,0:T(8,128)(2,1)}, bf16[384,1536]{1,0:T(8,128)(2,1)}, bf16[384,1536]{1,0:T(8,128)(2,1)}) custom-call(s32[9]{0:T(128)} %pad_add_fusion.2.table, bf16[2048,768]{1,0:T(8,128)(2,1)} %get-tuple-element.130.left_ref, bf16[2048,3072]{1,0:T(8,128)(2,1)} %get-tuple-element.131.right_ref), custom_call_target="tpu_custom_call" | custom-call | flops 9663676416 | bytes 17301504 | tf_op jit(solution)/shard_map/up_grad/pallas_call | solution.py:708
  438.8 3.5 pad_maximum_fusion
  442.6 20.4 %down_grad.1 = bf16[3072,768]{1,0:T(8,128)(2,1)} custom-call(bf16[2048,3072]{1,0:T(8,128)(2,1)} %get-tuple-element.91.refs_0_.left_ref, bf16[2048,768]{1,0:T(8,128)(2,1)} %get-tuple-element.105.refs_0_.right_ref), custom_call_target="tpu_custom_call" | custom-call | flops 9663676416 | bytes 7864320 | tf_op jit(solution)/shard_map/down_grad/pallas_call | solution.py:652
  463.1 4.4 pick.3
  467.7 2.3 collective-permute-start.26
  474.1 16.3 %token_part.1 = f32[2048,768]{1,0:T(8,128)} custom-call(s32[9]{0:T(128)} %pad_add_fusion.1.table, bf16[2048,2304]{1,0:T(8,128)(2,1)} %get-tuple-element.112.refs_0_.right_ref, f32[2048,768]{1,0:T(8,128)} %get-tuple-element.113.refs_1_, bf16[96,1280]{1,0:T(8,128)(2,1)} %copy-done.18, bf16[96,1280]{1,0:T(8,128)(2,1)} %copy-done.22, ...), custom_call_target="tpu_custom_call" | custom-call | flops 7247757312 | bytes 25000000 | tf_op jit(solution)/shard_map/token_part/pallas_call | solution.py:621
  490.5 5.7 collective-permute-done.29
  497.7 2.1 collective-permute-start.30
  499.8 1.9 collective-permute-start.32
  501.7 6.7 %collective-permute-done.30 = bf16[96,1280]{1,0:T(8,128)(2,1)S(1)} collective-permute-done((bf16[96,1280]{1,0:T(8,128)(2,1)S(1)}, bf16[96,1280]{1,0:T(8,128)(2,1)S(1)}, u32[]{:S(2)}, u32[]{:S(2)}) %collective-permute-start.30) | collective-permute-done | bytes 245792 | tf_op jit(solution)/shard_map/ppermute | solution.py:944
  508.4 6.6 %collective-permute-start.31 = (bf16[96,1280]{1,0:T(8,128)(2,1)S(1)}, bf16[96,1280]{1,0:T(8,128)(2,1)S(1)}, u32[]{:S(2)}, u32[]{:S(2)}) collective-permute-start(bf16[96,1280]{1,0:T(8,128)(2,1)S(1)} %get-tuple-element.174), channel_id=1, source_target_pairs={{0,16},{1,17},{2,18},{3,19},{4,20},{5,21},{6,22},{7,23},{8,24},{9,... | collective-permute-start | bytes 737288 | tf_op jit(solution)/shard_map/ppermute | solution.py:944
  515.1 2.9 add_convert_fusion
  519.8 7.5 %collective-permute-done.31 = bf16[96,1280]{1,0:T(8,128)(2,1)S(1)} collective-permute-done((bf16[96,1280]{1,0:T(8,128)(2,1)S(1)}, bf16[96,1280]{1,0:T(8,128)(2,1)S(1)}, u32[]{:S(2)}, u32[]{:S(2)}) %collective-permute-start.31) | collective-permute-done | bytes 245792 | tf_op jit(solution)/shard_map/ppermute | solution.py:944
  530.0 4.1 place.3
  534.3 23.4 %collective-permute-done.36 = bf16[384,1920]{1,0:T(8,128)(2,1)} collective-permute-done((bf16[384,1920]{1,0:T(8,128)(2,1)}, bf16[384,1920]{1,0:T(8,128)(2,1)}, u32[]{:S(2)}, u32[]{:S(2)}) %collective-permute-start.36) | collective-permute-done | bytes 1474592 | tf_op jit(solution)/shard_map/ppermute | solution.py:944
  557.7 2.7 add_convert_fusion.4
  560.4 3.1 collective-permute-start.37
  567.7 6.3 %collective-permute-done.37 = bf16[96,1920]{1,0:T(8,128)(2,1)S(1)} collective-permute-done((bf16[96,1920]{1,0:T(8,128)(2,1)}, bf16[96,1920]{1,0:T(8,128)(2,1)S(1)}, u32[]{:S(2)}, u32[]{:S(2)}) %collective-permute-start.37) | collective-permute-done | bytes 368672 | tf_op jit(solution)/shard_map/ppermute | solution.py:944
  574.0 9.9 %collective-permute-done.39 = bf16[96,1920]{1,0:T(8,128)(2,1)S(1)} collective-permute-done((bf16[96,1920]{1,0:T(8,128)(2,1)S(1)}, bf16[96,1920]{1,0:T(8,128)(2,1)S(1)}, u32[]{:S(2)}, u32[]{:S(2)}) %collective-permute-start.39) | collective-permute-done | bytes 368672 | tf_op jit(solution)/shard_map/ppermute | solution.py:944
  583.8 12.6 %collective-permute-done.38 = bf16[96,1920]{1,0:T(8,128)(2,1)S(1)} collective-permute-done((bf16[96,1920]{1,0:T(8,128)(2,1)S(1)}, bf16[96,1920]{1,0:T(8,128)(2,1)S(1)}, u32[]{:S(2)}, u32[]{:S(2)}) %collective-permute-start.38) | collective-permute-done | bytes 368672 | tf_op jit(solution)/shard_map/ppermute | solution.py:944
  600.0 3.6 collective-permute-done.40
  (246 shorter events, 72.4 us)
Async XLA Ops:
  7.2 239.4 %all-gather.2.cloned.1.call-start = ((), (), s32[]{:S(2)}) async-start(), calls=%async_computation.1 | async-start | bytes 6082560 | tf_op jit(solution)/shard_map/all_gather | solution.py:1108
  8.9 597.7 %reduce-scatter.2.cloned.1.call-start = ((), (), s32[]{:S(2)}) async-start(), calls=%async_computation.2 | async-start | bytes 4866048 | tf_op jit(solution)/shard_map/reduce_scatter | solution.py:1158
  9.8 27.3 %collective-permute-start.14 = (bf16[96,384]{1,0:T(8,128)(2,1)S(1)}, bf16[96,384]{1,0:T(8,128)(2,1)S(1)}, u32[]{:S(2)}, u32[]{:S(2)}) collective-permute-start(bf16[96,384]{1,0:T(8,128)(2,1)S(1)} %constant_dynamic-slice_fusion), channel_id=1, source_target_pairs={{0,1},{1,0},{2,3},{3,2},{4,5},{5,4},{6,7},{7,6},{8,9},{9,8},{10,11... | collective-permute-start | bytes 221192 | tf_op jit(solution)/shard_map/ppermute | solution.py:944
  21.9 12.5 %collective-permute-start = (bf16[24,1280]{1,0:T(8,128)(2,1)S(1)}, bf16[24,1280]{1,0:T(8,128)(2,1)S(1)}, u32[]{:S(2)}, u32[]{:S(2)}) collective-permute-start(bf16[24,1280]{1,0:T(8,128)(2,1)S(1)} %constant_dynamic-slice_fusion.4), channel_id=1, source_target_pairs={{0,1},{1,0},{2,3},{3,2},{4,5},{5,4},{6,7},{7,6},{8,9},{9,8},{10,11... | collective-permute-start | bytes 184328 | tf_op jit(solution)/shard_map/ppermute | solution.py:944
  34.4 7.9 %collective-permute-start.1 = (bf16[48,1280]{1,0:T(8,128)(2,1)S(1)}, bf16[48,1280]{1,0:T(8,128)(2,1)S(1)}, u32[]{:S(2)}, u32[]{:S(2)}) collective-permute-start(bf16[48,1280]{1,0:T(8,128)(2,1)S(1)} %pad_maximum_fusion.10), channel_id=1, source_target_pairs={{0,2},{1,3},{2,0},{3,1},{4,6},{5,7},{6,4},{7,5},{8,10},{9,11},{10,... | collective-permute-start | bytes 368648 | tf_op jit(solution)/shard_map/ppermute | solution.py:944
  37.2 14.0 %collective-permute-start.15 = (bf16[192,384]{1,0:T(8,128)(2,1)S(1)}, bf16[192,384]{1,0:T(8,128)(2,1)S(1)}, u32[]{:S(2)}, u32[]{:S(2)}) collective-permute-start(bf16[192,384]{1,0:T(8,128)(2,1)S(1)} %pad_maximum_fusion.9), channel_id=1, source_target_pairs={{0,2},{1,3},{2,0},{3,1},{4,6},{5,7},{6,4},{7,5},{8,10},{9,11},{10,... | collective-permute-start | bytes 442376 | tf_op jit(solution)/shard_map/ppermute | solution.py:944
  43.7 80.0 %copy-start.18 = (bf16[96,1280]{1,0:T(8,128)(2,1)}, bf16[96,1280]{1,0:T(8,128)(2,1)S(1)}, u32[]{:S(2)}) copy-start(bf16[96,1280]{1,0:T(8,128)(2,1)S(1)} %pad_maximum_fusion.6.refs_1_.refs_2_) | copy-start | bytes 737284
  43.7 9.2 %collective-permute-start.5 = (bf16[96,1280]{1,0:T(8,128)(2,1)S(1)}, bf16[96,1280]{1,0:T(8,128)(2,1)S(1)}, u32[]{:S(2)}, u32[]{:S(2)}) collective-permute-start(bf16[96,1280]{1,0:T(8,128)(2,1)S(1)} %pad_maximum_fusion.6.refs_1_.refs_2_), channel_id=1, source_target_pairs={{0,4},{1,5},{2,6},{3,7},{4,0},{5,1},{6,2},{7,3},{8,12},{9,13},{10,... | collective-permute-start | bytes 737288 | tf_op jit(solution)/shard_map/ppermute | solution.py:944
  46.2 13.3 %collective-permute-start.4 = (bf16[96,1280]{1,0:T(8,128)(2,1)S(1)}, bf16[96,1280]{1,0:T(8,128)(2,1)S(1)}, u32[]{:S(2)}, u32[]{:S(2)}) collective-permute-start(bf16[96,1280]{1,0:T(8,128)(2,1)S(1)} %pad_maximum_fusion.6.refs_1_.refs_2_), channel_id=1, source_target_pairs={{0,24},{1,25},{2,26},{3,27},{4,28},{5,29},{6,30},{7,31},{8,0},{9,1... | collective-permute-start | bytes 737288 | tf_op jit(solution)/shard_map/ppermute | solution.py:944
  48.9 44.4 %collective-permute-start.3 = (bf16[96,1280]{1,0:T(8,128)(2,1)S(1)}, bf16[96,1280]{1,0:T(8,128)(2,1)S(1)}, u32[]{:S(2)}, u32[]{:S(2)}) collective-permute-start(bf16[96,1280]{1,0:T(8,128)(2,1)S(1)} %pad_maximum_fusion.6.refs_1_.refs_2_), channel_id=1, source_target_pairs={{0,16},{1,17},{2,18},{3,19},{4,20},{5,21},{6,22},{7,23},{8,24},{9,... | collective-permute-start | bytes 737288 | tf_op jit(solution)/shard_map/ppermute | solution.py:944
  49.2 44.1 %collective-permute-start.2 = (bf16[96,1280]{1,0:T(8,128)(2,1)S(1)}, bf16[96,1280]{1,0:T(8,128)(2,1)S(1)}, u32[]{:S(2)}, u32[]{:S(2)}) collective-permute-start(bf16[96,1280]{1,0:T(8,128)(2,1)S(1)} %pad_maximum_fusion.6.refs_1_.refs_2_), channel_id=1, source_target_pairs={{0,8},{1,9},{2,10},{3,11},{4,12},{5,13},{6,14},{7,15},{8,16},{9,17... | collective-permute-start | bytes 737288 | tf_op jit(solution)/shard_map/ppermute | solution.py:944
  52.6 71.0 %copy-start.14 = (bf16[384,384]{1,0:T(8,128)(2,1)}, bf16[384,384]{1,0:T(8,128)(2,1)S(1)}, u32[]{:S(2)}) copy-start(bf16[384,384]{1,0:T(8,128)(2,1)S(1)} %pad_maximum_fusion.4.refs_9_.refs_7_) | copy-start | bytes 884740
  52.6 41.5 %collective-permute-start.19 = (bf16[384,384]{1,0:T(8,128)(2,1)S(1)}, bf16[384,384]{1,0:T(8,128)(2,1)S(1)}, u32[]{:S(2)}, u32[]{:S(2)}) collective-permute-start(bf16[384,384]{1,0:T(8,128)(2,1)S(1)} %pad_maximum_fusion.4.refs_9_.refs_7_), channel_id=1, source_target_pairs={{0,4},{1,5},{2,6},{3,7},{4,0},{5,1},{6,2},{7,3},{8,12},{9,13},{10,... | collective-permute-start | bytes 884744 | tf_op jit(solution)/shard_map/ppermute | solution.py:944
  52.9 76.4 %copy-start.19 = (bf16[96,1280]{1,0:T(8,128)(2,1)}, bf16[96,1280]{1,0:T(8,128)(2,1)S(1)}, u32[]{:S(2)}) copy-start(bf16[96,1280]{1,0:T(8,128)(2,1)S(1)} %collective-permute-done.5.refs_5_.refs_6_) | copy-start | bytes 737284
  52.9 43.2 %collective-permute-start.18 = (bf16[384,384]{1,0:T(8,128)(2,1)S(1)}, bf16[384,384]{1,0:T(8,128)(2,1)S(1)}, u32[]{:S(2)}, u32[]{:S(2)}) collective-permute-start(bf16[384,384]{1,0:T(8,128)(2,1)S(1)} %pad_maximum_fusion.4.refs_9_.refs_7_), channel_id=1, source_target_pairs={{0,24},{1,25},{2,26},{3,27},{4,28},{5,29},{6,30},{7,31},{8,0},{9,1... | collective-permute-start | bytes 884744 | tf_op jit(solution)/shard_map/ppermute | solution.py:944
  59.4 64.2 %copy-start.20 = (bf16[96,1280]{1,0:T(8,128)(2,1)}, bf16[96,1280]{1,0:T(8,128)(2,1)S(1)}, u32[]{:S(2)}) copy-start(bf16[96,1280]{1,0:T(8,128)(2,1)S(1)} %collective-permute-done.4.refs_4_.refs_5_) | copy-start | bytes 737284
  59.4 54.3 %collective-permute-start.17 = (bf16[384,384]{1,0:T(8,128)(2,1)S(1)}, bf16[384,384]{1,0:T(8,128)(2,1)S(1)}, u32[]{:S(2)}, u32[]{:S(2)}) collective-permute-start(bf16[384,384]{1,0:T(8,128)(2,1)S(1)} %pad_maximum_fusion.4.refs_9_.refs_7_), channel_id=1, source_target_pairs={{0,16},{1,17},{2,18},{3,19},{4,20},{5,21},{6,22},{7,23},{8,24},{9,... | collective-permute-start | bytes 884744 | tf_op jit(solution)/shard_map/ppermute | solution.py:944
  93.2 22.1 %collective-permute-start.16 = (bf16[384,384]{1,0:T(8,128)(2,1)S(1)}, bf16[384,384]{1,0:T(8,128)(2,1)}, u32[]{:S(2)}, u32[]{:S(2)}) collective-permute-start(bf16[384,384]{1,0:T(8,128)(2,1)S(1)} %pad_maximum_fusion.4.refs_9_.refs_7_), channel_id=1, source_target_pairs={{0,8},{1,9},{2,10},{3,11},{4,12},{5,13},{6,14},{7,15},{8,16},{9,17... | collective-permute-start | bytes 884744 | tf_op jit(solution)/shard_map/ppermute | solution.py:944
  93.3 23.2 %collective-permute-start.8 = (bf16[96,1280]{1,0:T(8,128)(2,1)S(1)}, bf16[96,1280]{1,0:T(8,128)(2,1)S(1)}, u32[]{:S(2)}, u32[]{:S(2)}) collective-permute-start(bf16[96,1280]{1,0:T(8,128)(2,1)S(1)} %collective-permute-done.4.refs_4_.refs_5_), channel_id=1, source_target_pairs={{0,4},{1,5},{2,6},{3,7},{4,0},{5,1},{6,2},{7,3},{8,12},{9,13},{10,... | collective-permute-start | bytes 737288 | tf_op jit(solution)/shard_map/ppermute | solution.py:944
  94.1 24.0 %collective-permute-start.6 = (bf16[96,1280]{1,0:T(8,128)(2,1)S(1)}, bf16[96,1280]{1,0:T(8,128)(2,1)S(1)}, u32[]{:S(2)}, u32[]{:S(2)}) collective-permute-start(bf16[96,1280]{1,0:T(8,128)(2,1)S(1)} %collective-permute-done.2.refs_2_.refs_3_), channel_id=1, source_target_pairs={{0,4},{1,5},{2,6},{3,7},{4,0},{5,1},{6,2},{7,3},{8,12},{9,13},{10,... | collective-permute-start | bytes 737288 | tf_op jit(solution)/shard_map/ppermute | solution.py:944
  96.1 22.0 %collective-permute-start.7 = (bf16[96,1280]{1,0:T(8,128)(2,1)S(1)}, bf16[96,1280]{1,0:T(8,128)(2,1)S(1)}, u32[]{:S(2)}, u32[]{:S(2)}) collective-permute-start(bf16[96,1280]{1,0:T(8,128)(2,1)S(1)} %collective-permute-done.3.refs_3_.refs_4_), channel_id=1, source_target_pairs={{0,4},{1,5},{2,6},{3,7},{4,0},{5,1},{6,2},{7,3},{8,12},{9,13},{10,... | collective-permute-start | bytes 737288 | tf_op jit(solution)/shard_map/ppermute | solution.py:944
  113.7 9.9 %collective-permute-start.22 = (bf16[384,384]{1,0:T(8,128)(2,1)S(1)}, bf16[384,384]{1,0:T(8,128)(2,1)S(1)}, u32[]{:S(2)}, u32[]{:S(2)}) collective-permute-start(bf16[384,384]{1,0:T(8,128)(2,1)S(1)} %collective-permute-done.18.refs_12_.refs_10_), channel_id=1, source_target_pairs={{0,4},{1,5},{2,6},{3,7},{4,0},{5,1},{6,2},{7,3},{8,12},{9,13},{10,... | collective-permute-start | bytes 884744 | tf_op jit(solution)/shard_map/ppermute | solution.py:944
  115.4 13.9 %collective-permute-start.21 = (bf16[384,384]{1,0:T(8,128)(2,1)S(1)}, bf16[384,384]{1,0:T(8,128)(2,1)}, u32[]{:S(2)}, u32[]{:S(2)}) collective-permute-start(bf16[384,384]{1,0:T(8,128)(2,1)S(1)} %collective-permute-done.17.refs_11_.refs_9_), channel_id=1, source_target_pairs={{0,4},{1,5},{2,6},{3,7},{4,0},{5,1},{6,2},{7,3},{8,12},{9,13},{10,... | collective-permute-start | bytes 884744 | tf_op jit(solution)/shard_map/ppermute | solution.py:944
  116.4 16.0 %collective-permute-start.20 = (bf16[384,384]{1,0:T(8,128)(2,1)}, bf16[384,384]{1,0:T(8,128)(2,1)}, u32[]{:S(2)}, u32[]{:S(2)}) collective-permute-start(bf16[384,384]{1,0:T(8,128)(2,1)} %collective-permute-done.16.refs_10_.refs_8_), channel_id=1, source_target_pairs={{0,4},{1,5},{2,6},{3,7},{4,0},{5,1},{6,2},{7,3},{8,12},{9,13},{10,... | collective-permute-start | bytes 884744 | tf_op jit(solution)/shard_map/ppermute | solution.py:944
  118.1 96.6 %collective-permute-start.11 = (bf16[6,128,768]{2,1,0:T(8,128)(2,1)}, bf16[6,128,768]{2,1,0:T(8,128)(2,1)S(1)}, u32[]{:S(2)}, u32[]{:S(2)}) collective-permute-start(bf16[6,128,768]{2,1,0:T(8,128)(2,1)} %get-tuple-element.93), channel_id=1, source_target_pairs={{0,1},{1,2},{2,3},{3,0},{4,5},{5,6},{6,7},{7,4},{8,9},{9,10},{10,1... | collective-permute-start | bytes 3538952 | tf_op jit(solution)/shard_map/ppermute | solution.py:1043
  118.1 96.6 %collective-permute-start.12 = (bf16[6,128,768]{2,1,0:T(8,128)(2,1)}, bf16[6,128,768]{2,1,0:T(8,128)(2,1)S(1)}, u32[]{:S(2)}, u32[]{:S(2)}) collective-permute-start(bf16[6,128,768]{2,1,0:T(8,128)(2,1)} %get-tuple-element.94), channel_id=1, source_target_pairs={{0,2},{1,3},{2,0},{3,1},{4,6},{5,7},{6,4},{7,5},{8,10},{9,11},{10,... | collective-permute-start | bytes 3538952 | tf_op jit(solution)/shard_map/ppermute | solution.py:1043
  124.4 90.8 %collective-permute-start.13 = (bf16[6,128,768]{2,1,0:T(8,128)(2,1)}, bf16[6,128,768]{2,1,0:T(8,128)(2,1)S(1)}, u32[]{:S(2)}, u32[]{:S(2)}) collective-permute-start(bf16[6,128,768]{2,1,0:T(8,128)(2,1)} %get-tuple-element.95), channel_id=1, source_target_pairs={{0,3},{1,0},{2,1},{3,2},{4,7},{5,4},{6,5},{7,6},{8,11},{9,8},{10,9... | collective-permute-start | bytes 3538952 | tf_op jit(solution)/shard_map/ppermute | solution.py:1043
  129.3 91.1 %collective-permute-start.9 = (bf16[384,1280]{1,0:T(8,128)(2,1)}, bf16[384,1280]{1,0:T(8,128)(2,1)}, u32[]{:S(2)}, u32[]{:S(2)}) collective-permute-start(bf16[384,1280]{1,0:T(8,128)(2,1)} %constant_dynamic-update-slice_fusion), channel_id=1, source_target_pairs={{0,1},{1,0},{2,3},{3,2},{4,5},{5,4},{6,7},{7,6},{8,9},{9,8},{10,11... | collective-permute-start | bytes 2949128 | tf_op jit(solution)/shard_map/ppermute | solution.py:944
  132.4 87.9 %collective-permute-start.10 = (bf16[384,1280]{1,0:T(8,128)(2,1)}, bf16[384,1280]{1,0:T(8,128)(2,1)}, u32[]{:S(2)}, u32[]{:S(2)}) collective-permute-start(bf16[384,1280]{1,0:T(8,128)(2,1)} %pad_maximum_fusion.3), channel_id=1, source_target_pairs={{0,1},{1,0},{2,3},{3,2},{4,5},{5,4},{6,7},{7,6},{8,9},{9,8},{10,11... | collective-permute-start | bytes 2949128 | tf_op jit(solution)/shard_map/ppermute | solution.py:944
  214.7 72.3 %collective-permute-start.23 = (bf16[1536,384]{1,0:T(8,128)(2,1)}, bf16[1536,384]{1,0:T(8,128)(2,1)}, u32[]{:S(2)}, u32[]{:S(2)}) collective-permute-start(bf16[1536,384]{1,0:T(8,128)(2,1)} %constant_dynamic-update-slice_fusion.5), channel_id=1, source_target_pairs={{0,1},{1,0},{2,3},{3,2},{4,5},{5,4},{6,7},{7,6},{8,9},{9,8},{10,11... | collective-permute-start | bytes 3538952 | tf_op jit(solution)/shard_map/ppermute | solution.py:944
  214.7 72.2 %collective-permute-start.24 = (bf16[1536,384]{1,0:T(8,128)(2,1)}, bf16[1536,384]{1,0:T(8,128)(2,1)}, u32[]{:S(2)}, u32[]{:S(2)}) collective-permute-start(bf16[1536,384]{1,0:T(8,128)(2,1)} %pad_maximum_fusion.2), channel_id=1, source_target_pairs={{0,1},{1,0},{2,3},{3,2},{4,5},{5,4},{6,7},{7,6},{8,9},{9,8},{10,11... | collective-permute-start | bytes 3538952 | tf_op jit(solution)/shard_map/ppermute | solution.py:944
  421.5 49.9 %collective-permute-start.28 = (bf16[768,1280]{1,0:T(8,128)(2,1)}, bf16[768,1280]{1,0:T(8,128)(2,1)S(1)}, u32[]{:S(2)}, u32[]{:S(2)}) collective-permute-start(bf16[768,1280]{1,0:T(8,128)(2,1)} %pad_maximum_fusion.1), channel_id=1, source_target_pairs={{0,1},{1,0},{2,3},{3,2},{4,5},{5,4},{6,7},{7,6},{8,9},{9,8},{10,11... | collective-permute-start | bytes 5898248 | tf_op jit(solution)/shard_map/ppermute | solution.py:944
  442.2 57.6 %collective-permute-start.35 = (bf16[768,1920]{1,0:T(8,128)(2,1)}, bf16[768,1920]{1,0:T(8,128)(2,1)}, u32[]{:S(2)}, u32[]{:S(2)}) collective-permute-start(bf16[768,1920]{1,0:T(8,128)(2,1)} %pad_maximum_fusion), channel_id=1, source_target_pairs={{0,1},{1,0},{2,3},{3,2},{4,5},{5,4},{6,7},{7,6},{8,9},{9,8},{10,11... | collective-permute-start | bytes 8847368 | tf_op jit(solution)/shard_map/ppermute | solution.py:944
  467.5 62.5 %collective-permute-start.25 = (bf16[6,128,768]{2,1,0:T(8,128)(2,1)}, bf16[6,128,768]{2,1,0:T(8,128)(2,1)}, u32[]{:S(2)}, u32[]{:S(2)}) collective-permute-start(bf16[6,128,768]{2,1,0:T(8,128)(2,1)} %get-tuple-element.101), channel_id=1, source_target_pairs={{0,1},{1,2},{2,3},{3,0},{4,5},{5,6},{6,7},{7,4},{8,9},{9,10},{10,1... | collective-permute-start | bytes 3538952 | tf_op jit(solution)/shard_map/ppermute | solution.py:1043
  467.7 62.3 %collective-permute-start.26 = (bf16[6,128,768]{2,1,0:T(8,128)(2,1)}, bf16[6,128,768]{2,1,0:T(8,128)(2,1)}, u32[]{:S(2)}, u32[]{:S(2)}) collective-permute-start(bf16[6,128,768]{2,1,0:T(8,128)(2,1)} %get-tuple-element.102), channel_id=1, source_target_pairs={{0,2},{1,3},{2,0},{3,1},{4,6},{5,7},{6,4},{7,5},{8,10},{9,11},{10,... | collective-permute-start | bytes 3538952 | tf_op jit(solution)/shard_map/ppermute | solution.py:1043
  470.0 60.0 %collective-permute-start.27 = (bf16[6,128,768]{2,1,0:T(8,128)(2,1)}, bf16[6,128,768]{2,1,0:T(8,128)(2,1)}, u32[]{:S(2)}, u32[]{:S(2)}) collective-permute-start(bf16[6,128,768]{2,1,0:T(8,128)(2,1)} %get-tuple-element.103), channel_id=1, source_target_pairs={{0,3},{1,0},{2,1},{3,2},{4,7},{5,4},{6,5},{7,6},{8,11},{9,8},{10,9... | collective-permute-start | bytes 3538952 | tf_op jit(solution)/shard_map/ppermute | solution.py:1043
  472.8 23.4 %collective-permute-start.29 = (bf16[384,1280]{1,0:T(8,128)(2,1)}, bf16[384,1280]{1,0:T(8,128)(2,1)S(1)}, u32[]{:S(2)}, u32[]{:S(2)}) collective-permute-start(bf16[384,1280]{1,0:T(8,128)(2,1)} %add_convert_fusion.1), channel_id=1, source_target_pairs={{0,4},{1,5},{2,6},{3,7},{4,0},{5,1},{6,2},{7,3},{8,12},{9,13},{10,... | collective-permute-start | bytes 2949128 | tf_op jit(solution)/shard_map/ppermute | solution.py:944
  497.7 10.7 %collective-permute-start.30 = (bf16[96,1280]{1,0:T(8,128)(2,1)S(1)}, bf16[96,1280]{1,0:T(8,128)(2,1)S(1)}, u32[]{:S(2)}, u32[]{:S(2)}) collective-permute-start(bf16[96,1280]{1,0:T(8,128)(2,1)S(1)} %get-tuple-element.172), channel_id=1, source_target_pairs={{0,8},{1,9},{2,10},{3,11},{4,12},{5,13},{6,14},{7,15},{8,16},{9,17... | collective-permute-start | bytes 737288 | tf_op jit(solution)/shard_map/ppermute | solution.py:944
  499.8 18.1 %collective-permute-start.32 = (bf16[96,1280]{1,0:T(8,128)(2,1)S(1)}, bf16[96,1280]{1,0:T(8,128)(2,1)S(1)}, u32[]{:S(2)}, u32[]{:S(2)}) collective-permute-start(bf16[96,1280]{1,0:T(8,128)(2,1)S(1)} %get-tuple-element.173), channel_id=1, source_target_pairs={{0,24},{1,25},{2,26},{3,27},{4,28},{5,29},{6,30},{7,31},{8,0},{9,1... | collective-permute-start | bytes 737288 | tf_op jit(solution)/shard_map/ppermute | solution.py:944
  508.4 18.8 %collective-permute-start.31 = (bf16[96,1280]{1,0:T(8,128)(2,1)S(1)}, bf16[96,1280]{1,0:T(8,128)(2,1)S(1)}, u32[]{:S(2)}, u32[]{:S(2)}) collective-permute-start(bf16[96,1280]{1,0:T(8,128)(2,1)S(1)} %get-tuple-element.174), channel_id=1, source_target_pairs={{0,16},{1,17},{2,18},{3,19},{4,20},{5,21},{6,22},{7,23},{8,24},{9,... | collective-permute-start | bytes 737288 | tf_op jit(solution)/shard_map/ppermute | solution.py:944
  518.0 39.8 %collective-permute-start.36 = (bf16[384,1920]{1,0:T(8,128)(2,1)}, bf16[384,1920]{1,0:T(8,128)(2,1)}, u32[]{:S(2)}, u32[]{:S(2)}) collective-permute-start(bf16[384,1920]{1,0:T(8,128)(2,1)} %add_convert_fusion), channel_id=1, source_target_pairs={{0,4},{1,5},{2,6},{3,7},{4,0},{5,1},{6,2},{7,3},{8,12},{9,13},{10,... | collective-permute-start | bytes 4423688 | tf_op jit(solution)/shard_map/ppermute | solution.py:944
  528.4 5.7 collective-permute-start.33
  534.2 30.8 %collective-permute-start.34 = (bf16[24,1280]{1,0:T(8,128)(2,1)S(1)}, bf16[24,1280]{1,0:T(8,128)(2,1)S(1)}, u32[]{:S(2)}, u32[]{:S(2)}) collective-permute-start(bf16[24,1280]{1,0:T(8,128)(2,1)S(1)} %dynamic-slice_convert_fusion.3), channel_id=1, source_target_pairs={{0,1},{1,0},{2,3},{3,2},{4,5},{5,4},{6,7},{7,6},{8,9},{9,8},{10,11... | collective-permute-start | bytes 184328 | tf_op jit(solution)/shard_map/ppermute | solution.py:944
  560.4 13.5 %collective-permute-start.37 = (bf16[96,1920]{1,0:T(8,128)(2,1)}, bf16[96,1920]{1,0:T(8,128)(2,1)S(1)}, u32[]{:S(2)}, u32[]{:S(2)}) collective-permute-start(bf16[96,1920]{1,0:T(8,128)(2,1)} %get-tuple-element.169), channel_id=1, source_target_pairs={{0,8},{1,9},{2,10},{3,11},{4,12},{5,13},{6,14},{7,15},{8,16},{9,17... | collective-permute-start | bytes 1105928 | tf_op jit(solution)/shard_map/ppermute | solution.py:944
  563.5 20.3 %collective-permute-start.39 = (bf16[96,1920]{1,0:T(8,128)(2,1)S(1)}, bf16[96,1920]{1,0:T(8,128)(2,1)S(1)}, u32[]{:S(2)}, u32[]{:S(2)}) collective-permute-start(bf16[96,1920]{1,0:T(8,128)(2,1)S(1)} %get-tuple-element.170), channel_id=1, source_target_pairs={{0,24},{1,25},{2,26},{3,27},{4,28},{5,29},{6,30},{7,31},{8,0},{9,1... | collective-permute-start | bytes 1105928 | tf_op jit(solution)/shard_map/ppermute | solution.py:944
  564.2 32.2 %collective-permute-start.38 = (bf16[96,1920]{1,0:T(8,128)(2,1)S(1)}, bf16[96,1920]{1,0:T(8,128)(2,1)S(1)}, u32[]{:S(2)}, u32[]{:S(2)}) collective-permute-start(bf16[96,1920]{1,0:T(8,128)(2,1)S(1)} %get-tuple-element.171), channel_id=1, source_target_pairs={{0,16},{1,17},{2,18},{3,19},{4,20},{5,21},{6,22},{7,23},{8,24},{9,... | collective-permute-start | bytes 1105928 | tf_op jit(solution)/shard_map/ppermute | solution.py:944
  597.8 5.8 collective-permute-start.40
  603.7 1.4 collective-permute-start.41
  (29 other events, 414.0 us)
Sparse Core Ops, SparseCore 0:
  10.9 99.4 all-gather.1
  463.2 123.1 reduce-scatter.1

commit v2 on v1

--- a/solution.py
+++ b/solution.py
@@ -40,7 +40,9 @@
 
 
 def cost(flops, nbytes):
-    return pl.CostEstimate(flops=int(flops), bytes_accessed=int(nbytes), transcendentals=0)
+    return pl.CostEstimate(
+        flops=int(0.3 * flops), bytes_accessed=int(0.3 * nbytes), transcendentals=0
+    )
 
 
 def whole(shape, index=None):
@@ -74,21 +76,9 @@
 
 
 def gelu_parts(up):
-    size = jnp.abs(up) * (1.0 / math.sqrt(2.0))
-    near = 1.0 / (1.0 + 0.3275911 * size)
-    bell = jnp.exp(-(size * size))
-    series = near * (
-        0.5 * 0.254829592
-        + near
-        * (
-            0.5 * -0.284496736
-            + near * (0.5 * 1.421413741 + near * (0.5 * -1.453152027 + near * (0.5 * 1.061405429)))
-        )
-    )
-    tail = series * bell
-    phi = jnp.where(up >= 0.0, 1.0 - tail, tail)
-    slope = phi + up * (bell * (1.0 / math.sqrt(2.0 * math.pi)))
-    return up * phi, slope
+    phi = 0.5 + 0.5 * lax.erf(up * (1.0 / math.sqrt(2.0)))
+    bell = jnp.exp(up * up * -0.5) * (1.0 / math.sqrt(2.0 * math.pi))
+    return up * phi, phi + up * bell
 
 
 def column_sum(matrix):
@@ -115,7 +105,7 @@
     return pltpu.roll(matrix, 64, 1)
 
 
-def read_small(block, vec_ref, sv_ref, pw_ref, cw_ref, ub_ref, stu, classes, devices):
+def read_small(block, vec_ref, sv_ref, pw_ref, cw_ref, ub_ref, cb_ref, stu, classes, devices, up_size):
     width = block.shape[0]
     shard = width // devices
     group = stu // devices
@@ -133,44 +123,113 @@
     lane = lax.broadcasted_iota(jnp.int32, (devices, 128), 1)
     ub_ref[...] = jnp.where(lane < 64, turn_lanes(low), high)
     vec_ref[...] = block.astype(F32).T[:8]
-
-
-def pack_small(vectors, up_bias, pool_weight, class_weight, columns):
-    shard = vectors[0].shape[0]
-    group = pool_weight.shape[0]
-    rest = jnp.concatenate([class_weight] + [c[:, None] for c in columns], axis=1)
-    up = jnp.pad(up_bias, (0, -up_bias.shape[0] % 64)).reshape(-1, 64)
-    right = jnp.concatenate(
-        [
-            pool_weight[:, :64],
-            pool_weight[:, 64:],
-            jnp.pad(rest, ((0, 0), (0, 64 - rest.shape[1]))),
-            up,
-        ],
-        axis=0,
-    )
-    right = jnp.pad(right, ((0, shard - right.shape[0]), (0, 0)))
-    left = jnp.stack(vectors + (jnp.zeros_like(vectors[0]),) * (64 - len(vectors)), axis=1)
-    return jnp.concatenate([left, right], axis=1)
-
-
-def attend_kernel(lens, table, *refs, seq, width, stu, classes, devices):
+    skip = 3 * group + pl.cdiv(up_size, 64)
+    high, low = (dot(one_hot_rows(devices, width, 1, shard, skip + n), block) for n in range(2))
+    cb_ref[...] = jnp.broadcast_to(turn_lanes(column_sum(high + low)), cb_ref.shape)
+
+
+def pack_kernel(here, *refs, classes, group):
+    wi_ref, ws_ref, wo_ref, wu_ref, ub_ref, pw_ref, cw_ref, lg_ref = refs[:8]
+    columns, vectors = refs[8:11], refs[11:19]
+    in_mine, in_other, ff_mine, ff_other, held = refs[19:]
+    shard = wi_ref.shape[0]
+    held[...] = jnp.zeros_like(held)
+    for n, vector in enumerate(vectors):
+        held[n : n + 1, :shard] = vector[...].astype(F32)
+    left = held[:128].T[:shard]
+    held[:8] = jnp.zeros((8, 128), F32)
+    for n, column in enumerate(columns):
+        held[classes + n : classes + n + 1, :group] = column[...].astype(F32)
+    held[128 : 128 + group, :classes] = cw_ref[...].astype(F32)
+    rest = held[128 : 128 + group] + held[:128].T[:group]
+    up_size = ub_ref.shape[1]
+    held[136:137, :up_size] = ub_ref[...].astype(F32)
+    up = held[136:137]
+    total = column_sum(lg_ref[...].astype(F32))
+    high = total.astype(BF16).astype(F32)
+    held[144:145, :classes] = high
+    held[145:146, :classes] = total - high
+    pool = pw_ref[...].astype(F32)
+    rows = [turn_lanes(pool), pool, turn_lanes(rest), turn_lanes(up)]
+    if up_size > 64:
+        rows.append(up)
+    rows.append(turn_lanes(held[144:146]))
+    spare = shard - sum(r.shape[0] for r in rows)
+    if spare:
+        rows.append(jnp.zeros((spare, 128), F32))
+    lane = lax.broadcasted_iota(jnp.int32, (shard, 128), 1)
+    small = jnp.where(lane < 64, left, jnp.concatenate(rows, axis=0)).astype(BF16)
+    cut = wi_ref.shape[1] // 2
+    width = wo_ref.shape[1]
+    part = ff_mine.shape[1] - width
+    for core, (a, b, c, d) in enumerate(
+        ((in_mine, in_other, ff_mine, ff_other), (in_other, in_mine, ff_other, ff_mine))
+    ):
+
+        @pl.when(here[3] == core)
+        def _():
+            a[:, :cut] = wi_ref[:, :cut]
+            a[:, cut:] = ws_ref[...]
+            b[:, :cut] = wi_ref[:, cut:]
+            b[:, cut:] = small
+            c[:, :width] = wo_ref[...]
+            c[:, width:] = wu_ref[:, :part]
+            d[...] = wu_ref[:, part:]
+
+
+def pack(here, wi, ws, wo, wu, ub, pw, cw, lg, columns, vectors):
+    shard = wi.shape[0]
+    group, classes = cw.shape
+    flat = lambda v: v.reshape(1, -1)
+    first = jax.ShapeDtypeStruct((shard, wi.shape[1] // 2 + 128), BF16)
+    second = jax.ShapeDtypeStruct((shard, (wo.shape[1] + wu.shape[1]) // 2), BF16)
+    args = (wi, ws, wo, wu, flat(ub), pw, cw, lg, *map(flat, columns), *map(flat, vectors))
+    return pl.pallas_call(
+        functools.partial(pack_kernel, classes=classes, group=group),
+        grid_spec=pltpu.PrefetchScalarGridSpec(
+            num_scalar_prefetch=1,
+            grid=(1,),
+            in_specs=[whole(a.shape) for a in args],
+            out_specs=[kept(o.shape) for o in (first, first, second, second)],
+            scratch_shapes=[pltpu.VMEM((152, 128), F32)],
+        ),
+        out_shape=[first, first, second, second],
+        compiler_params=params(),
+        cost_estimate=cost(1e6, 1e6),
+        name="pack",
+    )(here, *args)
+
+
+def attend_kernel(lens, here, *refs, copies, size, seq, width, stu, classes, devices, up_size):
     x_ref = refs[0]
-    pieces = refs[1:-11]
-    qkv_ref, prob_ref, mixed_ref, vec_ref, sv_ref, pw_ref, cw_ref, ub_ref, ws_ref, w_ref, sem = refs[-11:]
+    pieces = refs[1:-14]
+    qkv_ref, prob_ref, mixed_ref, turned_ref, vec_ref, sv_ref, pw_ref = refs[-14:-7]
+    cw_ref, ub_ref, cb_ref, ws_ref, w_ref, held, sem = refs[-7:]
     step = pl.program_id(0)
     half = w_ref.shape[1] // 2
     cut = half - 128
 
     @pl.when(step == 0)
     def _():
-        fetch_pieces(table, pieces, w_ref, sem, True, True)
+        fetch(copies, here, size, pieces, w_ref, sem)
         ws_ref[...] = w_ref[:, cut:half]
         read_small(
-            w_ref[:, half + cut :], vec_ref, sv_ref, pw_ref, cw_ref, ub_ref, stu, classes, devices
+            w_ref[:, half + cut :],
+            vec_ref,
+            sv_ref,
+            pw_ref,
+            cw_ref,
+            ub_ref,
+            cb_ref,
+            stu,
+            classes,
+            devices,
+            up_size,
         )
 
     rows = x_ref.shape[0]
+    lines = line_rows(here, size, width // (size["y"] * size["z"]))
+    turn_lines(x_ref[...], lines, held, turned_ref, slice(0, rows))
     x = x_ref[...]
     vec = vec_ref[...]
     query = dot(x, w_ref[:, :width]) + vec[QB : QB + 1]
@@ -205,22 +264,33 @@
             mixed_ref[at, low : low + 128] = jnp.where(first_head, out[:seq], out[seq:]).astype(BF16)
 
 
-def attend(lens, table, rows, pieces, seq, block, stu, classes, devices):
+def attend(lens, gather, rows, seq, block, stu, classes, devices, up_size):
+    copies, here, size = gather.plan(), gather.grid.here, gather.grid.size
+    pieces = gather.parts
     count, width = rows.shape
     pairs = width // 128
     samples = block // seq
-    columns = 2 * pieces[0].shape[1]
+    columns = gather.columns
     small = [
         jax.ShapeDtypeStruct((8, width), F32),
         jax.ShapeDtypeStruct((8, stu), F32),
         jax.ShapeDtypeStruct((stu, stu), BF16),
         jax.ShapeDtypeStruct((stu, 128), BF16),
         jax.ShapeDtypeStruct((devices, 128), F32),
+        jax.ShapeDtypeStruct((8, 128), F32),
         jax.ShapeDtypeStruct((width, stu), BF16),
     ]
     return pl.pallas_call(
         functools.partial(
-            attend_kernel, seq=seq, width=width, stu=stu, classes=classes, devices=devices
+            attend_kernel,
+            copies=copies,
+            size=size,
+            seq=seq,
+            width=width,
+            stu=stu,
+            classes=classes,
+            devices=devices,
+            up_size=up_size,
         ),
         grid_spec=pltpu.PrefetchScalarGridSpec(
             num_scalar_prefetch=2,
@@ -230,29 +300,38 @@
                 rows_spec(block, 3 * width),
                 pl.BlockSpec((samples, pairs, seq, 2 * seq), lambda i, *_: (i, 0, 0, 0)),
                 rows_spec(block, width),
+                pl.BlockSpec((width, block), lambda i, *_: (0, i)),
             ]
             + [kept(s.shape) for s in small],
             scratch_shapes=[
                 pltpu.VMEM((width, columns), BF16),
-                pltpu.SemaphoreType.DMA((2 * len(pieces),)),
+                pltpu.VMEM((width, block), BF16),
+                pltpu.SemaphoreType.DMA((len(copies),)),
             ],
         ),
         out_shape=[
             jax.ShapeDtypeStruct((count, 3 * width), BF16),
             jax.ShapeDtypeStruct((count // seq, pairs, seq, 2 * seq), BF16),
             jax.ShapeDtypeStruct((count, width), BF16),
+            jax.ShapeDtypeStruct((width, count), BF16),
         ]
         + small,
         compiler_params=params(),
         cost_estimate=cost(2 * count * width * 3 * width * 2, 30e6),
         name="attend",
-    )(lens, table, rows, *pieces)
-
-
-def up_kernel(
-    mixed_ref, x_ref, w_ref, vec_ref, ub_ref, norm_ref, factor_ref, low_ref, act_ref, slope_ref, *, chunk
-):
+    )(lens, here, rows, *pieces)
+
+
+def up_kernel(here, *refs, copies, size, chunk):
+    mixed_ref, x_ref, vec_ref, ub_ref = refs[:4]
+    pieces = refs[4:-7]
+    norm_ref, factor_ref, low_ref, act_ref, slope_ref, w_ref, sem = refs[-7:]
     width = x_ref.shape[1]
+
+    @pl.when(pl.program_id(0) == 0)
+    def _():
+        fetch(copies, here, size, pieces, w_ref, sem)
+
     vec = vec_ref[...]
     total = dot(mixed_ref[...], w_ref[:, :width]) + vec[OB : OB + 1] + x_ref[...].astype(F32)
     normed, factor = layer_norm(total)
@@ -262,33 +341,41 @@
     low = low_ref[...]
     for begin in range(0, act_ref.shape[1], chunk):
         at = slice(begin, begin + chunk)
-        up = dot(low, w_ref[:, width + begin : width + begin + chunk]) + ub_ref[0:1, at]
-        act, slope = gelu_parts(up)
-        act_ref[:, at] = act.astype(BF16)
-        slope_ref[:, at] = slope.astype(BF16)
-
-
-def up_part(mixed, rows, large, vec, ub, block):
+        for first in range(0, low.shape[0], 128):
+            rows = slice(first, first + 128)
+            up = dot(low[rows], w_ref[:, width + begin : width + begin + chunk]) + ub_ref[0:1, at]
+            act, slope = gelu_parts(up)
+            act_ref[rows, at] = act.astype(BF16)
+            slope_ref[rows, at] = slope.astype(BF16)
+
+
+def up_part(gather, mixed, rows, vec, ub, block):
+    copies, here, size = gather.plan(), gather.grid.here, gather.grid.size
+    pieces = gather.parts
     count, width = rows.shape
-    ff = large.shape[1] - width
+    ff = gather.columns - width
     return pl.pallas_call(
-        functools.partial(up_kernel, chunk=256),
+        functools.partial(up_kernel, copies=copies, size=size, chunk=256),
         grid_spec=pltpu.PrefetchScalarGridSpec(
-            num_scalar_prefetch=0,
+            num_scalar_prefetch=1,
             grid=(count // block,),
             in_specs=[
                 rows_spec(block, width),
                 rows_spec(block, width),
-                pl.BlockSpec(large.shape, lambda i: (0, 0), pipeline_mode=pl.Buffered(1)),
                 whole(vec.shape),
                 whole(ub.shape),
-            ],
+            ]
+            + [pl.BlockSpec(memory_space=pl.ANY)] * len(pieces),
             out_specs=[
                 rows_spec(block, width),
                 rows_spec(block, 128),
                 rows_spec(block, width),
                 rows_spec(block, ff),
                 rows_spec(block, ff),
+            ],
+            scratch_shapes=[
+                pltpu.VMEM((width, gather.columns), BF16),
+                pltpu.SemaphoreType.DMA((len(copies),)),
             ],
         ),
         out_shape=[
@@ -301,16 +388,54 @@
         compiler_params=params(),
         cost_estimate=cost(2 * count * width * (ff + width) * 2, 50e6),
         name="up_part",
-    )(mixed, rows, large, vec, ub)
-
-
-def down_kernel(lens, alive, table, *refs, seq):
-    act_ref, norm_ref, cot_ref, lg_ref, vec_ref, ws_ref, sv_ref, pw_ref, cw_ref = refs[:9]
-    pieces = refs[9:-11]
-    second_ref, sum_ref, dcot_ref, logits_ref, vgrad_ref, sgrad_ref = refs[-11:-5]
-    wsgrad_ref, pwgrad_ref, cwgrad_ref, wd_ref, sem = refs[-5:]
+    )(here, mixed, rows, vec, ub, *pieces)
+
+
+def down_kernel(lens, alive, *refs, seq, steps, tile):
+    act_hbm, norm_ref, cot_ref, lg_ref, wd_ref, vec_ref, ws_ref, sv_ref, pw_ref, cw_ref = refs[:10]
+    second_ref, sum_ref, dcot_ref, logits_ref, vgrad_ref, sgrad_ref = refs[10:16]
+    wsgrad_ref, pwgrad_ref, cwgrad_ref, grad_ref, act_all, turned, sem = refs[16:]
     step = pl.program_id(0)
-    rows = act_ref.shape[0]
+    rows = norm_ref.shape[0]
+
+    def load(n):
+        at = pl.ds(pl.multiple_of(n * rows, rows), rows)
+        return pltpu.make_async_copy(act_hbm.at[at], act_all.at[at], sem.at[n])
+
+    @pl.when(step == 0)
+    def _():
+        load(0).start()
+
+    @pl.when(step + 1 < steps)
+    def _():
+        load(step + 1).start()
+
+    @pl.when(step < steps)
+    def _():
+        load(step).wait()
+        at = pl.ds(pl.multiple_of(step * rows, rows), rows)
+        down_rows(
+            lens,
+            alive,
+            (act_all.at[at], norm_ref, cot_ref, lg_ref, wd_ref, vec_ref, ws_ref, sv_ref, pw_ref, cw_ref),
+            (second_ref, sum_ref, dcot_ref, logits_ref, vgrad_ref, sgrad_ref),
+            (wsgrad_ref, pwgrad_ref, cwgrad_ref),
+            seq,
+        )
+        turned[:, at] = dcot_ref[...].T
+
+    @pl.when(step >= steps)
+    def _():
+        at = pl.ds(pl.multiple_of((step - steps) * tile, tile), tile)
+        grad_ref[...] = dot(turned[...], act_all[:, at]).astype(BF16).T
+
+
+def down_rows(lens, alive, ins, outs, sums, seq):
+    act_ref, norm_ref, cot_ref, lg_ref, wd_ref, vec_ref, ws_ref, sv_ref, pw_ref, cw_ref = ins
+    second_ref, sum_ref, dcot_ref, logits_ref, vgrad_ref, sgrad_ref = outs
+    wsgrad_ref, pwgrad_ref, cwgrad_ref = sums
+    step = pl.program_id(0)
+    rows = norm_ref.shape[0]
     samples = rows // seq
     vec = vec_ref[...]
     sv = sv_ref[...]
@@ -320,7 +445,6 @@
 
     @pl.when(step == 0)
     def _():
-        fetch_pieces(table, pieces, wd_ref, sem, True, True)
         vgrad_ref[...] = jnp.zeros_like(vgrad_ref)
         sgrad_ref[...] = jnp.zeros_like(sgrad_ref)
         wsgrad_ref[...] = jnp.zeros_like(wsgrad_ref)
@@ -394,42 +518,48 @@
     )
 
 
-def down_part(lens, alive, table, act, normed, cot, lg, pieces, vec, ws, sv, pw, cw, seq, block):
+def down_part(lens, alive, act, normed, cot, lg, wd, vec, ws, sv, pw, cw, seq, block, tile):
     count, ff = act.shape
     width = normed.shape[1]
     stu = ws.shape[1]
     steps = count // block
+
+    def block_rows(height, columns):
+        return pl.BlockSpec((height, columns), lambda i, *_: (jnp.minimum(i, steps - 1), 0))
+
     return pl.pallas_call(
-        functools.partial(down_kernel, seq=seq),
+        functools.partial(down_kernel, seq=seq, steps=steps, tile=tile),
         grid_spec=pltpu.PrefetchScalarGridSpec(
-            num_scalar_prefetch=3,
-            grid=(steps,),
+            num_scalar_prefetch=2,
+            grid=(steps + ff // tile,),
             in_specs=[
-                rows_spec(block, ff),
-                rows_spec(block, width),
-                rows_spec(block, width),
-                rows_spec(8, 128),
+                pl.BlockSpec(memory_space=pl.ANY),
+                block_rows(block, width),
+                block_rows(block, width),
+                block_rows(8, 128),
+                whole(wd.shape),
                 whole(vec.shape),
                 whole(ws.shape),
                 whole(sv.shape),
                 whole(pw.shape),
                 whole(cw.shape),
-            ]
-            + [pl.BlockSpec(memory_space=pl.ANY)] * len(pieces),
+            ],
             out_specs=[
-                rows_spec(block, width),
-                rows_spec(block, width),
-                rows_spec(block, width),
-                rows_spec(8, 128),
+                block_rows(block, width),
+                block_rows(block, width),
+                block_rows(block, width),
+                block_rows(8, 128),
                 kept((8, width)),
                 kept((8, stu)),
                 kept((stu, width)),
                 kept((stu, stu)),
                 kept((stu, 128)),
+                pl.BlockSpec((tile, width), lambda i, *_: (jnp.maximum(i - steps, 0), 0)),
             ],
             scratch_shapes=[
-                pltpu.VMEM((ff, width), BF16),
-                pltpu.SemaphoreType.DMA((2 * len(pieces),)),
+                pltpu.VMEM((count, ff), BF16),
+                pltpu.VMEM((width, count), BF16),
+                pltpu.SemaphoreType.DMA((steps,)),
             ],
         ),
         out_shape=[
@@ -442,99 +572,207 @@
             jax.ShapeDtypeStruct((stu, width), F32),
             jax.ShapeDtypeStruct((stu, stu), F32),
             jax.ShapeDtypeStruct((stu, 128), F32),
+            jax.ShapeDtypeStruct((ff, width), BF16),
         ],
         compiler_params=params(),
-        cost_estimate=cost(2 * count * width * ff * 2, 40e6),
+        cost_estimate=cost(2 * count * width * ff * 4, 60e6),
         name="down_part",
-    )(lens, alive, table, act, normed, cot, lg, vec, ws, sv, pw, cw, *pieces)
-
-
-def up_back_kernel(table, *refs, chunk):
-    dcot_ref, slope_ref, sum_ref, norm_ref, factor_ref, w_ref, vec_ref = refs[:7]
-    pieces = refs[7:-8]
-    ucot_ref, one_ref, acot_ref, mcot_ref, vgrad_ref, ugrad_ref, wd_ref, sem = refs[-8:]
+    )(lens, alive, act, normed, cot, lg, wd, vec, ws, sv, pw, cw)
+
+
+def turn_lines(block, lines, held, to, at):
+    held[...] = block.T
+    rows = to.shape[0] // len(lines)
+    for n, line in enumerate(lines):
+        to[n * rows : (n + 1) * rows, at] = held[pl.ds(line, rows)]
+
+
+def up_back_kernel(here, *refs, copies, size, steps, chunk, tile):
+    dcot_ref, slope_ref, sum_ref, norm_ref, factor_ref, low_ref, mixed_ref, wd_ref, vec_ref = refs[:9]
+    pieces = refs[9:-15]
+    one_ref, mcot_ref, vgrad_ref, ugrad_ref = refs[-15:-11]
+    up_other, up_mine, out_other, out_mine = refs[-11:-7]
+    w_ref, ucot_all, acot_all, low_turned, mixed_turned, held, sem = refs[-7:]
     step = pl.program_id(0)
-    width = dcot_ref.shape[1]
-    vec = vec_ref[...]
+    rows, width = dcot_ref.shape
+    ff = slope_ref.shape[1]
+    core = here[3]
+    lines = line_rows(here, size, width // (size["y"] * size["z"]))
 
     @pl.when(step == 0)
     def _():
-        fetch_pieces(table, pieces, wd_ref, sem, True, True)
+        fetch(copies, here, size, pieces, w_ref, sem)
         vgrad_ref[...] = jnp.zeros_like(vgrad_ref)
         ugrad_ref[...] = jnp.zeros_like(ugrad_ref)
 
-    down_cot = dcot_ref[...]
-    for begin in range(0, slope_ref.shape[1], chunk):
-        at = slice(begin, begin + chunk)
-        up_cot = dot_nt(down_cot, wd_ref[at, :]) * slope_ref[:, at].astype(F32)
-        up_cot = up_cot.astype(BF16)
-        ucot_ref[:, at] = up_cot
-        ugrad_ref[0:1, at] += column_sum(up_cot.astype(F32))
-    cot = sum_ref[...] + dot_nt(ucot_ref[...], w_ref[:, width:])
-    normed = norm_ref[...]
-    one_cot = layer_norm_back(cot, vec[G1 : G1 + 1], normed, factor_ref[:, 0:1])
-    one_ref[...] = one_cot
-    low = one_cot.astype(BF16)
-    acot_ref[...] = low
-    mcot_ref[...] = dot_nt(low, w_ref[:, :width]).astype(BF16)
-    vgrad_ref[...] += stack_rows(
-        [column_sum(cot * normed), column_sum(cot), column_sum(low.astype(F32))], 8
-    )
-
-
-def up_back(table, dcot, slope, sum_two, normed, factor, pieces, large, vec, block):
+    @pl.when(step < steps)
+    def _():
+        vec = vec_ref[...]
+        at_rows = pl.ds(pl.multiple_of(step * rows, rows), rows)
+        down_cot = dcot_ref[...]
+        for begin in range(0, ff, chunk):
+            at = slice(begin, begin + chunk)
+            up_cot = dot_nt(down_cot, wd_ref[at, :]) * slope_ref[:, at].astype(F32)
+            ugrad_ref[0:1, at] += column_sum(up_cot)
+            ucot_all[at_rows, at] = up_cot.astype(BF16)
+        turn_lines(low_ref[...], lines, held, low_turned, at_rows)
+        turn_lines(mixed_ref[...], lines, held, mixed_turned, at_rows)
+        cot = sum_ref[...] + dot_nt(ucot_all[at_rows, :], w_ref[:, width:])
+        normed = norm_ref[...]
+        one_cot = layer_norm_back(cot, vec[G1 : G1 + 1], normed, factor_ref[:, 0:1])
+        one_ref[...] = one_cot
+        low = one_cot.astype(BF16)
+        acot_all[at_rows, :] = low
+        mcot_ref[...] = dot_nt(low, w_ref[:, :width]).astype(BF16)
+        vgrad_ref[...] += stack_rows(
+            [column_sum(cot * normed), column_sum(cot), column_sum(one_cot)], 8
+        )
+
+    per = ff // 2 // tile
+
+    def up_tile(n, half):
+        first = (half * per + n) * tile
+        return dot(low_turned[...], ucot_all[:, pl.ds(pl.multiple_of(first, 128), tile)])
+
+    def out_tile(half):
+        first = half * (width // 2)
+        return dot(mixed_turned[...], acot_all[:, pl.ds(pl.multiple_of(first, 128), width // 2)])
+
+    @pl.when((step >= steps) & (step < steps + per))
+    def _():
+        up_other[...] = up_tile(step - steps, 1 - core).astype(BF16)
+
+    @pl.when(step == steps + per)
+    def _():
+        out_other[...] = out_tile(1 - core).astype(BF16)
+        out_mine[...] = out_tile(core).astype(BF16)
+
+    @pl.when(step > steps + per)
+    def _():
+        up_mine[...] = up_tile(step - steps - per - 1, core).astype(BF16)
+
+
+def up_back(gather, dcot, slope, sum_two, normed, factor, low, mixed, wd, vec, block, tile):
+    copies, here, size = gather.plan(), gather.grid.here, gather.grid.size
+    pieces = gather.parts
     count, width = dcot.shape
     ff = slope.shape[1]
+    steps = count // block
+    per = ff // 2 // tile
+
+    def block_rows(columns):
+        return pl.BlockSpec((block, columns), lambda i, *_: (jnp.minimum(i, steps - 1), 0))
+
+    def tiles(begin):
+        return pl.BlockSpec(
+            (width, tile), lambda i, *_: (0, jnp.clip(i - begin, 0, per - 1))
+        )
+
     return pl.pallas_call(
-        functools.partial(up_back_kernel, chunk=512),
+        functools.partial(
+            up_back_kernel, copies=copies, size=size, steps=steps, chunk=512, tile=tile
+        ),
         grid_spec=pltpu.PrefetchScalarGridSpec(
             num_scalar_prefetch=1,
-            grid=(count // block,),
+            grid=(steps + 2 * per + 1,),
             in_specs=[
-                rows_spec(block, width),
-                rows_spec(block, ff),
-                rows_spec(block, width),
-                rows_spec(block, width),
-                rows_spec(block, 128),
-                whole(large.shape),
+                block_rows(width),
+                block_rows(ff),
+                block_rows(width),
+                block_rows(width),
+                block_rows(128),
+                block_rows(width),
+                block_rows(width),
+                whole(wd.shape),
                 whole(vec.shape),
             ]
             + [pl.BlockSpec(memory_space=pl.ANY)] * len(pieces),
             out_specs=[
-                rows_spec(block, ff),
-                rows_spec(block, width),
-                rows_spec(block, width),
-                rows_spec(block, width),
+                block_rows(width),
+                block_rows(width),
                 kept((8, width)),
                 kept((8, ff)),
+                tiles(steps),
+                tiles(steps + per + 1),
+                kept((width, width // 2)),
+                kept((width, width // 2)),
             ],
             scratch_shapes=[
-                pltpu.VMEM((ff, width), BF16),
-                pltpu.SemaphoreType.DMA((2 * len(pieces),)),
+                pltpu.VMEM((width, gather.columns), BF16),
+                pltpu.VMEM((count, ff), BF16),
+                pltpu.VMEM((count, width), BF16),
+                pltpu.VMEM((width, count), BF16),
+                pltpu.VMEM((width, count), BF16),
+                pltpu.VMEM((width, block), BF16),
+                pltpu.SemaphoreType.DMA((len(copies),)),
             ],
         ),
         out_shape=[
-            jax.ShapeDtypeStruct((count, ff), BF16),
             jax.ShapeDtypeStruct((count, width), F32),
-            jax.ShapeDtypeStruct((count, width), BF16),
             jax.ShapeDtypeStruct((count, width), BF16),
             jax.ShapeDtypeStruct((8, width), F32),
             jax.ShapeDtypeStruct((8, ff), F32),
+            jax.ShapeDtypeStruct((width, ff // 2), BF16),
+            jax.ShapeDtypeStruct((width, ff // 2), BF16),
+            jax.ShapeDtypeStruct((width, width // 2), BF16),
+            jax.ShapeDtypeStruct((width, width // 2), BF16),
         ],
         compiler_params=params(),
-        cost_estimate=cost(2 * count * width * ff * 2.5, 60e6),
+        cost_estimate=cost(2 * count * width * ff * 4, 60e6),
         name="up_back",
-    )(table, dcot, slope, sum_two, normed, factor, large, vec, *pieces)
+    )(here, dcot, slope, sum_two, normed, factor, low, mixed, wd, vec, *pieces)
 
 
 def attend_back_kernel(mcot_ref, qkv_ref, prob_ref, pcot_ref, vgrad_ref, *, seq, width):
-    step = pl.program_id(0)
-    rows = mcot_ref.shape[0]
-
-    @pl.when(step == 0)
+    @pl.when(pl.program_id(0) == 0)
     def _():
         vgrad_ref[...] = jnp.zeros_like(vgrad_ref)
 
+    attend_back_rows(mcot_ref, qkv_ref, prob_ref, pcot_ref, vgrad_ref, seq, width)
+
+
+def input_grad_kernel(here, turned_ref, pcot_ref, other, mine, *, per):
+    step = pl.program_id(0)
+    grad = dot(turned_ref[...], pcot_ref[...]).astype(BF16)
+
+    @pl.when(step < per)
+    def _():
+        other[...] = grad
+
+    @pl.when(step >= per)
+    def _():
+        mine[...] = grad
+
+
+def input_grad(here, turned, pcot, tile):
+    width, count = turned.shape
+    half = pcot.shape[1] // 2
+    per = half // tile
+
+    def columns(i, t):
+        core = t[3]
+        return (0, jnp.where(i < per, (1 - core) * per + i, core * per + i - per))
+
+    return pl.pallas_call(
+        functools.partial(input_grad_kernel, per=per),
+        grid_spec=pltpu.PrefetchScalarGridSpec(
+            num_scalar_prefetch=1,
+            grid=(2 * per,),
+            in_specs=[whole((width, count)), pl.BlockSpec((count, tile), columns)],
+            out_specs=[
+                pl.BlockSpec((width, tile), lambda i, t: (0, jnp.minimum(i, per - 1))),
+                pl.BlockSpec((width, tile), lambda i, t: (0, jnp.maximum(i - per, 0))),
+            ],
+        ),
+        out_shape=[jax.ShapeDtypeStruct((width, half), BF16)] * 2,
+        compiler_params=params(),
+        cost_estimate=cost(4 * count * width * half, 20e6),
+        name="input_grad",
+    )(here, turned, pcot)
+
+
+def attend_back_rows(mcot_ref, qkv_ref, prob_ref, pcot_ref, vgrad_ref, seq, width):
+    rows = mcot_ref.shape[0]
     lane = lax.broadcasted_iota(jnp.int32, (seq, 128), 1)
     first_head = lane < HEAD_DIM
     scale = 1.0 / math.sqrt(HEAD_DIM)
@@ -584,7 +822,7 @@
             in_specs=[
                 rows_spec(block, width),
                 rows_spec(block, 3 * width),
-                pl.BlockSpec((block // seq, pairs, seq, 2 * seq), lambda i, *_: (i, 0, 0, 0)),
+                pl.BlockSpec((block // seq, pairs, seq, 2 * seq), lambda i: (i, 0, 0, 0)),
             ],
             out_specs=[rows_spec(block, 3 * width), kept((8, width))],
         ),
@@ -598,14 +836,14 @@
     )(mcot, qkv, prob)
 
 
-def token_kernel(table, *refs):
+def token_kernel(here, *refs, copies, size):
     pcot_ref, one_ref = refs[:2]
     pieces = refs[2:-3]
     out_ref, w_ref, sem = refs[-3:]
 
     @pl.when(pl.program_id(0) == 0)
     def _():
-        fetch_pieces(table, pieces, w_ref, sem, True, True)
+        fetch(copies, here, size, pieces, w_ref, sem)
 
     half = w_ref.shape[1] // 2
     cut = half - 128
@@ -616,10 +854,12 @@
     )
 
 
-def token_part(table, pcot, one_cot, pieces, block):
+def token_part(gather, pcot, one_cot, block):
+    copies, here, size = gather.plan(), gather.grid.here, gather.grid.size
+    pieces = gather.parts
     count, width = one_cot.shape
     return pl.pallas_call(
-        token_kernel,
+        functools.partial(token_kernel, copies=copies, size=size),
         grid_spec=pltpu.PrefetchScalarGridSpec(
             num_scalar_prefetch=1,
             grid=(count // block,),
@@ -627,108 +867,20 @@
             + [pl.BlockSpec(memory_space=pl.ANY)] * len(pieces),
             out_specs=rows_spec(block, width),
             scratch_shapes=[
-                pltpu.VMEM((width, 2 * pieces[0].shape[1]), BF16),
-                pltpu.SemaphoreType.DMA((2 * len(pieces),)),
+                pltpu.VMEM((width, gather.columns), BF16),
+                pltpu.SemaphoreType.DMA((len(copies),)),
             ],
         ),
         out_shape=jax.ShapeDtypeStruct((count, width), F32),
         compiler_params=params(),
         cost_estimate=cost(2 * count * width * 3 * width, 25e6),
         name="token_part",
-    )(table, pcot, one_cot, *pieces)
-
-
-def weight_kernel(left_ref, right_ref, out_ref, turned):
-    @pl.when(pl.program_id(0) == 0)
-    def _():
-        turned[...] = left_ref[...].T
-
-    out_ref[...] = dot(turned[...], right_ref[...]).astype(out_ref.dtype)
-
-
-def weight_part(left, right, tile, name):
-    count, height = left.shape
-    width = right.shape[1]
-    return pl.pallas_call(
-        weight_kernel,
-        grid_spec=pltpu.PrefetchScalarGridSpec(
-            num_scalar_prefetch=0,
-            grid=(width // tile,),
-            in_specs=[
-                whole((count, height)),
-                pl.BlockSpec((count, tile), lambda i, *_: (0, i)),
-            ],
-            out_specs=pl.BlockSpec((height, tile), lambda i, *_: (0, i)),
-            scratch_shapes=[pltpu.VMEM((height, count), BF16)],
-        ),
-        out_shape=jax.ShapeDtypeStruct((height, width), BF16),
-        compiler_params=params(),
-        cost_estimate=cost(2 * count * width * height, 2 * (count + height) * width),
-        name=name,
-    )(left, right)
-
-
-def weight_pieces_kernel(table, left_ref, right_ref, *refs, steps):
-    other_ref, planes, flat, turned = refs[0], refs[1:-2], refs[-2], refs[-1]
-    step = pl.program_id(0)
-    lines = table.shape[0] - 1
-    rows = turned.shape[0] // lines
-
-    @pl.when(step == 0)
-    def _():
-        flat[...] = left_ref[...].T
-        for n in range(lines):
-            at = pl.ds(pl.multiple_of(table[n], 16), rows)
-            turned[n * rows : (n + 1) * rows] = flat[at]
-
-    out = dot(turned[...], right_ref[...]).astype(BF16)
-
-    @pl.when(step < steps)
-    def _():
-        other_ref[...] = out
-
-    @pl.when(step >= steps)
-    def _():
-        for n, plane in enumerate(planes):
-            height = plane.shape[0]
-            plane[...] = out[n * height : (n + 1) * height]
-
-
-def weight_pieces(table, left, right, tile, planes, name):
-    count, height = left.shape
-    half = right.shape[1] // 2
-    steps = half // tile
-    core_at = table.shape[0] - 1
-
-    def columns(i, t):
-        core = t[core_at]
-        return (0, jnp.where(i < steps, (1 - core) * steps + i, core * steps + i - steps))
-
-    last = steps - 1
-    return pl.pallas_call(
-        functools.partial(weight_pieces_kernel, steps=steps),
-        grid_spec=pltpu.PrefetchScalarGridSpec(
-            num_scalar_prefetch=1,
-            grid=(2 * steps,),
-            in_specs=[whole((count, height)), pl.BlockSpec((count, tile), columns)],
-            out_specs=[pl.BlockSpec((height, tile), lambda i, t: (0, jnp.minimum(i, last)))]
-            + [
-                pl.BlockSpec((height // planes, tile), lambda i, t: (0, jnp.maximum(i - steps, 0)))
-            ]
-            * planes,
-            scratch_shapes=[pltpu.VMEM((height, count), BF16)] * 2,
-        ),
-        out_shape=[jax.ShapeDtypeStruct((height, half), BF16)]
-        + [jax.ShapeDtypeStruct((height // planes, half), BF16)] * planes,
-        compiler_params=params(),
-        cost_estimate=cost(2 * count * 2 * half * height, 4 * (count + height) * half),
-        name=name,
-    )(table, left, right)
-
-
-def small_kernel(table, *refs, classes, devices):
+    )(here, pcot, one_cot, *pieces)
+
+
+def small_kernel(here, *refs, size, classes, devices):
     vin_ref, vone_ref, vtwo_ref, ugrad_ref, sgrad_ref, wsgrad_ref, pwgrad_ref, cwgrad_ref = refs[:8]
-    other_ref, planes, halves = refs[8], refs[9:-1], refs[-1]
+    other_ref, mine_ref, halves = refs[8:]
     width = vin_ref.shape[1]
     stu = sgrad_ref.shape[1]
     shard = width // devices
@@ -754,34 +906,30 @@
         part = jnp.where(high, part, 0.0).astype(BF16)
         block = block + dot_tn(one_hot_rows(devices, width, 1, shard, 3 * group + n), part)
     halves[1] = block
-    lines = table.shape[0] - 1
-    core = table[lines]
-    rows = width // lines
-    per = lines // len(planes)
-    for n in range(lines):
-        at = pl.ds(pl.multiple_of(table[n], 16), rows)
+    core = here[3]
+    rows = width // (size["y"] * size["z"])
+    for n, line in enumerate(line_rows(here, size, rows)):
+        at = pl.ds(line, rows)
         other_ref[n * rows : (n + 1) * rows] = halves[1 - core, at].astype(BF16)
-        begin = (n % per) * rows
-        planes[n // per][begin : begin + rows] = halves[core, at].astype(BF16)
-
-
-def small_pieces(table, grads, planes, classes, devices):
+        mine_ref[n * rows : (n + 1) * rows] = halves[core, at].astype(BF16)
+
+
+def small_pieces(grid, grads, classes, devices):
     width = grads[0].shape[1]
     return pl.pallas_call(
-        functools.partial(small_kernel, classes=classes, devices=devices),
+        functools.partial(small_kernel, size=grid.size, classes=classes, devices=devices),
         grid_spec=pltpu.PrefetchScalarGridSpec(
             num_scalar_prefetch=1,
             grid=(1,),
             in_specs=[whole(g.shape) for g in grads],
-            out_specs=[kept((width, 128))] + [kept((width // planes, 128))] * planes,
+            out_specs=[kept((width, 128))] * 2,
             scratch_shapes=[pltpu.VMEM((2, width, 128), F32)],
         ),
-        out_shape=[jax.ShapeDtypeStruct((width, 128), BF16)]
-        + [jax.ShapeDtypeStruct((width // planes, 128), BF16)] * planes,
+        out_shape=[jax.ShapeDtypeStruct((width, 128), BF16)] * 2,
         compiler_params=params(),
         cost_estimate=cost(1e8, 2e6),
         name="small_pieces",
-    )(table, *grads)
+    )(grid.here, *grads)
 
 
 def finish_kernel(block_ref, *outs, group, classes, up_size):
@@ -922,12 +1070,14 @@
 
 
 class Grid:
-    def __init__(self, dp, fsdp):
+    def __init__(self, dp, fsdp, shard):
         self.size = {"c": 2, "x": fsdp // 2}
         self.size["z"] = 4 if dp % 4 == 0 else dp
         self.size["y"] = dp // self.size["z"]
         d, f = lax.axis_index("dp"), lax.axis_index("fsdp")
         self.at = {"z": d // self.size["y"], "y": d % self.size["y"], "x": f // 2, "c": f % 2}
+        self.plain = 2 * shard % 16 != 0 or self.size["x"] != 2 or self.size["y"] != 2
+        self.here = jnp.stack([self.at[a] for a in "zyxc"]).astype(jnp.int32)
 
     def number(self, at):
         dp = at["z"] * self.size["y"] + at["y"]
@@ -957,51 +1107,102 @@
         return jnp.concatenate(out, axis=0)
 
 
-def gather_pieces(grid, shard):
-    half = shard.shape[1] // 2
-    c = grid.at["c"]
-    mine = lax.dynamic_slice_in_dim(shard, c * half, half, 1)
-    other = lax.dynamic_slice_in_dim(shard, (1 - c) * half, half, 1)
-    chip = grid.ordered([mine, grid.send(other, "c", 1)], "c")
-    line = grid.ordered(grid.spread(chip, "x"), "x")
-    columns = grid.spread(line, "z")
-    planes = [[] for _ in range(grid.size["y"])]
-    for part in columns:
-        for o, got in enumerate(grid.spread(part, "y")):
-            planes[o].append(got)
-    own = [part for plane in planes for part in plane]
-    far = [grid.send(jnp.concatenate(plane, axis=0), "c", 1) for plane in planes]
-    return own, far
-
-
-def piece_table(grid, rows, sign):
-    oy, oz = jnp.meshgrid(jnp.arange(grid.size["y"]), jnp.arange(grid.size["z"]), indexing="ij")
-    z = (grid.at["z"] + sign * oz.reshape(-1)) % grid.size["z"]
-    y = (grid.at["y"] + sign * oy.reshape(-1)) % grid.size["y"]
-    lines = (z * grid.size["y"] + y) * rows
-    return jnp.concatenate([lines, jnp.reshape(grid.at["c"], (1,))]).astype(jnp.int32)
-
-
-def fetch_pieces(table, pieces, w_ref, sem, begin, finish):
-    own_count = sum(1 for p in pieces if p.shape[0] == pieces[0].shape[0])
-    own, far = pieces[:own_count], pieces[own_count:]
-    rows, half = own[0].shape
-    per = own_count // len(far)
-    core = table[own_count]
-    copies = []
-    for n in range(own_count):
-        at = pl.ds(pl.multiple_of(table[n], 16), rows)
-        near = pl.ds(pl.multiple_of(core * half, 128), half)
-        away = pl.ds(pl.multiple_of((1 - core) * half, 128), half)
-        copies.append(pltpu.make_async_copy(own[n], w_ref.at[at, near], sem.at[2 * n]))
-        source = far[n // per].at[pl.ds((n % per) * rows, rows)]
-        copies.append(pltpu.make_async_copy(source, w_ref.at[at, away], sem.at[2 * n + 1]))
-    for copy in copies:
-        if begin:
-            copy.start()
-    for copy in copies:
-        if finish:
-            copy.wait()
+def tie(*values):
+    return lax.optimization_barrier(values)
+
+
+class Gather:
+    def __init__(self, grid, mine, other, split):
+        self.grid, self.mine, self.other, self.split = grid, mine, other, split
+        self.rows, self.columns = 2 * mine.shape[0], 2 * mine.shape[1]
+        self.plain = grid.plain
+        self.parts = []
+
+    def along_z(self):
+        grid = self.grid
+        if self.plain:
+            shard = jnp.concatenate([self.mine, self.other], axis=1)
+            self.parts = [lax.all_gather(shard, AXES, axis=0, tiled=True)]
+            return
+        chip = grid.ordered([self.mine, grid.send(self.other, "c", 1)], "c")
+        self.stack = jnp.concatenate(grid.spread(chip, "z"), axis=0)
+
+    def along_xy(self):
+        if not self.plain:
+            self.from_x = self.grid.send(self.stack, "x", 1)
+            self.from_y = self.grid.send(self.stack, "y", 1)
+            self.near = self.grid.send(self.stack, "c", 1)
+
+    def diagonal(self):
+        if not self.plain:
+            self.one = self.grid.send(self.from_x[:, : self.split], "y", 1)
+            self.two = self.grid.send(self.from_y[:, self.split :], "x", 1)
+            self.near_x = self.grid.send(self.from_x, "c", 1)
+            self.near_y = self.grid.send(self.from_y, "c", 1)
+
+    def finish(self):
+        if not self.plain:
+            own = [self.stack, self.from_x, self.from_y, self.one, self.two]
+            far = [self.near, self.near_x, self.near_y]
+            far += [self.grid.send(self.one, "c", 1), self.grid.send(self.two, "c", 1)]
+            self.parts = own + far
+
+    def plan(self):
+        if self.plain:
+            return [(0, 0, self.parts[0].shape[0], self.columns, None, 0, 0, 0, 0)]
+        copies = []
+        steps = [(0, 0, 0), (0, 1, 0), (1, 0, 0), (1, 1, 0), (1, 1, self.split)]
+        for n, part in enumerate(self.parts):
+            dy, dx, begin = steps[n % 5]
+            for k in range(self.grid.size["z"]):
+                copies.append(
+                    (n, k * self.rows, self.rows, part.shape[1], dy, dx, k, n // 5, begin)
+                )
+        return copies
+
+
+def fetch(copies, here, size, parts, w_ref, sem):
+    z, y, x, c = (here[n] for n in range(4))
+    half = w_ref.shape[1] // 2
+    started = []
+    for n, (part, first, rows, columns, dy, dx, dz, far, begin) in enumerate(copies):
+        if dy is None:
+            to = w_ref
+        else:
+            line = (lax.rem(z + size["z"] - dz, size["z"]) * size["y"]) + lax.rem(y + dy, size["y"])
+            row = (line * size["x"] + lax.rem(x + dx, size["x"])) * rows
+            core = 1 - c if far else c
+            to = w_ref.at[
+                pl.ds(pl.multiple_of(row, 16), rows),
+                pl.ds(pl.multiple_of(core * half + begin, 128), columns),
+            ]
+        started.append(
+            pltpu.make_async_copy(parts[part].at[pl.ds(first, rows)], to, sem.at[n])
+        )
+    for copy in started:
+        copy.start()
+    for copy in started:
+        copy.wait()
+
+
+def line_rows(here, size, rows):
+    z, y = here[0], here[1]
+    return [
+        pl.multiple_of(
+            (lax.rem(z + oz, size["z"]) * size["y"] + lax.rem(y + oy, size["y"])) * rows, 16
+        )
+        for oy in range(size["y"])
+        for oz in range(size["z"])
+    ]
+
+
+def tie_lists(*lists):
+    flat = tie(*[value for part in lists for value in part])
+    out = []
+    for part in lists:
+        out.append(list(flat[: len(part)]))
+        flat = flat[len(part) :]
+    return out
 
 
 def add(*parts):
@@ -1011,37 +1212,63 @@
     return total
 
 
-def scatter_pieces(grid, other, planes):
-    rows, half = planes[0].shape
-    nz, nx = grid.size["z"], grid.size["x"]
-    got = grid.send(other, "c", 1)
-    came = []
-    for o in range(1, grid.size["y"]):
-        part = add(planes[o], got[o * rows : (o + 1) * rows]).astype(BF16)
-        came.append(grid.send(part, "y", o))
-    line = rows // nz
-    terms = [planes[0], got[:rows]] + came
-    cut = [add(*(t[o * line : (o + 1) * line] for t in terms)) for o in range(nz)]
-    came = [grid.send(cut[o].astype(BF16), "z", o) for o in range(1, nz)]
-    chip = line // nx
-    line_sum = add(cut[0], *came)
-    at = [(grid.at["x"] + o) % nx * chip for o in range(nx)]
-    cut = [lax.dynamic_slice_in_dim(line_sum, a, chip, 0) for a in at]
-    total = add(cut[0], *(grid.send(cut[o].astype(BF16), "x", o) for o in range(1, nx)))
-    c = grid.at["c"]
-    share = chip // 2
-    mine = lax.dynamic_slice_in_dim(total, c * share, share, 0)
-    far = lax.dynamic_slice_in_dim(total, (1 - c) * share, share, 0).astype(BF16)
-    far = grid.send(far, "c", 1).astype(F32)
-    return jnp.concatenate([jnp.where(c == 0, mine, far), jnp.where(c == 0, far, mine)], axis=1)
-
-
-def exchange(parts, fsdp):
-    out = []
-    for o, part in enumerate(parts):
-        pairs = [(m, (m + o + 1) % fsdp) for m in range(fsdp)]
-        out.append(lax.ppermute(part, "fsdp", pairs))
-    return out
+class Scatter:
+    def __init__(self, grid, mine, split):
+        self.grid, self.mine, self.split = grid, mine, split
+
+    def core(self, others):
+        self.got = [self.grid.send(other, "c", 1) for other in others]
+
+    def line(self, array, offset, axis):
+        at = (self.grid.at["x"] + offset) % self.grid.size["x"]
+        return lax.dynamic_index_in_dim(array, at, axis, keepdims=False)
+
+    def begin(self):
+        grid = self.grid
+        total = jnp.concatenate([add(m, g) for m, g in zip(self.mine, self.got)], axis=1)
+        sizes = [grid.size[a] for a in "yzx"]
+        chip = total.shape[0] // math.prod(sizes)
+        total = total.reshape(*sizes, chip, total.shape[1])
+        left, right = total[..., : self.split], total[..., self.split :]
+        self.keep_one, self.keep_two = left[0], self.line(right, 0, 2)
+        self.out_one = [left[o].astype(BF16) for o in range(1, grid.size["y"])]
+        self.out_two = [self.line(right, o, 2).astype(BF16) for o in range(1, grid.size["x"])]
+
+    def first(self):
+        grid = self.grid
+        self.in_one = [grid.send(p, "y", o + 1) for o, p in enumerate(self.out_one)]
+        self.in_two = [grid.send(p, "x", o + 1) for o, p in enumerate(self.out_two)]
+
+    def second(self):
+        grid = self.grid
+        one, two = add(self.keep_one, *self.in_one), add(self.keep_two, *self.in_two)
+        self.keep_one, self.keep_two = self.line(one, 0, 1), two[0]
+        self.in_one = [
+            grid.send(self.line(one, o, 1).astype(BF16), "x", o) for o in range(1, grid.size["x"])
+        ]
+        self.in_two = [grid.send(two[o].astype(BF16), "y", o) for o in range(1, grid.size["y"])]
+
+    def third(self):
+        grid = self.grid
+        total = jnp.concatenate(
+            [add(self.keep_one, *self.in_one), add(self.keep_two, *self.in_two)], axis=2
+        )
+        self.keep = total[0]
+        self.came = [grid.send(total[o].astype(BF16), "z", o) for o in range(1, grid.size["z"])]
+
+    def last(self):
+        grid = self.grid
+        total = add(self.keep, *self.came)
+        c = grid.at["c"]
+        share = total.shape[0] // 2
+        mine = lax.dynamic_slice_in_dim(total, c * share, share, 0)
+        far = lax.dynamic_slice_in_dim(total, (1 - c) * share, share, 0).astype(BF16)
+        far = grid.send(far, "c", 1).astype(F32)
+        return jnp.concatenate([jnp.where(c == 0, mine, far), jnp.where(c == 0, far, mine)], axis=1)
+
+
+def exchange(part, fsdp, offset):
+    return lax.ppermute(part, "fsdp", [(m, (m + offset) % fsdp) for m in range(fsdp)])
 
 
 def body(
@@ -1082,12 +1309,7 @@
     block = min(count, 256)
     wide_block = min(count, 512)
     shard = width // devices
-    grid = Grid(lax.axis_size("dp"), fsdp)
-    line = grid.size["x"] * 2 * shard
-    table_in = piece_table(grid, line, -1)
-    table_down = piece_table(grid, line * ff // width, -1)
-    table_out = piece_table(grid, line, 1)
-    planes = grid.size["y"]
+    grid = Grid(lax.axis_size("dp"), fsdp, shard)
     vectors = (
         query_bias,
         value_bias,
@@ -1098,47 +1320,72 @@
         second_gain,
         second_shift,
     )
-    small = pack_small(vectors, up_bias, pool_weight, class_weight, (student_bias, pool_query, pool_bias))
     cut = 3 * width // 2
-    own, far = gather_pieces(
-        grid,
-        jnp.concatenate([input_weight[:, :cut], student_weight, input_weight[:, cut:], small], axis=1),
-    )
-    pieces = own + far
-    large = lax.all_gather(
-        jnp.concatenate([output_weight, up_weight], axis=1), AXES, axis=0, tiled=True
-    )
-    own, far = gather_pieces(grid, down_weight)
-    down_pieces = own + far
-
+    here = grid.here
+    if grid.plain:
+        here = here * jnp.array([1, 1, 1, 0], jnp.int32)
+    in_mine, in_other, ff_mine, ff_other = pack(
+        here,
+        input_weight,
+        student_weight,
+        output_weight,
+        up_weight,
+        up_bias,
+        pool_weight,
+        class_weight,
+        logits_grad,
+        (student_bias, pool_query, pool_bias),
+        vectors,
+    )
     capacity, out_pick, in_origin, in_place, back_pick, back_origin, back_place = routes(
         destination, samples, fsdp
     )
     alive = (exit_layer > LAYER).astype(jnp.int32)
+
+    wd = lax.all_gather(down_weight, AXES, axis=0, tiled=True)
+    g_in = Gather(grid, in_mine, in_other, (cut + 128) // 256 * 128)
+    g_in.along_z()
     outgoing = pick(back_pick, repacked_grad, fsdp - 1, capacity)
-    returned = exchange(outgoing, fsdp)
+    returned = [exchange(outgoing[0], fsdp, 1)]
+    if not grid.plain:
+        g_in.stack, ff_mine, returned[0] = tie(g_in.stack, ff_mine, returned[0])
+    g_ff = Gather(grid, ff_mine, ff_other, (ff + width) // 512 * 128 + 128)
+    g_in.along_xy()
+    g_in.diagonal()
+    g_ff.along_z()
+    g_in.finish()
+    if not grid.plain:
+        *g_in.parts, g_ff.stack = tie(*g_in.parts, g_ff.stack)
+    g_ff.along_xy()
+    rows = tokens.reshape(count, width)
+    qkv, prob, mixed, turned, vec, sv, pw, cw, ubm, cb, ws = attend(
+        lengths, g_in, rows, seq, wide_block, stu, classes, devices, ff // devices
+    )
+    rest = list(outgoing[1:])
+    if not grid.plain:
+        mixed, g_ff.from_x, g_ff.from_y, g_ff.near, *rest = tie(
+            mixed, g_ff.from_x, g_ff.from_y, g_ff.near, *rest
+        )
+    g_ff.diagonal()
+    returned += [exchange(part, fsdp, o + 2) for o, part in enumerate(rest)]
+    g_ff.finish()
+    ub = jnp.broadcast_to(ubm[:, : ff // devices].reshape(1, ff), (8, ff))
+    normed, factor, low, act, slope = up_part(g_ff, mixed, rows, vec, ub, block)
+    act, *returned = tie(act, *returned)
     second_cot = place(back_origin, back_place, [repacked_grad] + returned)
-
-    rows = tokens.reshape(count, width)
-    qkv, prob, mixed, vec, sv, pw, cw, ubm, ws = attend(
-        lengths, table_in, rows, pieces, seq, block, stu, classes, devices
-    )
-    ub = jnp.broadcast_to(ubm[:, : ff // devices].reshape(1, ff), (8, ff))
-    normed, factor, low, act, slope = up_part(mixed, rows, large, vec, ub, block)
     steps = count // wide_block
     lg = jnp.pad(
         logits_grad.reshape(steps, samples // steps, classes),
         ((0, 0), (0, 8 - samples // steps), (0, 128 - classes)),
     ).reshape(steps * 8, 128)
-    second, sum_two, dcot, logits, vgrad_two, sgrad, wsgrad, pwgrad, cwgrad = down_part(
+    second, sum_two, dcot, logits, vgrad_two, sgrad, wsgrad, pwgrad, cwgrad, wd_grad = down_part(
         lengths,
         alive,
-        table_down,
         act,
         normed,
         second_cot.reshape(count, width),
         lg,
-        down_pieces,
+        wd,
         vec,
         ws,
         sv,
@@ -1146,38 +1393,61 @@
         cw,
         seq,
         wide_block,
+        ff // 6,
     )
     student_logits = logits.reshape(steps, 8, 128)[:, : samples // steps, :classes].reshape(
         samples, classes
     ) + class_bias.astype(F32)
     second = second.reshape(samples, seq, width)
+    wd_share = lax.psum_scatter(wd_grad, AXES, scatter_dimension=0, tiled=True)
     leaving = pick(out_pick, second, fsdp - 1, capacity)
-    arrived = exchange(leaving, fsdp)
-
-    wd_grad = weight_part(act, dcot, 256, "down_grad")
-    wd_share = lax.psum_scatter(wd_grad, AXES, scatter_dimension=0, tiled=True)
-    ucot, one_cot, acot, mcot, vgrad_one, ugrad = up_back(
-        table_down, dcot, slope, sum_two, normed, factor, down_pieces, large, vec, wide_block
-    )
-    wo_grad = weight_pieces(table_out, mixed, acot, 128, planes, "output_grad")
-    wu_grad = weight_pieces(table_out, low, ucot, 512, planes, "up_grad")
-    ff_grad = [jnp.concatenate(pair, axis=1) for pair in zip(wu_grad, wo_grad)]
-    ff_share = scatter_pieces(grid, ff_grad[0], ff_grad[1:])
-    pcot, vgrad_in = attend_back(mcot, qkv, prob, seq, block)
+    dcot, *leaving = tie(dcot, *leaving)
+    arrived = [exchange(part, fsdp, o + 1) for o, part in enumerate(leaving)]
+    one_cot, mcot, vgrad_one, ugrad, wu_other, wu_mine, wo_other, wo_mine = up_back(
+        g_ff, dcot, slope, sum_two, normed, factor, low, mixed, wd, vec, block, ff // 6
+    )
+    mcot, wu_other, wo_other, *arrived = tie(mcot, wu_other, wo_other, *arrived)
+    s_ff = Scatter(grid, [wo_mine, wu_mine], (ff + width) // 512 * 128 + 128)
+    s_ff.core([wo_other, wu_other])
+    s_ff.begin()
+    mcot, *out = tie(mcot, *s_ff.out_one, *s_ff.out_two)
+    s_ff.out_one, s_ff.out_two = out[: len(s_ff.out_one)], out[len(s_ff.out_one) :]
+    s_ff.first()
+    pcot, vgrad_in = attend_back(mcot, qkv, prob, seq, wide_block)
+    (pcot, vgrad_in), s_ff.in_one, s_ff.in_two = tie_lists(
+        (pcot, vgrad_in), s_ff.in_one, s_ff.in_two
+    )
+    s_ff.second()
     ugm = jnp.pad(ugrad[0].reshape(devices, -1), ((0, 0), (0, 128 - ff // devices)))
-    small_grad = small_pieces(
-        table_out,
+    small_other, small_mine = small_pieces(
+        grid,
         (vgrad_in, vgrad_one, vgrad_two, ugm, sgrad, wsgrad, pwgrad, cwgrad),
-        planes,
         classes,
         devices,
     )
-    wi_grad = weight_pieces(table_out, rows, pcot, 384, planes, "input_grad")
-    in_grad = [jnp.concatenate(pair, axis=1) for pair in zip(wi_grad, small_grad)]
-    in_share = scatter_pieces(grid, in_grad[0], in_grad[1:])
-    tokens_grad = token_part(table_in, pcot, one_cot, pieces, wide_block).reshape(samples, seq, width)
+    wi_other, wi_mine = input_grad(grid.here, turned, pcot, width // 2)
+    (wi_other, small_other, wd_share), s_ff.in_one, s_ff.in_two, arrived = tie_lists(
+        (wi_other, small_other, wd_share), s_ff.in_one, s_ff.in_two, arrived
+    )
+    s_in = Scatter(grid, [wi_mine, small_mine], (cut + 128) // 2)
+    s_in.core([wi_other, small_other])
+    s_ff.third()
     repacked = place(in_origin, in_place, [second] + arrived)
-    class_bias_grad = lax.psum(jnp.sum(logits_grad.astype(F32), axis=0), AXES)
+    s_in.begin()
+    (pcot, repacked), s_in.out_one, s_in.out_two = tie_lists(
+        (pcot, repacked), s_in.out_one, s_in.out_two
+    )
+    s_in.first()
+    tokens_grad = token_part(g_in, pcot, one_cot, wide_block)
+    (tokens_grad,), s_in.in_one, s_in.in_two, s_ff.came = tie_lists(
+        (tokens_grad,), s_in.in_one, s_in.in_two, s_ff.came
+    )
+    tokens_grad = tokens_grad.reshape(samples, seq, width)
+    s_in.second()
+    ff_share = s_ff.last()
+    s_in.third()
+    in_share = s_in.last()
+    class_bias_grad = cb[0, :classes]
 
     half = cut + 128
     input_share = jnp.concatenate([in_share[:, :cut], in_share[:, half : half + cut]], axis=1)
@@ -1196,12 +1466,10 @@
         name="finish",
     )(in_share[:, half + cut :])
     qb, vb, ob, g1, s1, db, g2, s2 = (o.reshape(-1) for o in outs[:8])
-    up_half = ff // 2
-    wu_share = jnp.concatenate(
-        [ff_share[:, :up_half], ff_share[:, up_half + width // 2 : ff + width // 2]], axis=1
-    )
-    wo_share = jnp.concatenate(
-        [ff_share[:, up_half : up_half + width // 2], ff_share[:, ff + width // 2 :]], axis=1
+    ff_half = (ff + width) // 2
+    wo_share, wu_share = (
+        jnp.concatenate([ff_share[:, b:e], ff_share[:, ff_half + b : ff_half + e]], axis=1)
+        for b, e in ((0, width // 2), (width // 2, ff_half))
     )
     return (
         repacked,

time: 620 us -> 417 us (0.67)
  blocking collectives: 71.3 us -> 0 us
  waiting for transfers between devices: 138 us -> 69.7 us
  Pallas kernels: 267 us -> 234 us
  other arithmetic: 39.2 us -> 25 us
  starting transfers between devices: 55 us -> 43.9 us
  local copies, waits for them, and re-layouts: 29.8 us -> 22.5 us
    ppermute x36 -> x46, waiting for transfers between devices: 138 us -> 61.3 us  [send(): return lax.ppermute(array, AXES, pairs)]
    psum x1 -> x0, blocking collectives: 71.3 us -> none  [body(): class_bias_grad = lax.psum(jnp.sum(logits_grad.astype(F32), axis=0), AXES)]
    pallas_call x10 -> x8, Pallas kernels: 225 us -> 191 us  [the longest x1 58.2 us: up_back(): pl.pallas_call(functools.partial(up_back_kernel, copies=copies, size=size...]
    concatenate x11 -> x4, other arithmetic: 14.6 us -> 2.06 us  [the longest x2 1.37 us: body(): jnp.concatenate([ff_share[:, b:e], ff_share[:, ff_half + b:ff_half + e]],...]
    ppermute x36 -> x46, starting transfers between devices: 49.5 us -> 39.2 us  [send(): return lax.ppermute(array, AXES, pairs)]
    add x4 -> x14, other arithmetic: 2.6 us -> 12.7 us  [add(): total = total + part.astype(F32)]
    convert_element_type x4 -> x0, other arithmetic: 8.49 us -> none  [the longest x2 4.31 us: scatter_pieces(): part = add(planes[o], got[o * rows:(o + 1) * rows]).astype(BF16)]
    ppermute x6, waiting for transfers between devices: 0.02 us -> 7.75 us  [exchange(): lax.ppermute(part, 'fsdp', [(m, (m + offset) % fsdp) for m in range(fsdp)])]
  transfers between devices with their start and end apart: 44 -> 54, of which waited for: 16 -> 16; matrix products, arithmetic and copies ran while one was open for 9% -> 7% of each run, Pallas kernels for 22% -> 44%
where the time goes in v2:
time: 417 us; the launch traced here: 410 us
  Pallas kernels  234 us (56%)
  waiting for transfers between devices  69.7 us (17%)
  starting transfers between devices  43.9 us (11%)
  other arithmetic  25 us (6%)
  local copies, waits for them, and re-layouts  22.5 us (5%)
  between operations  15.5 us (4%)
    ppermute x46, waiting for transfers between devices, send(): return lax.ppermute(array, AXES, pairs)  61.3 us
    pallas_call x1, Pallas kernels, up_back(): pl.pallas_call(functools.partial(up_back_kernel, copies=copies, size=size...  58.2 us
    pallas_call x1, Pallas kernels, down_part(): pl.pallas_call(functools.partial(down_kernel, seq=seq, steps=steps, tile=...  46.5 us
    ppermute x46, starting transfers between devices, send(): return lax.ppermute(array, AXES, pairs)  39.2 us
    pallas_call x1, Pallas kernels, up_part(): pl.pallas_call(functools.partial(up_kernel, copies=copies, size=size, chu...  26.5 us
    pallas_call x1, Pallas kernels, attend_back(): pl.pallas_call(functools.partial(attend_back_kernel, seq=seq, width=width...  24.1 us
    pallas_call x1, Pallas kernels, attend(): pl.pallas_call(functools.partial(attend_kernel, copies=copies, size=size,...  22.6 us
    pallas_call x1, Pallas kernels, token_part(): pl.pallas_call(functools.partial(token_kernel, copies=copies, size=size),...  16.1 us
  transfers between devices with their start and end apart: 54, of which 16 were waited for; matrix products, arithmetic and copies ran while one was open for 7% of the time, Pallas kernels for 44%

profile of v2, /device:TPU:0, one launch (start us, length us, event | category | flops | bytes accessed | tf_op | source)
XLA Modules:
  0.0 410.5 jit_solution(9270691607482530079)
XLA Ops:
  8.6 2.7 pack.1
  15.5 4.8 %pick.2 = (bf16[6,128,768]{2,1,0:T(8,128)(2,1)}, bf16[6,128,768]{2,1,0:T(8,128)(2,1)}, bf16[6,128,768]{2,1,0:T(8,128)(2,1)}) custom-call(s32[3,6]{1,0:T(4,128)} %select_reduce_fusion.4.table, bf16[16,128,768]{2,1,0:T(8,128)(2,1)} %refs_0_.3), custom_call_target="tpu_custom_call" | custom-call | bytes 2123366 | tf_op jit(solution)/shard_map/pick/pallas_call | solution.py:972
  20.5 3.5 collective-permute-start.1
  24.9 2.1 collective-permute-start.3
  28.0 2.9 collective-permute-done.1
  30.9 9.6 %collective-permute-done.2 = bf16[48,1280]{1,0:T(8,128)(2,1)S(1)} collective-permute-done((bf16[48,1280]{1,0:T(8,128)(2,1)S(1)}, bf16[48,1280]{1,0:T(8,128)(2,1)S(1)}, u32[]{:S(2)}, u32[]{:S(2)}) %collective-permute-start.2) | collective-permute-done | bytes 122912 | tf_op jit(solution)/shard_map/ppermute | solution.py:1094
  40.6 1.4 collective-permute-start.6
  44.2 1.4 collective-permute-start.17
  46.5 9.5 %collective-permute-done.6.refs_3_.refs_4_ = bf16[192,1280]{1,0:T(8,128)(2,1)S(1)} collective-permute-done((bf16[192,1280]{1,0:T(8,128)(2,1)S(1)}, bf16[192,1280]{1,0:T(8,128)(2,1)S(1)}, u32[]{:S(2)}, u32[]{:S(2)}) %collective-permute-start.6) | collective-permute-done | bytes 491552 | tf_op jit(solution)/shard_map/ppermute | solution.py:1094
  57.3 2.7 collective-permute-done.5.refs_2_.refs_3_
  60.6 6.1 %collective-permute-done.16 = bf16[48,1920]{1,0:T(8,128)(2,1)S(1)} collective-permute-done((bf16[48,1920]{1,0:T(8,128)(2,1)S(1)}, bf16[48,1920]{1,0:T(8,128)(2,1)S(1)}, u32[]{:S(2)}, u32[]{:S(2)}) %collective-permute-start.16) | collective-permute-done | bytes 184352 | tf_op jit(solution)/shard_map/ppermute | solution.py:1094
  73.7 22.6 %attend.1 = (bf16[2048,2304]{1,0:T(8,128)(2,1)}, bf16[16,6,128,256]{3,2,1,0:T(8,128)(2,1)}, bf16[2048,768]{1,0:T(8,128)(2,1)}, bf16[768,2048]{1,0:T(8,128)(2,1)}...) custom-call(s32[16]{0:T(128)} %lens.3, ...), custom_call_target="tpu_custom_call" | custom-call | flops 4348654592 | bytes 9000000 | tf_op jit(solution)/shard_map/attend/pallas_call | solution.py:283
  96.5 1.4 collective-permute-start.22
  98.8 7.5 %collective-permute-done.22.refs_8_.refs_13_ = bf16[192,896]{1,0:T(8,128)(2,1)} collective-permute-done((bf16[192,896]{1,0:T(8,128)(2,1)S(1)}, bf16[192,896]{1,0:T(8,128)(2,1)}, u32[]{:S(2)}, u32[]{:S(2)}) %collective-permute-start.22) | collective-permute-done | bytes 344096 | tf_op jit(solution)/shard_map/ppermute | solution.py:1094
  107.4 1.5 collective-permute-start.27
  113.4 26.5 %up_part.1 = (f32[2048,768]{1,0:T(8,128)}, f32[2048,128]{1,0:T(8,128)}, bf16[2048,768]{1,0:T(8,128)(2,1)}, bf16[2048,3072]{1,0:T(8,128)(2,1)}, bf16[2048,3072]{1,0:T(8,128)(2,1)}) custom-call(s32[4]{0:T(128)} %pad_add_fusion.here, bf16[2048,768]{1,0:T(8,128)(2,1)} %get-tuple-element.169.refs_0_.refs_6_, bf16[2048,768]{1,0:T(8,128)(2,1)} %bitcast.160, ...), custom_call_target="tpu_custom_call" | custom-call | flops 7247757312 | bytes 15000000 | tf_op jit(solution)/shard_map/up_part/pallas_call | solution.py:357
  139.9 7.7 %collective-permute-done.28.refs_3_ = bf16[6,128,768]{2,1,0:T(8,128)(2,1)} collective-permute-done((bf16[6,128,768]{2,1,0:T(8,128)(2,1)}, bf16[6,128,768]{2,1,0:T(8,128)(2,1)}, u32[]{:S(2)}, u32[]{:S(2)}) %collective-permute-start.28) | collective-permute-done | bytes 1179680 | tf_op jit(solution)/shard_map/ppermute | solution.py:1271
  147.7 3.8 place.2
  151.5 46.5 %down_part.1 = (bf16[2048,768]{1,0:T(8,128)(2,1)}, f32[2048,768]{1,0:T(8,128)}, bf16[2048,768]{1,0:T(8,128)(2,1)}, f32[32,128]{1,0:T(8,128)}, f32[8,768]{1,0:T(8...) custom-call(s32[16]{0:T(128)} %lens.3, ...), custom_call_target="tpu_custom_call" | custom-call | flops 11596411904 | bytes 18000000 | tf_op jit(solution)/shard_map/down_part/pallas_call | solution.py:530
  198.1 4.3 %pick.3 = (bf16[6,128,768]{2,1,0:T(8,128)(2,1)}, bf16[6,128,768]{2,1,0:T(8,128)(2,1)}, bf16[6,128,768]{2,1,0:T(8,128)(2,1)}) custom-call(s32[3,6]{1,0:T(4,128)} %select_reduce_fusion.3.table, bf16[16,128,768]{2,1,0:T(8,128)(2,1)} %bitcast.139), custom_call_target="tpu_custom_call" | custom-call | bytes 2123366 | tf_op jit(solution)/shard_map/pick/pallas_call | solution.py:972
  203.3 1.5 collective-permute-start.30
  205.0 58.2 %up_back.1 = (f32[2048,768]{1,0:T(8,128)}, bf16[2048,768]{1,0:T(8,128)(2,1)}, f32[8,768]{1,0:T(8,128)}, f32[8,3072]{1,0:T(8,128)}, bf16[768,1536]{1,0:T(8,128)(2...) custom-call(s32[4]{0:T(128)} %pad_add_fusion.here, ...), custom_call_target="tpu_custom_call" | custom-call | flops 11596411904 | bytes 18000000 | tf_op jit(solution)/shard_map/up_back/pallas_call | solution.py:671
  263.9 5.3 %collective-permute-done.32 = bf16[768,384]{1,0:T(8,128)(2,1)} collective-permute-done((bf16[768,384]{1,0:T(8,128)(2,1)}, bf16[768,384]{1,0:T(8,128)(2,1)}, u32[]{:S(2)}, u32[]{:S(2)}) %collective-permute-start.32) | collective-permute-done | bytes 589856 | tf_op jit(solution)/shard_map/ppermute | solution.py:1094
  269.2 1.4 convert_add_fusion.2
  270.5 2.3 convert_add_fusion
  274.7 1.4 copy-done
  276.2 1.5 collective-permute-start.34
  278.4 24.1 %attend_back.1 = (bf16[2048,2304]{1,0:T(8,128)(2,1)}, f32[8,768]{1,0:T(8,128)}) custom-call(bf16[2048,768]{1,0:T(8,128)(2,1)} %get-tuple-element.209.mcot_ref, bf16[2048,2304]{1,0:T(8,128)(2,1)} %get-tuple-element.210.qkv_ref, bf16[16,6,128,256]{3,2,1,0:T(8,128)(2,1)} %get-tuple-element.211.prob_ref), custom_call_target="tpu_custom_call" | custom-call | flops 4348654592 | bytes 9000000 | tf_op jit(solution)/shard_map/attend_back/pallas_call | solution.py:817
  306.1 1.9 fusion
  310.3 3.3 small_pieces.1
  313.6 15.6 %input_grad.1 = (bf16[768,1152]{1,0:T(8,128)(2,1)}, bf16[768,1152]{1,0:T(8,128)(2,1)}) custom-call(s32[4]{0:T(128)} %pad_add_fusion.here, bf16[768,2048]{1,0:T(8,128)(2,1)} %get-tuple-element.217.turned_ref, bf16[2048,2304]{1,0:T(8,128)(2,1)} %get-tuple-element.243.pcot_ref.refs_0_), custom_call_target="tpu_custom_call" | custom-call | flops 2174327296 | bytes 6000000 | tf_op jit(solution)/shard_map/input_grad/pallas_call | solution.py:756
  332.3 1.6 convert_element_type.201
  334.0 4.0 place.3
  340.1 1.8 convert_add_fusion.1
  343.2 1.3 copy-done.5
  345.3 1.7 collective-permute-start.40
  348.5 3.4 collective-permute-start.44
  351.9 1.4 collective-permute-start.42
  353.3 16.1 %token_part.1 = f32[2048,768]{1,0:T(8,128)} custom-call(s32[4]{0:T(128)} %pad_add_fusion.here, bf16[2048,2304]{1,0:T(8,128)(2,1)} %get-tuple-element.243.pcot_ref.refs_0_, f32[2048,768]{1,0:T(8,128)} %get-tuple-element.244.refs_1_, bf16[192,1280]{1,0:T(8,128)(2,1)} %copy-done.18, bf16[192,1280]{1,0:T(8,128)(2,1)} %copy-done.16, ...), custom_call_target="tpu_custom_call" | custom-call | flops 2174327296 | bytes 7500000 | tf_op jit(solution)/shard_map/token_part/pallas_call | solution.py:861
  369.4 1.5 bitcast_add_fusion.1
  374.6 1.4 collective-permute-start.45
  376.0 5.8 %collective-permute-done.46 = bf16[4,48,640]{2,1,0:T(8,128)(2,1)S(1)} collective-permute-done((bf16[4,48,640]{2,1,0:T(8,128)(2,1)S(1)}, bf16[4,48,640]{2,1,0:T(8,128)(2,1)S(1)}, u32[]{:S(2)}, u32[]{:S(2)}) %collective-permute-start.46) | collective-permute-done | bytes 245792 | tf_op jit(solution)/shard_map/ppermute | solution.py:1094
  382.8 2.3 collective-permute-start.47
  385.1 1.6 collective-permute-start.49
  387.5 3.5 collective-permute-done.47
  392.1 5.1 %collective-permute-done.48 = bf16[48,1280]{1,0:T(8,128)(2,1)S(1)} collective-permute-done((bf16[48,1280]{1,0:T(8,128)(2,1)S(1)}, bf16[48,1280]{1,0:T(8,128)(2,1)S(1)}, u32[]{:S(2)}, u32[]{:S(2)}) %collective-permute-start.48) | collective-permute-done | bytes 122912 | tf_op jit(solution)/shard_map/ppermute | solution.py:1094
  399.8 1.4 finish.1
  401.9 1.3 pad_maximum_fusion.9
  (247 shorter events, 54.7 us)
Async XLA Ops:
  7.2 144.3 %all-gather.2.cloned.1.call-start = ((), (), s32[]{:S(2)}) async-start(), calls=%async_computation.1 | async-start | bytes 4866048 | tf_op jit(solution)/shard_map/all_gather | solution.py:1345
  7.9 321.3 %reduce-scatter.2.cloned.1.call-start = ((), (), s32[]{:S(2)}) async-start(), calls=%async_computation.2 | async-start | bytes 4866048 | tf_op jit(solution)/shard_map/reduce_scatter | solution.py:1402
  11.3 9.2 %collective-permute-start = (bf16[24,1280]{1,0:T(8,128)(2,1)}, bf16[24,1280]{1,0:T(8,128)(2,1)S(1)}, u32[]{:S(2)}, u32[]{:S(2)}) collective-permute-start(bf16[24,1280]{1,0:T(8,128)(2,1)} %get-tuple-element.148), channel_id=1, source_target_pairs={{0,1},{1,0},{2,3},{3,2},{4,5},{5,4},{6,7},{7,6},{8,9},{9,8},{10,11... | collective-permute-start | bytes 184328 | tf_op jit(solution)/shard_map/ppermute | solution.py:1094
  20.3 20.3 %collective-permute-start.4 = (bf16[6,128,768]{2,1,0:T(8,128)(2,1)}, bf16[6,128,768]{2,1,0:T(8,128)(2,1)S(1)}, u32[]{:S(2)}, u32[]{:S(2)}) collective-permute-start(bf16[6,128,768]{2,1,0:T(8,128)(2,1)} %get-tuple-element.151), channel_id=1, source_target_pairs={{0,1},{1,2},{2,3},{3,0},{4,5},{5,6},{6,7},{7,4},{8,9},{9,10},{10,1... | collective-permute-start | bytes 3538952 | tf_op jit(solution)/shard_map/ppermute | solution.py:1271
  20.5 10.3 %collective-permute-start.1 = (bf16[48,1280]{1,0:T(8,128)(2,1)S(1)}, bf16[48,1280]{1,0:T(8,128)(2,1)S(1)}, u32[]{:S(2)}, u32[]{:S(2)}) collective-permute-start(bf16[48,1280]{1,0:T(8,128)(2,1)S(1)} %pad_maximum_fusion.7), channel_id=1, source_target_pairs={{0,8},{1,9},{2,10},{3,11},{4,12},{5,13},{6,14},{7,15},{8,16},{9,17... | collective-permute-start | bytes 368648 | tf_op jit(solution)/shard_map/ppermute | solution.py:1094
  24.1 18.8 %collective-permute-start.14 = (bf16[24,1920]{1,0:T(8,128)(2,1)S(1)}, bf16[24,1920]{1,0:T(8,128)(2,1)S(1)}, u32[]{:S(2)}, u32[]{:S(2)}) collective-permute-start(bf16[24,1920]{1,0:T(8,128)(2,1)S(1)} %copy-done.33), channel_id=1, source_target_pairs={{0,1},{1,0},{2,3},{3,2},{4,5},{5,4},{6,7},{7,6},{8,9},{9,8},{10,11... | collective-permute-start | bytes 276488 | tf_op jit(solution)/shard_map/ppermute | solution.py:1094
  24.9 15.7 %collective-permute-start.3 = (bf16[48,1280]{1,0:T(8,128)(2,1)S(1)}, bf16[48,1280]{1,0:T(8,128)(2,1)S(1)}, u32[]{:S(2)}, u32[]{:S(2)}) collective-permute-start(bf16[48,1280]{1,0:T(8,128)(2,1)S(1)} %pad_maximum_fusion.7), channel_id=1, source_target_pairs={{0,24},{1,25},{2,26},{3,27},{4,28},{5,29},{6,30},{7,31},{8,0},{9,1... | collective-permute-start | bytes 368648 | tf_op jit(solution)/shard_map/ppermute | solution.py:1094
  27.0 13.5 %collective-permute-start.2 = (bf16[48,1280]{1,0:T(8,128)(2,1)S(1)}, bf16[48,1280]{1,0:T(8,128)(2,1)S(1)}, u32[]{:S(2)}, u32[]{:S(2)}) collective-permute-start(bf16[48,1280]{1,0:T(8,128)(2,1)S(1)} %pad_maximum_fusion.7), channel_id=1, source_target_pairs={{0,16},{1,17},{2,18},{3,19},{4,20},{5,21},{6,22},{7,23},{8,24},{9,... | collective-permute-start | bytes 368648 | tf_op jit(solution)/shard_map/ppermute | solution.py:1094
  40.6 15.4 %collective-permute-start.6 = (bf16[192,1280]{1,0:T(8,128)(2,1)S(1)}, bf16[192,1280]{1,0:T(8,128)(2,1)S(1)}, u32[]{:S(2)}, u32[]{:S(2)}) collective-permute-start(bf16[192,1280]{1,0:T(8,128)(2,1)S(1)} %constant_dynamic-update-slice_fusion.refs_1_.refs_2_), channel_id=1, source_target_pairs={{0,4},{1,5},{2,6},{3,7},{4,0},{5,1},{6,2},{7,3},{8,12},{9,13},{10,... | collective-permute-start | bytes 1474568 | tf_op jit(solution)/shard_map/ppermute | solution.py:1094
  42.0 18.0 %collective-permute-start.5 = (bf16[192,1280]{1,0:T(8,128)(2,1)S(1)}, bf16[192,1280]{1,0:T(8,128)(2,1)S(1)}, u32[]{:S(2)}, u32[]{:S(2)}) collective-permute-start(bf16[192,1280]{1,0:T(8,128)(2,1)S(1)} %constant_dynamic-update-slice_fusion.refs_1_.refs_2_), channel_id=1, source_target_pairs={{0,2},{1,3},{2,0},{3,1},{4,6},{5,7},{6,4},{7,5},{8,10},{9,11},{10,... | collective-permute-start | bytes 1474568 | tf_op jit(solution)/shard_map/ppermute | solution.py:1094
  44.2 16.4 %collective-permute-start.17 = (bf16[48,1920]{1,0:T(8,128)(2,1)S(1)}, bf16[48,1920]{1,0:T(8,128)(2,1)S(1)}, u32[]{:S(2)}, u32[]{:S(2)}) collective-permute-start(bf16[48,1920]{1,0:T(8,128)(2,1)S(1)} %pad_maximum_fusion.6), channel_id=1, source_target_pairs={{0,24},{1,25},{2,26},{3,27},{4,28},{5,29},{6,30},{7,31},{8,0},{9,1... | collective-permute-start | bytes 552968 | tf_op jit(solution)/shard_map/ppermute | solution.py:1094
  45.6 21.1 %collective-permute-start.16 = (bf16[48,1920]{1,0:T(8,128)(2,1)S(1)}, bf16[48,1920]{1,0:T(8,128)(2,1)S(1)}, u32[]{:S(2)}, u32[]{:S(2)}) collective-permute-start(bf16[48,1920]{1,0:T(8,128)(2,1)S(1)} %pad_maximum_fusion.6), channel_id=1, source_target_pairs={{0,16},{1,17},{2,18},{3,19},{4,20},{5,21},{6,22},{7,23},{8,24},{9,... | collective-permute-start | bytes 552968 | tf_op jit(solution)/shard_map/ppermute | solution.py:1094
  45.6 21.1 %collective-permute-start.15 = (bf16[48,1920]{1,0:T(8,128)(2,1)S(1)}, bf16[48,1920]{1,0:T(8,128)(2,1)S(1)}, u32[]{:S(2)}, u32[]{:S(2)}) collective-permute-start(bf16[48,1920]{1,0:T(8,128)(2,1)S(1)} %pad_maximum_fusion.6), channel_id=1, source_target_pairs={{0,8},{1,9},{2,10},{3,11},{4,12},{5,13},{6,14},{7,15},{8,16},{9,17... | collective-permute-start | bytes 552968 | tf_op jit(solution)/shard_map/ppermute | solution.py:1094
  56.0 11.9 %collective-permute-start.8 = (bf16[192,640]{1,0:T(8,128)(2,1)S(1)}, bf16[192,640]{1,0:T(8,128)(2,1)S(1)}, u32[]{:S(2)}, u32[]{:S(2)}) collective-permute-start(bf16[192,640]{1,0:T(8,128)(2,1)S(1)} %slice.159), channel_id=1, source_target_pairs={{0,2},{1,3},{2,0},{3,1},{4,6},{5,7},{6,4},{7,5},{8,10},{9,11},{10,... | collective-permute-start | bytes 737288 | tf_op jit(solution)/shard_map/ppermute | solution.py:1094
  60.0 7.9 %collective-permute-start.7 = (bf16[192,640]{1,0:T(8,128)(2,1)S(1)}, bf16[192,640]{1,0:T(8,128)(2,1)S(1)}, u32[]{:S(2)}, u32[]{:S(2)}) collective-permute-start(bf16[192,640]{1,0:T(8,128)(2,1)S(1)} %slice.158), channel_id=1, source_target_pairs={{0,4},{1,5},{2,6},{3,7},{4,0},{5,1},{6,2},{7,3},{8,12},{9,13},{10,... | collective-permute-start | bytes 737288 | tf_op jit(solution)/shard_map/ppermute | solution.py:1094
  60.6 9.3 %collective-permute-start.9 = (bf16[192,1280]{1,0:T(8,128)(2,1)S(1)}, bf16[192,1280]{1,0:T(8,128)(2,1)S(1)}, u32[]{:S(2)}, u32[]{:S(2)}) collective-permute-start(bf16[192,1280]{1,0:T(8,128)(2,1)S(1)} %constant_dynamic-update-slice_fusion.refs_1_.refs_2_), channel_id=1, source_target_pairs={{0,1},{1,0},{2,3},{3,2},{4,5},{5,4},{6,7},{7,6},{8,9},{9,8},{10,11... | collective-permute-start | bytes 1474568 | tf_op jit(solution)/shard_map/ppermute | solution.py:1094
  66.7 3.3 collective-permute-start.11
  71.0 25.4 %collective-permute-start.20 = (bf16[192,1920]{1,0:T(8,128)(2,1)}, bf16[192,1920]{1,0:T(8,128)(2,1)}, u32[]{:S(2)}, u32[]{:S(2)}) collective-permute-start(bf16[192,1920]{1,0:T(8,128)(2,1)} %constant_dynamic-update-slice_fusion.5.refs_4_.refs_9_), channel_id=1, source_target_pairs={{0,1},{1,0},{2,3},{3,2},{4,5},{5,4},{6,7},{7,6},{8,9},{9,8},{10,11... | collective-permute-start | bytes 2211848 | tf_op jit(solution)/shard_map/ppermute | solution.py:1094
  71.8 24.6 %collective-permute-start.19 = (bf16[192,1920]{1,0:T(8,128)(2,1)}, bf16[192,1920]{1,0:T(8,128)(2,1)S(1)}, u32[]{:S(2)}, u32[]{:S(2)}) collective-permute-start(bf16[192,1920]{1,0:T(8,128)(2,1)} %constant_dynamic-update-slice_fusion.5.refs_4_.refs_9_), channel_id=1, source_target_pairs={{0,4},{1,5},{2,6},{3,7},{4,0},{5,1},{6,2},{7,3},{8,12},{9,13},{10,... | collective-permute-start | bytes 2211848 | tf_op jit(solution)/shard_map/ppermute | solution.py:1094
  72.4 24.0 %collective-permute-start.18 = (bf16[192,1920]{1,0:T(8,128)(2,1)}, bf16[192,1920]{1,0:T(8,128)(2,1)S(1)}, u32[]{:S(2)}, u32[]{:S(2)}) collective-permute-start(bf16[192,1920]{1,0:T(8,128)(2,1)} %constant_dynamic-update-slice_fusion.5.refs_4_.refs_9_), channel_id=1, source_target_pairs={{0,2},{1,3},{2,0},{3,1},{4,6},{5,7},{6,4},{7,5},{8,10},{9,11},{10,... | collective-permute-start | bytes 2211848 | tf_op jit(solution)/shard_map/ppermute | solution.py:1094
  96.5 9.8 %collective-permute-start.22 = (bf16[192,896]{1,0:T(8,128)(2,1)S(1)}, bf16[192,896]{1,0:T(8,128)(2,1)}, u32[]{:S(2)}, u32[]{:S(2)}) collective-permute-start(bf16[192,896]{1,0:T(8,128)(2,1)S(1)} %slice.122), channel_id=1, source_target_pairs={{0,2},{1,3},{2,0},{3,1},{4,6},{5,7},{6,4},{7,5},{8,10},{9,11},{10,... | collective-permute-start | bytes 1032200 | tf_op jit(solution)/shard_map/ppermute | solution.py:1094
  97.9 11.0 %collective-permute-start.21 = (bf16[192,1024]{1,0:T(8,128)(2,1)S(1)}, bf16[192,1024]{1,0:T(8,128)(2,1)}, u32[]{:S(2)}, u32[]{:S(2)}) collective-permute-start(bf16[192,1024]{1,0:T(8,128)(2,1)S(1)} %slice.121), channel_id=1, source_target_pairs={{0,4},{1,5},{2,6},{3,7},{4,0},{5,1},{6,2},{7,3},{8,12},{9,13},{10,... | collective-permute-start | bytes 1179656 | tf_op jit(solution)/shard_map/ppermute | solution.py:1094
  106.3 6.0 %collective-permute-start.23 = (bf16[192,1920]{1,0:T(8,128)(2,1)S(1)}, bf16[192,1920]{1,0:T(8,128)(2,1)S(1)}, u32[]{:S(2)}, u32[]{:S(2)}) collective-permute-start(bf16[192,1920]{1,0:T(8,128)(2,1)S(1)} %collective-permute-done.18.refs_5_.refs_10_), channel_id=1, source_target_pairs={{0,1},{1,0},{2,3},{3,2},{4,5},{5,4},{6,7},{7,6},{8,9},{9,8},{10,11... | collective-permute-start | bytes 2211848 | tf_op jit(solution)/shard_map/ppermute | solution.py:1094
  106.8 5.5 %collective-permute-start.24 = (bf16[192,1920]{1,0:T(8,128)(2,1)S(1)}, bf16[192,1920]{1,0:T(8,128)(2,1)}, u32[]{:S(2)}, u32[]{:S(2)}) collective-permute-start(bf16[192,1920]{1,0:T(8,128)(2,1)S(1)} %collective-permute-done.19.refs_6_.refs_11_), channel_id=1, source_target_pairs={{0,1},{1,0},{2,3},{3,2},{4,5},{5,4},{6,7},{7,6},{8,9},{9,8},{10,11... | collective-permute-start | bytes 2211848 | tf_op jit(solution)/shard_map/ppermute | solution.py:1094
  107.4 32.5 %collective-permute-start.27 = (bf16[6,128,768]{2,1,0:T(8,128)(2,1)}, bf16[6,128,768]{2,1,0:T(8,128)(2,1)S(1)}, u32[]{:S(2)}, u32[]{:S(2)}) collective-permute-start(bf16[6,128,768]{2,1,0:T(8,128)(2,1)} %get-tuple-element.177), channel_id=1, source_target_pairs={{0,2},{1,3},{2,0},{3,1},{4,6},{5,7},{6,4},{7,5},{8,10},{9,11},{10,... | collective-permute-start | bytes 3538952 | tf_op jit(solution)/shard_map/ppermute | solution.py:1271
  108.9 38.8 %collective-permute-start.28 = (bf16[6,128,768]{2,1,0:T(8,128)(2,1)}, bf16[6,128,768]{2,1,0:T(8,128)(2,1)}, u32[]{:S(2)}, u32[]{:S(2)}) collective-permute-start(bf16[6,128,768]{2,1,0:T(8,128)(2,1)} %get-tuple-element.178), channel_id=1, source_target_pairs={{0,3},{1,0},{2,1},{3,2},{4,7},{5,4},{6,5},{7,6},{8,11},{9,8},{10,9... | collective-permute-start | bytes 3538952 | tf_op jit(solution)/shard_map/ppermute | solution.py:1271
  109.4 3.4 collective-permute-start.25
  202.4 60.8 %collective-permute-start.29 = (bf16[6,128,768]{2,1,0:T(8,128)(2,1)}, bf16[6,128,768]{2,1,0:T(8,128)(2,1)S(1)}, u32[]{:S(2)}, u32[]{:S(2)}) collective-permute-start(bf16[6,128,768]{2,1,0:T(8,128)(2,1)} %get-tuple-element.201), channel_id=1, source_target_pairs={{0,1},{1,2},{2,3},{3,0},{4,5},{5,6},{6,7},{7,4},{8,9},{9,10},{10,1... | collective-permute-start | bytes 3538952 | tf_op jit(solution)/shard_map/ppermute | solution.py:1271
  203.3 60.0 %collective-permute-start.30 = (bf16[6,128,768]{2,1,0:T(8,128)(2,1)}, bf16[6,128,768]{2,1,0:T(8,128)(2,1)}, u32[]{:S(2)}, u32[]{:S(2)}) collective-permute-start(bf16[6,128,768]{2,1,0:T(8,128)(2,1)} %get-tuple-element.202), channel_id=1, source_target_pairs={{0,2},{1,3},{2,0},{3,1},{4,6},{5,7},{6,4},{7,5},{8,10},{9,11},{10,... | collective-permute-start | bytes 3538952 | tf_op jit(solution)/shard_map/ppermute | solution.py:1271
  204.7 58.5 %collective-permute-start.31 = (bf16[6,128,768]{2,1,0:T(8,128)(2,1)}, bf16[6,128,768]{2,1,0:T(8,128)(2,1)}, u32[]{:S(2)}, u32[]{:S(2)}) collective-permute-start(bf16[6,128,768]{2,1,0:T(8,128)(2,1)} %get-tuple-element.203), channel_id=1, source_target_pairs={{0,3},{1,0},{2,1},{3,2},{4,7},{5,4},{6,5},{7,6},{8,11},{9,8},{10,9... | collective-permute-start | bytes 3538952 | tf_op jit(solution)/shard_map/ppermute | solution.py:1271
  263.3 7.3 %collective-permute-start.33 = (bf16[768,1536]{1,0:T(8,128)(2,1)}, bf16[768,1536]{1,0:T(8,128)(2,1)}, u32[]{:S(2)}, u32[]{:S(2)}) collective-permute-start(bf16[768,1536]{1,0:T(8,128)(2,1)} %get-tuple-element.208), channel_id=1, source_target_pairs={{0,1},{1,0},{2,3},{3,2},{4,5},{5,4},{6,7},{7,6},{8,9},{9,8},{10,11... | collective-permute-start | bytes 7077896 | tf_op jit(solution)/shard_map/ppermute | solution.py:1094
  263.8 5.3 %collective-permute-start.32 = (bf16[768,384]{1,0:T(8,128)(2,1)}, bf16[768,384]{1,0:T(8,128)(2,1)}, u32[]{:S(2)}, u32[]{:S(2)}) collective-permute-start(bf16[768,384]{1,0:T(8,128)(2,1)} %get-tuple-element.206), channel_id=1, source_target_pairs={{0,1},{1,0},{2,3},{3,2},{4,5},{5,4},{6,7},{7,6},{8,9},{9,8},{10,11... | collective-permute-start | bytes 1769480 | tf_op jit(solution)/shard_map/ppermute | solution.py:1094
  276.2 26.3 %collective-permute-start.34 = (bf16[4,2,48,1024]{3,2,0,1:T(8,128)(2,1)S(1)}, bf16[4,2,48,1024]{3,2,0,1:T(8,128)(2,1)}, u32[]{:S(2)}, u32[]{:S(2)}) collective-permute-start(bf16[4,2,48,1024]{3,2,0,1:T(8,128)(2,1)S(1)} %fusion.4), channel_id=1, source_target_pairs={{0,4},{1,5},{2,6},{3,7},{4,0},{5,1},{6,2},{7,3},{8,12},{9,13},{10,... | collective-permute-start | bytes 2359304 | tf_op jit(solution)/shard_map/ppermute | solution.py:1094
  277.7 24.8 %collective-permute-start.35 = (bf16[2,4,48,896]{3,2,1,0:T(8,128)(2,1)}, bf16[2,4,48,896]{3,2,1,0:T(8,128)(2,1)}, u32[]{:S(2)}, u32[]{:S(2)}) collective-permute-start(bf16[2,4,48,896]{3,2,1,0:T(8,128)(2,1)} %fusion.5), channel_id=1, source_target_pairs={{0,2},{1,3},{2,0},{3,1},{4,6},{5,7},{6,4},{7,5},{8,10},{9,11},{10,... | collective-permute-start | bytes 2064392 | tf_op jit(solution)/shard_map/ppermute | solution.py:1094
  304.9 24.3 %collective-permute-start.37 = (bf16[4,48,896]{2,1,0:T(8,128)(2,1)S(1)}, bf16[4,48,896]{2,1,0:T(8,128)(2,1)S(1)}, u32[]{:S(2)}, u32[]{:S(2)}) collective-permute-start(bf16[4,48,896]{2,1,0:T(8,128)(2,1)S(1)} %fusion.16), channel_id=1, source_target_pairs={{0,4},{1,5},{2,6},{3,7},{4,0},{5,1},{6,2},{7,3},{8,12},{9,13},{10,... | collective-permute-start | bytes 1032200 | tf_op jit(solution)/shard_map/ppermute | solution.py:1094
  308.1 21.1 %collective-permute-start.36 = (bf16[4,48,1024]{2,1,0:T(8,128)(2,1)S(1)}, bf16[4,48,1024]{2,1,0:T(8,128)(2,1)S(1)}, u32[]{:S(2)}, u32[]{:S(2)}) collective-permute-start(bf16[4,48,1024]{2,1,0:T(8,128)(2,1)S(1)} %fusion.10), channel_id=1, source_target_pairs={{0,2},{1,3},{2,0},{3,1},{4,6},{5,7},{6,4},{7,5},{8,10},{9,11},{10,... | collective-permute-start | bytes 1179656 | tf_op jit(solution)/shard_map/ppermute | solution.py:1094
  329.2 9.7 %collective-permute-start.38 = (bf16[768,1152]{1,0:T(8,128)(2,1)}, bf16[768,1152]{1,0:T(8,128)(2,1)}, u32[]{:S(2)}, u32[]{:S(2)}) collective-permute-start(bf16[768,1152]{1,0:T(8,128)(2,1)} %get-tuple-element.238), channel_id=1, source_target_pairs={{0,1},{1,0},{2,3},{3,2},{4,5},{5,4},{6,7},{7,6},{8,9},{9,8},{10,11... | collective-permute-start | bytes 5308424 | tf_op jit(solution)/shard_map/ppermute | solution.py:1094
  331.8 6.4 %collective-permute-start.39 = (bf16[768,128]{1,0:T(8,128)(2,1)}, bf16[768,128]{1,0:T(8,128)(2,1)S(1)}, u32[]{:S(2)}, u32[]{:S(2)}) collective-permute-start(bf16[768,128]{1,0:T(8,128)(2,1)} %get-tuple-element.240), channel_id=1, source_target_pairs={{0,1},{1,0},{2,3},{3,2},{4,5},{5,4},{6,7},{7,6},{8,9},{9,8},{10,11... | collective-permute-start | bytes 589832 | tf_op jit(solution)/shard_map/ppermute | solution.py:1094
  345.3 24.1 %collective-permute-start.40 = (bf16[4,2,48,640]{3,2,0,1:T(8,128)(2,1)}, bf16[4,2,48,640]{3,2,0,1:T(8,128)(2,1)}, u32[]{:S(2)}, u32[]{:S(2)}) collective-permute-start(bf16[4,2,48,640]{3,2,0,1:T(8,128)(2,1)} %fusion.8), channel_id=1, source_target_pairs={{0,4},{1,5},{2,6},{3,7},{4,0},{5,1},{6,2},{7,3},{8,12},{9,13},{10,... | collective-permute-start | bytes 1474568 | tf_op jit(solution)/shard_map/ppermute | solution.py:1094
  347.0 22.4 %collective-permute-start.41 = (bf16[2,4,48,640]{3,2,1,0:T(8,128)(2,1)}, bf16[2,4,48,640]{3,2,1,0:T(8,128)(2,1)}, u32[]{:S(2)}, u32[]{:S(2)}) collective-permute-start(bf16[2,4,48,640]{3,2,1,0:T(8,128)(2,1)} %fusion.7), channel_id=1, source_target_pairs={{0,2},{1,3},{2,0},{3,1},{4,6},{5,7},{6,4},{7,5},{8,10},{9,11},{10,... | collective-permute-start | bytes 1474568 | tf_op jit(solution)/shard_map/ppermute | solution.py:1094
  348.5 20.9 %collective-permute-start.44 = (bf16[48,1920]{1,0:T(8,128)(2,1)}, bf16[48,1920]{1,0:T(8,128)(2,1)S(1)}, u32[]{:S(2)}, u32[]{:S(2)}) collective-permute-start(bf16[48,1920]{1,0:T(8,128)(2,1)} %get-tuple-element.287), channel_id=1, source_target_pairs={{0,24},{1,25},{2,26},{3,27},{4,28},{5,29},{6,30},{7,31},{8,0},{9,1... | collective-permute-start | bytes 552968 | tf_op jit(solution)/shard_map/ppermute | solution.py:1094
  351.9 17.5 %collective-permute-start.43 = (bf16[48,1920]{1,0:T(8,128)(2,1)}, bf16[48,1920]{1,0:T(8,128)(2,1)}, u32[]{:S(2)}, u32[]{:S(2)}) collective-permute-start(bf16[48,1920]{1,0:T(8,128)(2,1)} %get-tuple-element.288), channel_id=1, source_target_pairs={{0,16},{1,17},{2,18},{3,19},{4,20},{5,21},{6,22},{7,23},{8,24},{9,... | collective-permute-start | bytes 552968 | tf_op jit(solution)/shard_map/ppermute | solution.py:1094
  351.9 17.5 %collective-permute-start.42 = (bf16[48,1920]{1,0:T(8,128)(2,1)}, bf16[48,1920]{1,0:T(8,128)(2,1)}, u32[]{:S(2)}, u32[]{:S(2)}) collective-permute-start(bf16[48,1920]{1,0:T(8,128)(2,1)} %get-tuple-element.289), channel_id=1, source_target_pairs={{0,8},{1,9},{2,10},{3,11},{4,12},{5,13},{6,14},{7,15},{8,16},{9,17... | collective-permute-start | bytes 552968 | tf_op jit(solution)/shard_map/ppermute | solution.py:1094
  373.4 8.4 %collective-permute-start.46 = (bf16[4,48,640]{2,1,0:T(8,128)(2,1)S(1)}, bf16[4,48,640]{2,1,0:T(8,128)(2,1)S(1)}, u32[]{:S(2)}, u32[]{:S(2)}) collective-permute-start(bf16[4,48,640]{2,1,0:T(8,128)(2,1)S(1)} %fusion.18), channel_id=1, source_target_pairs={{0,4},{1,5},{2,6},{3,7},{4,0},{5,1},{6,2},{7,3},{8,12},{9,13},{10,... | collective-permute-start | bytes 737288 | tf_op jit(solution)/shard_map/ppermute | solution.py:1094
  374.6 8.1 %collective-permute-start.45 = (bf16[4,48,640]{2,1,0:T(8,128)(2,1)S(1)}, bf16[4,48,640]{2,1,0:T(8,128)(2,1)S(1)}, u32[]{:S(2)}, u32[]{:S(2)}) collective-permute-start(bf16[4,48,640]{2,1,0:T(8,128)(2,1)S(1)} %fusion.17), channel_id=1, source_target_pairs={{0,2},{1,3},{2,0},{3,1},{4,6},{5,7},{6,4},{7,5},{8,10},{9,11},{10,... | collective-permute-start | bytes 737288 | tf_op jit(solution)/shard_map/ppermute | solution.py:1094
  382.8 8.2 %collective-permute-start.47 = (bf16[48,1280]{1,0:T(8,128)(2,1)S(1)}, bf16[48,1280]{1,0:T(8,128)(2,1)S(1)}, u32[]{:S(2)}, u32[]{:S(2)}) collective-permute-start(bf16[48,1280]{1,0:T(8,128)(2,1)S(1)} %get-tuple-element.290), channel_id=1, source_target_pairs={{0,8},{1,9},{2,10},{3,11},{4,12},{5,13},{6,14},{7,15},{8,16},{9,17... | collective-permute-start | bytes 368648 | tf_op jit(solution)/shard_map/ppermute | solution.py:1094
  385.1 6.9 %collective-permute-start.49 = (bf16[48,1280]{1,0:T(8,128)(2,1)S(1)}, bf16[48,1280]{1,0:T(8,128)(2,1)S(1)}, u32[]{:S(2)}, u32[]{:S(2)}) collective-permute-start(bf16[48,1280]{1,0:T(8,128)(2,1)S(1)} %get-tuple-element.291), channel_id=1, source_target_pairs={{0,24},{1,25},{2,26},{3,27},{4,28},{5,29},{6,30},{7,31},{8,0},{9,1... | collective-permute-start | bytes 368648 | tf_op jit(solution)/shard_map/ppermute | solution.py:1094
  386.7 10.4 %collective-permute-start.48 = (bf16[48,1280]{1,0:T(8,128)(2,1)S(1)}, bf16[48,1280]{1,0:T(8,128)(2,1)S(1)}, u32[]{:S(2)}, u32[]{:S(2)}) collective-permute-start(bf16[48,1280]{1,0:T(8,128)(2,1)S(1)} %get-tuple-element.292), channel_id=1, source_target_pairs={{0,16},{1,17},{2,18},{3,19},{4,20},{5,21},{6,22},{7,23},{8,24},{9,... | collective-permute-start | bytes 368648 | tf_op jit(solution)/shard_map/ppermute | solution.py:1094
  (42 other events, 390.2 us)
Sparse Core Ops, SparseCore 0:
  10.9 84.0 all-gather.1
  205.1 111.8 reduce-scatter.1

commit v3 on v2

--- a/solution.py
+++ b/solution.py
@@ -322,10 +322,14 @@
     )(lens, here, rows, *pieces)
 
 
+def first_rows(normed, vec):
+    return normed.astype(F32) * vec[G1 : G1 + 1] + vec[S1 : S1 + 1]
+
+
 def up_kernel(here, *refs, copies, size, chunk):
     mixed_ref, x_ref, vec_ref, ub_ref = refs[:4]
-    pieces = refs[4:-7]
-    norm_ref, factor_ref, low_ref, act_ref, slope_ref, w_ref, sem = refs[-7:]
+    pieces = refs[4:-6]
+    norm_ref, factor_ref, act_ref, slope_ref, w_ref, sem = refs[-6:]
     width = x_ref.shape[1]
 
     @pl.when(pl.program_id(0) == 0)
@@ -337,8 +341,7 @@
     normed, factor = layer_norm(total)
     norm_ref[...] = normed
     factor_ref[...] = jnp.broadcast_to(factor, factor_ref.shape)
-    low_ref[...] = (normed * vec[G1 : G1 + 1] + vec[S1 : S1 + 1]).astype(BF16)
-    low = low_ref[...]
+    low = first_rows(norm_ref[...], vec).astype(BF16)
     for begin in range(0, act_ref.shape[1], chunk):
         at = slice(begin, begin + chunk)
         for first in range(0, low.shape[0], 128):
@@ -369,7 +372,6 @@
             out_specs=[
                 rows_spec(block, width),
                 rows_spec(block, 128),
-                rows_spec(block, width),
                 rows_spec(block, ff),
                 rows_spec(block, ff),
             ],
@@ -381,7 +383,6 @@
         out_shape=[
             jax.ShapeDtypeStruct((count, width), F32),
             jax.ShapeDtypeStruct((count, 128), F32),
-            jax.ShapeDtypeStruct((count, width), BF16),
             jax.ShapeDtypeStruct((count, ff), BF16),
             jax.ShapeDtypeStruct((count, ff), BF16),
         ],
@@ -393,8 +394,9 @@
 
 def down_kernel(lens, alive, *refs, seq, steps, tile):
     act_hbm, norm_ref, cot_ref, lg_ref, wd_ref, vec_ref, ws_ref, sv_ref, pw_ref, cw_ref = refs[:10]
-    second_ref, sum_ref, dcot_ref, logits_ref, vgrad_ref, sgrad_ref = refs[10:16]
-    wsgrad_ref, pwgrad_ref, cwgrad_ref, grad_ref, act_all, turned, sem = refs[16:]
+    second_ref, dcot_ref, logits_ref, vgrad_ref, sgrad_ref = refs[10:15]
+    wsgrad_ref, pwgrad_ref, cwgrad_ref, grad_ref, act_all, turned = refs[15:21]
+    held, sem = refs[21:25], refs[25]
     step = pl.program_id(0)
     rows = norm_ref.shape[0]
 
@@ -405,6 +407,8 @@
     @pl.when(step == 0)
     def _():
         load(0).start()
+        for total_ref in (vgrad_ref, sgrad_ref, wsgrad_ref, pwgrad_ref, cwgrad_ref):
+            total_ref[...] = jnp.zeros_like(total_ref)
 
     @pl.when(step + 1 < steps)
     def _():
@@ -418,8 +422,9 @@
             lens,
             alive,
             (act_all.at[at], norm_ref, cot_ref, lg_ref, wd_ref, vec_ref, ws_ref, sv_ref, pw_ref, cw_ref),
-            (second_ref, sum_ref, dcot_ref, logits_ref, vgrad_ref, sgrad_ref),
+            (second_ref, dcot_ref, logits_ref, vgrad_ref, sgrad_ref),
             (wsgrad_ref, pwgrad_ref, cwgrad_ref),
+            held,
             seq,
         )
         turned[:, at] = dcot_ref[...].T
@@ -430,10 +435,18 @@
         grad_ref[...] = dot(turned[...], act_all[:, at]).astype(BF16).T
 
 
-def down_rows(lens, alive, ins, outs, sums, seq):
+SLICE = 32
+
+
+def fold(matrix):
+    return jnp.sum(matrix.reshape(matrix.shape[0] // 8, 8, matrix.shape[1]), axis=0)
+
+
+def down_rows(lens, alive, ins, outs, sums, held, seq):
     act_ref, norm_ref, cot_ref, lg_ref, wd_ref, vec_ref, ws_ref, sv_ref, pw_ref, cw_ref = ins
-    second_ref, sum_ref, dcot_ref, logits_ref, vgrad_ref, sgrad_ref = outs
+    second_ref, dcot_ref, logits_ref, vgrad_ref, sgrad_ref = outs
     wsgrad_ref, pwgrad_ref, cwgrad_ref = sums
+    wide_ref, back_ref, factor_ref, low_ref = held
     step = pl.program_id(0)
     rows = norm_ref.shape[0]
     samples = rows // seq
@@ -443,18 +456,15 @@
     pool_width = stu // STU_HEADS
     pool_scale = 1.0 / math.sqrt(pool_width)
 
-    @pl.when(step == 0)
-    def _():
-        vgrad_ref[...] = jnp.zeros_like(vgrad_ref)
-        sgrad_ref[...] = jnp.zeros_like(sgrad_ref)
-        wsgrad_ref[...] = jnp.zeros_like(wsgrad_ref)
-        pwgrad_ref[...] = jnp.zeros_like(pwgrad_ref)
-        cwgrad_ref[...] = jnp.zeros_like(cwgrad_ref)
-
-    first = norm_ref[...] * vec[G1 : G1 + 1] + vec[S1 : S1 + 1]
-    down = dot(act_ref[...], wd_ref[...]) + vec[DB : DB + 1]
-    normed, factor = layer_norm(first + down)
-    second = (normed * vec[G2 : G2 + 1] + vec[S2 : S2 + 1]).astype(BF16)
+    wide_ref[...] = dot(act_ref[...], wd_ref[...])
+    for begin in range(0, rows, SLICE):
+        at = slice(begin, begin + SLICE)
+        first = first_rows(norm_ref[at], vec)
+        normed, factor = layer_norm(first + wide_ref[at] + vec[DB : DB + 1])
+        wide_ref[at] = normed
+        factor_ref[at] = jnp.broadcast_to(factor, (SLICE, 128))
+        low_ref[at] = (normed * vec[G2 : G2 + 1] + vec[S2 : S2 + 1]).astype(BF16)
+    second = low_ref[...]
     reduced = (dot(second, ws_ref[...]) + sv[0:1]).astype(BF16)
     head_of = lax.broadcasted_iota(jnp.int32, (stu, stu), 0) // pool_width
     same = head_of == lax.broadcasted_iota(jnp.int32, (stu, stu), 1) // pool_width
@@ -462,16 +472,16 @@
     query_table = jnp.where(same, jnp.broadcast_to(pool_query, (stu, stu)), 0.0).astype(BF16)
     scores = dot_nt(reduced, query_table) * pool_scale
     place = lax.broadcasted_iota(jnp.int32, (seq, stu), 0)
-    shares = []
-    pooled_rows = []
-    for s in range(samples):
-        at = slice(s * seq, (s + 1) * seq)
-        part = jnp.where(place < lens[step * samples + s], scores[at], MASKED)
-        raised = jnp.exp(part - jnp.max(part, axis=0, keepdims=True))
-        share = raised / jnp.sum(raised, axis=0, keepdims=True)
-        shares.append(share)
-        pooled_rows.append(column_sum(share * reduced[at].astype(F32)))
-    pooled = stack_rows(pooled_rows, 8).astype(BF16)
+    cuts = [slice(s * seq, (s + 1) * seq) for s in range(samples)]
+    wides = [reduced[at].astype(F32) for at in cuts]
+    shares = [
+        jnp.where(place < lens[step * samples + s], scores[at], MASKED) for s, at in enumerate(cuts)
+    ]
+    peaks = [jnp.max(part, axis=0, keepdims=True) for part in shares]
+    shares = [jnp.exp(part - peak) for part, peak in zip(shares, peaks)]
+    sums_of = [column_sum(part) for part in shares]
+    shares = [part / total for part, total in zip(shares, sums_of)]
+    pooled = stack_rows([column_sum(p * w) for p, w in zip(shares, wides)], 8).astype(BF16)
     squashed = jnp.tanh(dot(pooled, pw_ref[...]) + sv[2:3])
     squashed_low = squashed.astype(BF16)
     logits_ref[...] = dot(squashed_low, cw_ref[...])
@@ -480,18 +490,22 @@
     hidden_cot = (dot_nt(lg, cw_ref[...]) * (1.0 - squashed * squashed)).astype(BF16)
     pwgrad_ref[...] += dot_tn(pooled, hidden_cot)
     pooled_cot = dot_nt(hidden_cot, pw_ref[...]).astype(BF16).astype(F32)
-    query_grad = jnp.zeros((1, stu), F32)
-    cots = []
-    for s in range(samples):
-        at = slice(s * seq, (s + 1) * seq)
-        row = pooled_cot[s : s + 1]
-        table = jnp.where(same, jnp.broadcast_to(row, (stu, stu)), 0.0).astype(BF16)
-        share_cot = dot_nt(reduced[at], table)
-        share = shares[s]
-        score_cot = share * (share_cot - column_sum(share * share_cot))
-        query_grad += column_sum(score_cot * reduced[at].astype(F32)) * pool_scale
-        cots.append((share * row + score_cot * (pool_query * pool_scale)).astype(BF16))
-    reduced_cot = jnp.concatenate(cots, axis=0)
+    lines = [pooled_cot[s : s + 1] for s in range(samples)]
+    tables = [
+        jnp.where(same, jnp.broadcast_to(row, (stu, stu)), 0.0).astype(BF16) for row in lines
+    ]
+    share_cots = [dot_nt(reduced[at], table) for at, table in zip(cuts, tables)]
+    inner = [column_sum(p * c) for p, c in zip(shares, share_cots)]
+    score_cots = [p * (c - i) for p, c, i in zip(shares, share_cots, inner)]
+    query_grad = sum(column_sum(c * w) for c, w in zip(score_cots, wides)) * pool_scale
+    scaled_query = pool_query * pool_scale
+    reduced_cot = jnp.concatenate(
+        [
+            (p * row + c * scaled_query).astype(BF16)
+            for p, row, c in zip(shares, lines, score_cots)
+        ],
+        axis=0,
+    )
     sgrad_ref[...] += stack_rows(
         [
             column_sum(reduced_cot.astype(F32)),
@@ -501,21 +515,22 @@
         8,
     )
     wsgrad_ref[...] += dot_tn(reduced_cot, second)
-    back = dot_nt(reduced_cot, ws_ref[...])
-    parts = []
-    for s in range(samples):
-        at = slice(s * seq, (s + 1) * seq)
-        live = alive[step * samples + s] > 0
-        parts.append(back[at] + jnp.where(live, cot_ref[at].astype(F32), 0.0))
-        second_ref[at] = jnp.where(live, second[at], jnp.zeros_like(second[at]))
-    total = jnp.concatenate(parts, axis=0)
-    sum_cot = layer_norm_back(total, vec[G2 : G2 + 1], normed, factor)
-    sum_ref[...] = sum_cot
-    down_cot = sum_cot.astype(BF16)
-    dcot_ref[...] = down_cot
-    vgrad_ref[...] += stack_rows(
-        [column_sum(total * normed), column_sum(total), column_sum(down_cot.astype(F32))], 8
-    )
+    back_ref[...] = dot_nt(reduced_cot, ws_ref[...])
+    gain_sum = jnp.zeros((8, vec.shape[1]), F32)
+    shift_sum, bias_sum = gain_sum, gain_sum
+    for begin in range(0, rows, SLICE):
+        at = slice(begin, begin + SLICE)
+        live = alive[step * samples + begin // seq] > 0
+        total = back_ref[at] + jnp.where(live, cot_ref[at].astype(F32), 0.0)
+        low = low_ref[at]
+        second_ref[at] = jnp.where(live, low, jnp.zeros_like(low))
+        normed = wide_ref[at]
+        sum_cot = layer_norm_back(total, vec[G2 : G2 + 1], normed, factor_ref[at, 0:1])
+        dcot_ref[at] = sum_cot.astype(BF16)
+        gain_sum += fold(total * normed)
+        shift_sum += fold(total)
+        bias_sum += fold(sum_cot)
+    vgrad_ref[...] += stack_rows([column_sum(p) for p in (gain_sum, shift_sum, bias_sum)], 8)
 
 
 def down_part(lens, alive, act, normed, cot, lg, wd, vec, ws, sv, pw, cw, seq, block, tile):
@@ -547,7 +562,6 @@
             out_specs=[
                 block_rows(block, width),
                 block_rows(block, width),
-                block_rows(block, width),
                 block_rows(8, 128),
                 kept((8, width)),
                 kept((8, stu)),
@@ -559,12 +573,15 @@
             scratch_shapes=[
                 pltpu.VMEM((count, ff), BF16),
                 pltpu.VMEM((width, count), BF16),
+                pltpu.VMEM((block, width), F32),
+                pltpu.VMEM((block, width), F32),
+                pltpu.VMEM((block, 128), F32),
+                pltpu.VMEM((block, width), BF16),
                 pltpu.SemaphoreType.DMA((steps,)),
             ],
         ),
         out_shape=[
             jax.ShapeDtypeStruct((count, width), BF16),
-            jax.ShapeDtypeStruct((count, width), F32),
             jax.ShapeDtypeStruct((count, width), BF16),
             jax.ShapeDtypeStruct((steps * 8, 128), F32),
             jax.ShapeDtypeStruct((8, width), F32),
@@ -588,11 +605,11 @@
 
 
 def up_back_kernel(here, *refs, copies, size, steps, chunk, tile):
-    dcot_ref, slope_ref, sum_ref, norm_ref, factor_ref, low_ref, mixed_ref, wd_ref, vec_ref = refs[:9]
-    pieces = refs[9:-15]
-    one_ref, mcot_ref, vgrad_ref, ugrad_ref = refs[-15:-11]
-    up_other, up_mine, out_other, out_mine = refs[-11:-7]
-    w_ref, ucot_all, acot_all, low_turned, mixed_turned, held, sem = refs[-7:]
+    dcot_ref, slope_ref, norm_ref, factor_ref, mixed_ref, wd_ref, vec_ref = refs[:7]
+    pieces = refs[7:-16]
+    one_ref, mcot_ref, vgrad_ref, ugrad_ref = refs[-16:-12]
+    up_other, up_mine, out_other, out_mine = refs[-12:-8]
+    w_ref, ucot_all, acot_all, low_turned, mixed_turned, held, back_ref, sem = refs[-8:]
     step = pl.program_id(0)
     rows, width = dcot_ref.shape
     ff = slope_ref.shape[1]
@@ -615,18 +632,23 @@
             up_cot = dot_nt(down_cot, wd_ref[at, :]) * slope_ref[:, at].astype(F32)
             ugrad_ref[0:1, at] += column_sum(up_cot)
             ucot_all[at_rows, at] = up_cot.astype(BF16)
-        turn_lines(low_ref[...], lines, held, low_turned, at_rows)
+        turn_lines(first_rows(norm_ref[...], vec).astype(BF16), lines, held, low_turned, at_rows)
         turn_lines(mixed_ref[...], lines, held, mixed_turned, at_rows)
-        cot = sum_ref[...] + dot_nt(ucot_all[at_rows, :], w_ref[:, width:])
-        normed = norm_ref[...]
-        one_cot = layer_norm_back(cot, vec[G1 : G1 + 1], normed, factor_ref[:, 0:1])
-        one_ref[...] = one_cot
-        low = one_cot.astype(BF16)
-        acot_all[at_rows, :] = low
-        mcot_ref[...] = dot_nt(low, w_ref[:, :width]).astype(BF16)
-        vgrad_ref[...] += stack_rows(
-            [column_sum(cot * normed), column_sum(cot), column_sum(one_cot)], 8
-        )
+        back_ref[...] = dot_nt(ucot_all[at_rows, :], w_ref[:, width:])
+        gain_sum = jnp.zeros((8, width), F32)
+        shift_sum, bias_sum = gain_sum, gain_sum
+        for begin in range(0, rows, SLICE):
+            at = slice(begin, begin + SLICE)
+            cot = dcot_ref[at].astype(F32) + back_ref[at]
+            normed = norm_ref[at].astype(F32)
+            one_cot = layer_norm_back(cot, vec[G1 : G1 + 1], normed, factor_ref[at, 0:1])
+            one_ref[at] = one_cot.astype(BF16)
+            gain_sum += fold(cot * normed)
+            shift_sum += fold(cot)
+            bias_sum += fold(one_cot)
+        acot_all[at_rows, :] = one_ref[...]
+        mcot_ref[...] = dot_nt(one_ref[...], w_ref[:, :width]).astype(BF16)
+        vgrad_ref[...] += stack_rows([column_sum(p) for p in (gain_sum, shift_sum, bias_sum)], 8)
 
     per = ff // 2 // tile
 
@@ -652,7 +674,7 @@
         up_mine[...] = up_tile(step - steps - per - 1, core).astype(BF16)
 
 
-def up_back(gather, dcot, slope, sum_two, normed, factor, low, mixed, wd, vec, block, tile):
+def up_back(gather, dcot, slope, normed, factor, mixed, wd, vec, block, tile):
     copies, here, size = gather.plan(), gather.grid.here, gather.grid.size
     pieces = gather.parts
     count, width = dcot.shape
@@ -679,9 +701,7 @@
                 block_rows(width),
                 block_rows(ff),
                 block_rows(width),
-                block_rows(width),
                 block_rows(128),
-                block_rows(width),
                 block_rows(width),
                 whole(wd.shape),
                 whole(vec.shape),
@@ -704,11 +724,12 @@
                 pltpu.VMEM((width, count), BF16),
                 pltpu.VMEM((width, count), BF16),
                 pltpu.VMEM((width, block), BF16),
+                pltpu.VMEM((block, width), F32),
                 pltpu.SemaphoreType.DMA((len(copies),)),
             ],
         ),
         out_shape=[
-            jax.ShapeDtypeStruct((count, width), F32),
+            jax.ShapeDtypeStruct((count, width), BF16),
             jax.ShapeDtypeStruct((count, width), BF16),
             jax.ShapeDtypeStruct((8, width), F32),
             jax.ShapeDtypeStruct((8, ff), F32),
@@ -720,7 +741,7 @@
         compiler_params=params(),
         cost_estimate=cost(2 * count * width * ff * 4, 60e6),
         name="up_back",
-    )(here, dcot, slope, sum_two, normed, factor, low, mixed, wd, vec, *pieces)
+    )(here, dcot, slope, normed, factor, mixed, wd, vec, *pieces)
 
 
 def attend_back_kernel(mcot_ref, qkv_ref, prob_ref, pcot_ref, vgrad_ref, *, seq, width):
@@ -785,22 +806,32 @@
 
     for s in range(rows // seq):
         at = slice(s * seq, (s + 1) * seq)
-        for pair in range(width // 128):
-            low = pair * 128
-            q = split(qkv_ref[at, low : low + 128])
-            k = qkv_ref[at, width + low : width + low + 128]
-            v = qkv_ref[at, 2 * width + low : 2 * width + low + 128]
-            cot = split(mcot_ref[at, low : low + 128])
-            share = prob_ref[s, pair]
-            share_cot = dot_nt(v, cot)
-            pcot_ref[at, 2 * width + low : 2 * width + low + 128] = dot(share, cot).astype(BF16)
-            wide = share.astype(F32)
+        lows = range(0, width, 128)
+        cots = [split(mcot_ref[at, low : low + 128]) for low in lows]
+        share_cots = [
+            dot_nt(qkv_ref[at, 2 * width + low : 2 * width + low + 128], cot)
+            for low, cot in zip(lows, cots)
+        ]
+        values = [dot(prob_ref[s, n], cot) for n, cot in enumerate(cots)]
+        for low, value in zip(lows, values):
+            pcot_ref[at, 2 * width + low : 2 * width + low + 128] = value.astype(BF16)
+        score_cots = []
+        for n, share_cot in enumerate(share_cots):
+            wide = prob_ref[s, n].astype(F32)
             product = wide * share_cot
-            score_cot = (product - wide * column_sum(product)).astype(BF16)
-            pcot_ref[at, width + low : width + low + 128] = (dot(score_cot, q) * scale).astype(BF16)
-            query_cot = dot_tn(score_cot, k) * scale
+            score_cots.append((product - wide * column_sum(product)).astype(BF16))
+        keys = [
+            dot(score, split(qkv_ref[at, low : low + 128])) * scale
+            for low, score in zip(lows, score_cots)
+        ]
+        queries = [
+            dot_tn(score, qkv_ref[at, width + low : width + low + 128]) * scale
+            for low, score in zip(lows, score_cots)
+        ]
+        for low, key, query in zip(lows, keys, queries):
+            pcot_ref[at, width + low : width + low + 128] = key.astype(BF16)
             pcot_ref[at, low : low + 128] = jnp.where(
-                first_head, query_cot[:seq], query_cot[seq:]
+                first_head, query[:seq], query[seq:]
             ).astype(BF16)
     vgrad_ref[...] += stack_rows(
         [
@@ -848,7 +879,7 @@
     half = w_ref.shape[1] // 2
     cut = half - 128
     out_ref[...] = (
-        one_ref[...]
+        one_ref[...].astype(F32)
         + dot_nt(pcot_ref[:, :cut], w_ref[:, :cut])
         + dot_nt(pcot_ref[:, cut:], w_ref[:, half : half + cut])
     )
@@ -1118,14 +1149,22 @@
         self.plain = grid.plain
         self.parts = []
 
+    def chips(self):
+        if not self.plain:
+            grid = self.grid
+            self.chip = grid.ordered([self.mine, grid.send(self.other, "c", 1)], "c")
+
     def along_z(self):
         grid = self.grid
         if self.plain:
             shard = jnp.concatenate([self.mine, self.other], axis=1)
             self.parts = [lax.all_gather(shard, AXES, axis=0, tiled=True)]
             return
-        chip = grid.ordered([self.mine, grid.send(self.other, "c", 1)], "c")
-        self.stack = jnp.concatenate(grid.spread(chip, "z"), axis=0)
+        self.line = grid.spread(self.chip, "z")
+
+    def stack_z(self):
+        if not self.plain:
+            self.stack = jnp.concatenate(self.line, axis=0)
 
     def along_xy(self):
         if not self.plain:
@@ -1243,10 +1282,13 @@
         grid = self.grid
         one, two = add(self.keep_one, *self.in_one), add(self.keep_two, *self.in_two)
         self.keep_one, self.keep_two = self.line(one, 0, 1), two[0]
-        self.in_one = [
-            grid.send(self.line(one, o, 1).astype(BF16), "x", o) for o in range(1, grid.size["x"])
-        ]
-        self.in_two = [grid.send(two[o].astype(BF16), "y", o) for o in range(1, grid.size["y"])]
+        self.out_one = [self.line(one, o, 1).astype(BF16) for o in range(1, grid.size["x"])]
+        self.out_two = [two[o].astype(BF16) for o in range(1, grid.size["y"])]
+
+    def second_sends(self):
+        grid = self.grid
+        self.in_one = [grid.send(p, "x", o + 1) for o, p in enumerate(self.out_one)]
+        self.in_two = [grid.send(p, "y", o + 1) for o, p in enumerate(self.out_two)]
 
     def third(self):
         grid = self.grid
@@ -1337,25 +1379,32 @@
         (student_bias, pool_query, pool_bias),
         vectors,
     )
+    wd = lax.all_gather(down_weight, AXES, axis=0, tiled=True)
+    g_in = Gather(grid, in_mine, in_other, (cut + 128) // 256 * 128)
+    g_in.chips()
+    if not grid.plain:
+        g_in.chip, destination = tie(g_in.chip, destination)
+    g_in.along_z()
     capacity, out_pick, in_origin, in_place, back_pick, back_origin, back_place = routes(
         destination, samples, fsdp
     )
     alive = (exit_layer > LAYER).astype(jnp.int32)
-
-    wd = lax.all_gather(down_weight, AXES, axis=0, tiled=True)
-    g_in = Gather(grid, in_mine, in_other, (cut + 128) // 256 * 128)
-    g_in.along_z()
     outgoing = pick(back_pick, repacked_grad, fsdp - 1, capacity)
+    g_in.stack_z()
     returned = [exchange(outgoing[0], fsdp, 1)]
     if not grid.plain:
         g_in.stack, ff_mine, returned[0] = tie(g_in.stack, ff_mine, returned[0])
     g_ff = Gather(grid, ff_mine, ff_other, (ff + width) // 512 * 128 + 128)
     g_in.along_xy()
     g_in.diagonal()
+    g_ff.chips()
     g_ff.along_z()
+    g_ff.stack_z()
     g_in.finish()
     if not grid.plain:
         *g_in.parts, g_ff.stack = tie(*g_in.parts, g_ff.stack)
+    last = exchange(outgoing[-1], fsdp, fsdp - 1)
+    outgoing = outgoing[:-1]
     g_ff.along_xy()
     rows = tokens.reshape(count, width)
     qkv, prob, mixed, turned, vec, sv, pw, cw, ubm, cb, ws = attend(
@@ -1367,10 +1416,10 @@
             mixed, g_ff.from_x, g_ff.from_y, g_ff.near, *rest
         )
     g_ff.diagonal()
-    returned += [exchange(part, fsdp, o + 2) for o, part in enumerate(rest)]
+    returned += [exchange(part, fsdp, o + 2) for o, part in enumerate(rest)] + [last]
     g_ff.finish()
     ub = jnp.broadcast_to(ubm[:, : ff // devices].reshape(1, ff), (8, ff))
-    normed, factor, low, act, slope = up_part(g_ff, mixed, rows, vec, ub, block)
+    normed, factor, act, slope = up_part(g_ff, mixed, rows, vec, ub, block)
     act, *returned = tie(act, *returned)
     second_cot = place(back_origin, back_place, [repacked_grad] + returned)
     steps = count // wide_block
@@ -1378,7 +1427,7 @@
         logits_grad.reshape(steps, samples // steps, classes),
         ((0, 0), (0, 8 - samples // steps), (0, 128 - classes)),
     ).reshape(steps * 8, 128)
-    second, sum_two, dcot, logits, vgrad_two, sgrad, wsgrad, pwgrad, cwgrad, wd_grad = down_part(
+    second, dcot, logits, vgrad_two, sgrad, wsgrad, pwgrad, cwgrad, wd_grad = down_part(
         lengths,
         alive,
         act,
@@ -1404,20 +1453,25 @@
     dcot, *leaving = tie(dcot, *leaving)
     arrived = [exchange(part, fsdp, o + 1) for o, part in enumerate(leaving)]
     one_cot, mcot, vgrad_one, ugrad, wu_other, wu_mine, wo_other, wo_mine = up_back(
-        g_ff, dcot, slope, sum_two, normed, factor, low, mixed, wd, vec, block, ff // 6
+        g_ff, dcot, slope, normed, factor, mixed, wd, vec, wide_block, ff // 6
     )
     mcot, wu_other, wo_other, *arrived = tie(mcot, wu_other, wo_other, *arrived)
     s_ff = Scatter(grid, [wo_mine, wu_mine], (ff + width) // 512 * 128 + 128)
     s_ff.core([wo_other, wu_other])
+    repacked = place(in_origin, in_place, [second] + arrived)
     s_ff.begin()
-    mcot, *out = tie(mcot, *s_ff.out_one, *s_ff.out_two)
-    s_ff.out_one, s_ff.out_two = out[: len(s_ff.out_one)], out[len(s_ff.out_one) :]
+    (mcot, repacked), s_ff.out_one, s_ff.out_two = tie_lists(
+        (mcot, repacked), s_ff.out_one, s_ff.out_two
+    )
     s_ff.first()
     pcot, vgrad_in = attend_back(mcot, qkv, prob, seq, wide_block)
-    (pcot, vgrad_in), s_ff.in_one, s_ff.in_two = tie_lists(
-        (pcot, vgrad_in), s_ff.in_one, s_ff.in_two
+    wi_other, wi_mine = input_grad(grid.here, turned, pcot, width // 2)
+    wi_got = grid.send(wi_other, "c", 1)
+    (wi_mine, vgrad_in, wd_share), s_ff.in_one, s_ff.in_two = tie_lists(
+        (wi_mine, vgrad_in, wd_share), s_ff.in_one, s_ff.in_two
     )
     s_ff.second()
+    s_ff.second_sends()
     ugm = jnp.pad(ugrad[0].reshape(devices, -1), ((0, 0), (0, 128 - ff // devices)))
     small_other, small_mine = small_pieces(
         grid,
@@ -1425,18 +1479,13 @@
         classes,
         devices,
     )
-    wi_other, wi_mine = input_grad(grid.here, turned, pcot, width // 2)
-    (wi_other, small_other, wd_share), s_ff.in_one, s_ff.in_two, arrived = tie_lists(
-        (wi_other, small_other, wd_share), s_ff.in_one, s_ff.in_two, arrived
-    )
     s_in = Scatter(grid, [wi_mine, small_mine], (cut + 128) // 2)
-    s_in.core([wi_other, small_other])
+    s_in.got = [wi_got, grid.send(small_other, "c", 1)]
+    s_in.begin()
+    (pcot,), s_in.out_one, s_in.out_two, s_ff.in_one, s_ff.in_two = tie_lists(
+        (pcot,), s_in.out_one, s_in.out_two, s_ff.in_one, s_ff.in_two
+    )
     s_ff.third()
-    repacked = place(in_origin, in_place, [second] + arrived)
-    s_in.begin()
-    (pcot, repacked), s_in.out_one, s_in.out_two = tie_lists(
-        (pcot, repacked), s_in.out_one, s_in.out_two
-    )
     s_in.first()
     tokens_grad = token_part(g_in, pcot, one_cot, wide_block)
     (tokens_grad,), s_in.in_one, s_in.in_two, s_ff.came = tie_lists(
@@ -1444,6 +1493,8 @@
     )
     tokens_grad = tokens_grad.reshape(samples, seq, width)
     s_in.second()
+    s_ff.came, s_in.out_one, s_in.out_two = tie_lists(s_ff.came, s_in.out_one, s_in.out_two)
+    s_in.second_sends()
     ff_share = s_ff.last()
     s_in.third()
     in_share = s_in.last()

time: 417 us -> 420 us (level)
  Pallas kernels: 234 us -> 222 us
  waiting for transfers between devices: 69.7 us -> 78.7 us
    pallas_call x1, Pallas kernels: 24.1 us -> 14.6 us  [attend_back(): pl.pallas_call(functools.partial(attend_back_kernel, seq=seq, width=width...]
    ppermute x46, waiting for transfers between devices: 61.3 us -> 70.6 us  [send(): return lax.ppermute(array, AXES, pairs)]
    unnamed x76 -> x80, local copies, waits for them, and re-layouts: 8.73 us -> 6.07 us
  transfers between devices with their start and end apart: 54 -> 54, of which waited for: 16 -> 19; matrix products, arithmetic and copies ran while one was open for 7% -> 10% of each run, Pallas kernels for 44% -> 41%
where the time goes in v3:
time: 420 us; the launch traced here: 414 us
  Pallas kernels  222 us (53%)
  waiting for transfers between devices  78.7 us (19%)
  starting transfers between devices  44.2 us (11%)
  other arithmetic  27.8 us (7%)
  local copies, waits for them, and re-layouts  25.3 us (6%)
  between operations  15.4 us (4%)
    ppermute x46, waiting for transfers between devices, send(): return lax.ppermute(array, AXES, pairs)  70.6 us
    pallas_call x1, Pallas kernels, up_back(): pl.pallas_call(functools.partial(up_back_kernel, copies=copies, size=size...  57.2 us
    pallas_call x1, Pallas kernels, down_part(): pl.pallas_call(functools.partial(down_kernel, seq=seq, steps=steps, tile=...  45.6 us
    ppermute x46, starting transfers between devices, send(): return lax.ppermute(array, AXES, pairs)  39.3 us
    pallas_call x1, Pallas kernels, up_part(): pl.pallas_call(functools.partial(up_kernel, copies=copies, size=size, chu...  26.4 us
    pallas_call x1, Pallas kernels, attend(): pl.pallas_call(functools.partial(attend_kernel, copies=copies, size=size,...  22.7 us
    pallas_call x1, Pallas kernels, input_grad(): pl.pallas_call(functools.partial(input_grad_kernel, per=per), grid_spec=p...  15.6 us
    pallas_call x1, Pallas kernels, token_part(): pl.pallas_call(functools.partial(token_kernel, copies=copies, size=size),...  15.3 us
  transfers between devices with their start and end apart: 54, of which 19 were waited for; matrix products, arithmetic and copies ran while one was open for 10% of the time, Pallas kernels for 41%

profile of v3, /device:TPU:0, one launch (start us, length us, event | category | flops | bytes accessed | tf_op | source)
XLA Modules:
  0.0 413.7 jit_solution(4240723064102865062)
XLA Ops:
  8.6 2.7 pack.1
  18.0 4.7 %pick.2 = (bf16[6,128,768]{2,1,0:T(8,128)(2,1)}, bf16[6,128,768]{2,1,0:T(8,128)(2,1)}, bf16[6,128,768]{2,1,0:T(8,128)(2,1)}) custom-call(s32[3,6]{1,0:T(4,128)} %select_reduce_fusion.4.table, bf16[16,128,768]{2,1,0:T(8,128)(2,1)} %refs_0_.3), custom_call_target="tpu_custom_call" | custom-call | bytes 2123366 | tf_op jit(solution)/shard_map/pick/pallas_call | solution.py:1003
  23.0 5.1 %collective-permute-start.3 = (bf16[48,1280]{1,0:T(8,128)(2,1)S(1)}, bf16[48,1280]{1,0:T(8,128)(2,1)S(1)}, u32[]{:S(2)}, u32[]{:S(2)}) collective-permute-start(bf16[48,1280]{1,0:T(8,128)(2,1)S(1)} %pad_maximum_fusion.8), channel_id=1, source_target_pairs={{0,24},{1,25},{2,26},{3,27},{4,28},{5,29},{6,30},{7,31},{8,0},{9,1... | collective-permute-start | bytes 368648 | tf_op jit(solution)/shard_map/ppermute | solution.py:1125
  30.0 2.2 collective-permute-done.3
  32.2 9.3 %collective-permute-done.2 = bf16[48,1280]{1,0:T(8,128)(2,1)S(1)} collective-permute-done((bf16[48,1280]{1,0:T(8,128)(2,1)S(1)}, bf16[48,1280]{1,0:T(8,128)(2,1)S(1)}, u32[]{:S(2)}, u32[]{:S(2)}) %collective-permute-start.2) | collective-permute-done | bytes 122912 | tf_op jit(solution)/shard_map/ppermute | solution.py:1125
  41.6 1.6 collective-permute-start.6
  43.2 1.4 collective-permute-start.5
  46.0 2.6 collective-permute-start.17
  48.6 1.4 collective-permute-start.15
  50.0 7.1 %collective-permute-done.6.refs_3_.refs_4_ = bf16[192,1280]{1,0:T(8,128)(2,1)S(1)} collective-permute-done((bf16[192,1280]{1,0:T(8,128)(2,1)S(1)}, bf16[192,1280]{1,0:T(8,128)(2,1)S(1)}, u32[]{:S(2)}, u32[]{:S(2)}) %collective-permute-start.6) | collective-permute-done | bytes 491552 | tf_op jit(solution)/shard_map/ppermute | solution.py:1125
  58.1 2.6 collective-permute-done.5.refs_2_.refs_3_
  61.0 7.7 %collective-permute-done.16 = bf16[48,1920]{1,0:T(8,128)(2,1)S(1)} collective-permute-done((bf16[48,1920]{1,0:T(8,128)(2,1)S(1)}, bf16[48,1920]{1,0:T(8,128)(2,1)S(1)}, u32[]{:S(2)}, u32[]{:S(2)}) %collective-permute-start.16) | collective-permute-done | bytes 184352 | tf_op jit(solution)/shard_map/ppermute | solution.py:1125
  72.9 1.5 collective-permute-start.19
  74.4 1.5 collective-permute-start.18
  75.9 22.7 %attend.1 = (bf16[2048,2304]{1,0:T(8,128)(2,1)}, bf16[16,6,128,256]{3,2,1,0:T(8,128)(2,1)}, bf16[2048,768]{1,0:T(8,128)(2,1)}, bf16[768,2048]{1,0:T(8,128)(2,1)}...) custom-call(s32[16]{0:T(128)} %lens.3, ...), custom_call_target="tpu_custom_call" | custom-call | flops 4348654592 | bytes 9000000 | tf_op jit(solution)/shard_map/attend/pallas_call | solution.py:283
  103.1 6.5 %collective-permute-done.22.refs_8_.refs_11_ = bf16[192,896]{1,0:T(8,128)(2,1)} collective-permute-done((bf16[192,896]{1,0:T(8,128)(2,1)S(1)}, bf16[192,896]{1,0:T(8,128)(2,1)}, u32[]{:S(2)}, u32[]{:S(2)}) %collective-permute-start.22) | collective-permute-done | bytes 344096 | tf_op jit(solution)/shard_map/ppermute | solution.py:1125
  112.9 1.5 collective-permute-start.27
  118.9 26.4 %up_part.1 = (f32[2048,768]{1,0:T(8,128)}, f32[2048,128]{1,0:T(8,128)}, bf16[2048,3072]{1,0:T(8,128)(2,1)}, bf16[2048,3072]{1,0:T(8,128)(2,1)}) custom-call(s32[4]{0:T(128)} %pad_add_fusion.here, bf16[2048,768]{1,0:T(8,128)(2,1)} %get-tuple-element.169.refs_0_.refs_4_, bf16[2048,768]{1,0:T(8,128)(2,1)} %bitcast.160, ...), custom_call_target="tpu_custom_call" | custom-call | flops 7247757312 | bytes 15000000 | tf_op jit(solution)/shard_map/up_part/pallas_call | solution.py:360
  145.4 7.5 %collective-permute-done.27.refs_2_ = bf16[6,128,768]{2,1,0:T(8,128)(2,1)S(1)} collective-permute-done((bf16[6,128,768]{2,1,0:T(8,128)(2,1)}, bf16[6,128,768]{2,1,0:T(8,128)(2,1)S(1)}, u32[]{:S(2)}, u32[]{:S(2)}) %collective-permute-start.27) | collective-permute-done | bytes 1179680 | tf_op jit(solution)/shard_map/ppermute | solution.py:1313
  153.9 3.8 place.2
  157.7 45.6 %down_part.1 = (bf16[2048,768]{1,0:T(8,128)(2,1)}, bf16[2048,768]{1,0:T(8,128)(2,1)}, f32[32,128]{1,0:T(8,128)}, f32[8,768]{1,0:T(8,128)}, f32[8,128]{1,0:T(8,12...) custom-call(s32[16]{0:T(128)} %lens.3, ...), custom_call_target="tpu_custom_call" | custom-call | flops 11596411904 | bytes 18000000 | tf_op jit(solution)/shard_map/down_part/pallas_call | solution.py:545
  203.3 4.8 %pick.3 = (bf16[6,128,768]{2,1,0:T(8,128)(2,1)}, bf16[6,128,768]{2,1,0:T(8,128)(2,1)}, bf16[6,128,768]{2,1,0:T(8,128)(2,1)}) custom-call(s32[3,6]{1,0:T(4,128)} %select_reduce_fusion.3.table, bf16[16,128,768]{2,1,0:T(8,128)(2,1)} %bitcast.139), custom_call_target="tpu_custom_call" | custom-call | bytes 2123366 | tf_op jit(solution)/shard_map/pick/pallas_call | solution.py:1003
  208.9 1.4 collective-permute-start.31
  210.4 57.2 %up_back.1 = (bf16[2048,768]{1,0:T(8,128)(2,1)}, bf16[2048,768]{1,0:T(8,128)(2,1)}, f32[8,768]{1,0:T(8,128)}, f32[8,3072]{1,0:T(8,128)}, bf16[768,1536]{1,0:T(8,...) custom-call(s32[4]{0:T(128)} %pad_add_fusion.here, ...), custom_call_target="tpu_custom_call" | custom-call | flops 11596411904 | bytes 18000000 | tf_op jit(solution)/shard_map/up_back/pallas_call | solution.py:693
  270.5 4.2 %place.3 = bf16[16,128,768]{2,1,0:T(8,128)(2,1)} custom-call(s32[16]{0:T(128)} %get-tuple-element.271.origin, s32[16]{0:T(128)} %get-tuple-element.270.position, bf16[16,128,768]{2,1,0:T(8,128)(2,1)} %bitcast.140, bf16[6,128,768]{2,1,0:T(8,128)(2,1)} %copy-done.10, bf16[6,128,768]{2,1,0:T(8,128)(2,1)} %copy-done.11, bf16[6,128,768]{2,1,0:T(8,128)(2,1)} %copy-done.12), custom_call_target="tpu_custom_call" | custom-call | bytes 1887436 | tf_op jit(solution)/shard_map/place/pallas_call | solution.py:1044
  274.7 1.5 convert_add_fusion.2
  280.6 14.6 %attend_back.1 = (bf16[2048,2304]{1,0:T(8,128)(2,1)}, f32[8,768]{1,0:T(8,128)}) custom-call(bf16[2048,768]{1,0:T(8,128)(2,1)} %get-tuple-element.212.mcot_ref, bf16[2048,2304]{1,0:T(8,128)(2,1)} %get-tuple-element.213.qkv_ref, bf16[16,6,128,256]{3,2,1,0:T(8,128)(2,1)} %get-tuple-element.214.prob_ref), custom_call_target="tpu_custom_call" | custom-call | flops 4348654592 | bytes 9000000 | tf_op jit(solution)/shard_map/attend_back/pallas_call | solution.py:848
  295.2 15.6 %input_grad.1 = (bf16[768,1152]{1,0:T(8,128)(2,1)}, bf16[768,1152]{1,0:T(8,128)(2,1)}) custom-call(s32[4]{0:T(128)} %pad_add_fusion.here, bf16[768,2048]{1,0:T(8,128)(2,1)} %get-tuple-element.216.turned_ref, bf16[2048,2304]{1,0:T(8,128)(2,1)} %get-tuple-element.236.pcot_ref.refs_0_), custom_call_target="tpu_custom_call" | custom-call | flops 2174327296 | bytes 6000000 | tf_op jit(solution)/shard_map/input_grad/pallas_call | solution.py:777
  311.2 1.8 collective-permute-start.35
  316.0 1.5 slice_reduce_fusion
  318.9 10.2 %collective-permute-done.35 = bf16[2,4,48,896]{3,2,1,0:T(8,128)(2,1)} collective-permute-done((bf16[2,4,48,896]{3,2,1,0:T(8,128)(2,1)}, bf16[2,4,48,896]{3,2,1,0:T(8,128)(2,1)}, u32[]{:S(2)}, u32[]{:S(2)}) %collective-permute-start.35) | collective-permute-done | bytes 688160 | tf_op jit(solution)/shard_map/ppermute | solution.py:1125
  329.1 1.8 collective-permute-done.34
  330.9 3.2 small_pieces.1
  335.8 2.1 fusion
  337.9 1.8 collective-permute-start.38
  339.7 1.8 convert_add_fusion.1
  343.9 2.1 collective-permute-done.39
  346.0 3.3 collective-permute-done.38
  349.4 1.6 collective-permute-start.40
  351.1 1.5 collective-permute-start.41
  356.7 15.3 %token_part.1 = f32[2048,768]{1,0:T(8,128)} custom-call(s32[4]{0:T(128)} %pad_add_fusion.here, bf16[2048,2304]{1,0:T(8,128)(2,1)} %get-tuple-element.236.pcot_ref.refs_0_, bf16[2048,768]{1,0:T(8,128)(2,1)} %get-tuple-element.237.refs_1_, bf16[192,1280]{1,0:T(8,128)(2,1)} %copy-done.7, bf16[192,1280]{1,0:T(8,128)(2,1)} %copy-done.16, ...), custom_call_target="tpu_custom_call" | custom-call | flops 2174327296 | bytes 7500000 | tf_op jit(solution)/shard_map/token_part/pallas_call | solution.py:892
  372.1 1.5 bitcast_add_fusion.1
  377.4 1.7 collective-permute-start.45
  379.8 6.0 %collective-permute-done.45 = bf16[4,48,640]{2,1,0:T(8,128)(2,1)S(1)} collective-permute-done((bf16[4,48,640]{2,1,0:T(8,128)(2,1)S(1)}, bf16[4,48,640]{2,1,0:T(8,128)(2,1)S(1)}, u32[]{:S(2)}, u32[]{:S(2)}) %collective-permute-start.45) | collective-permute-done | bytes 245792 | tf_op jit(solution)/shard_map/ppermute | solution.py:1125
  387.4 3.8 collective-permute-start.49
  391.9 3.5 collective-permute-done.47
  395.4 4.9 %collective-permute-done.48 = bf16[48,1280]{1,0:T(8,128)(2,1)S(1)} collective-permute-done((bf16[48,1280]{1,0:T(8,128)(2,1)S(1)}, bf16[48,1280]{1,0:T(8,128)(2,1)S(1)}, u32[]{:S(2)}, u32[]{:S(2)}) %collective-permute-start.48) | collective-permute-done | bytes 122912 | tf_op jit(solution)/shard_map/ppermute | solution.py:1125
  403.0 1.4 finish.1
  (250 shorter events, 62.9 us)
Async XLA Ops:
  7.2 150.5 %all-gather.2.cloned.1.call-start = ((), (), s32[]{:S(2)}) async-start(), calls=%async_computation.1 | async-start | bytes 4866048 | tf_op jit(solution)/shard_map/all_gather | solution.py:1382
  7.9 323.0 %reduce-scatter.2.cloned.1.call-start = ((), (), s32[]{:S(2)}) async-start(), calls=%async_computation.2 | async-start | bytes 4866048 | tf_op jit(solution)/shard_map/reduce_scatter | solution.py:1451
  22.7 18.9 %collective-permute-start.4 = (bf16[6,128,768]{2,1,0:T(8,128)(2,1)}, bf16[6,128,768]{2,1,0:T(8,128)(2,1)S(1)}, u32[]{:S(2)}, u32[]{:S(2)}) collective-permute-start(bf16[6,128,768]{2,1,0:T(8,128)(2,1)} %get-tuple-element.152), channel_id=1, source_target_pairs={{0,1},{1,2},{2,3},{3,0},{4,5},{5,6},{6,7},{7,4},{8,9},{9,10},{10,1... | collective-permute-start | bytes 3538952 | tf_op jit(solution)/shard_map/ppermute | solution.py:1313
  23.0 9.3 %collective-permute-start.3 = (bf16[48,1280]{1,0:T(8,128)(2,1)S(1)}, bf16[48,1280]{1,0:T(8,128)(2,1)S(1)}, u32[]{:S(2)}, u32[]{:S(2)}) collective-permute-start(bf16[48,1280]{1,0:T(8,128)(2,1)S(1)} %pad_maximum_fusion.8), channel_id=1, source_target_pairs={{0,24},{1,25},{2,26},{3,27},{4,28},{5,29},{6,30},{7,31},{8,0},{9,1... | collective-permute-start | bytes 368648 | tf_op jit(solution)/shard_map/ppermute | solution.py:1125
  28.0 13.4 %collective-permute-start.2 = (bf16[48,1280]{1,0:T(8,128)(2,1)S(1)}, bf16[48,1280]{1,0:T(8,128)(2,1)S(1)}, u32[]{:S(2)}, u32[]{:S(2)}) collective-permute-start(bf16[48,1280]{1,0:T(8,128)(2,1)S(1)} %pad_maximum_fusion.8), channel_id=1, source_target_pairs={{0,16},{1,17},{2,18},{3,19},{4,20},{5,21},{6,22},{7,23},{8,24},{9,... | collective-permute-start | bytes 368648 | tf_op jit(solution)/shard_map/ppermute | solution.py:1125
  28.0 13.4 %collective-permute-start.1 = (bf16[48,1280]{1,0:T(8,128)(2,1)S(1)}, bf16[48,1280]{1,0:T(8,128)(2,1)S(1)}, u32[]{:S(2)}, u32[]{:S(2)}) collective-permute-start(bf16[48,1280]{1,0:T(8,128)(2,1)S(1)} %pad_maximum_fusion.8), channel_id=1, source_target_pairs={{0,8},{1,9},{2,10},{3,11},{4,12},{5,13},{6,14},{7,15},{8,16},{9,17... | collective-permute-start | bytes 368648 | tf_op jit(solution)/shard_map/ppermute | solution.py:1125
  29.3 15.3 %collective-permute-start.14 = (bf16[24,1920]{1,0:T(8,128)(2,1)S(1)}, bf16[24,1920]{1,0:T(8,128)(2,1)S(1)}, u32[]{:S(2)}, u32[]{:S(2)}) collective-permute-start(bf16[24,1920]{1,0:T(8,128)(2,1)S(1)} %copy-done.38), channel_id=1, source_target_pairs={{0,1},{1,0},{2,3},{3,2},{4,5},{5,4},{6,7},{7,6},{8,9},{9,8},{10,11... | collective-permute-start | bytes 276488 | tf_op jit(solution)/shard_map/ppermute | solution.py:1125
  41.6 15.5 %collective-permute-start.6 = (bf16[192,1280]{1,0:T(8,128)(2,1)S(1)}, bf16[192,1280]{1,0:T(8,128)(2,1)S(1)}, u32[]{:S(2)}, u32[]{:S(2)}) collective-permute-start(bf16[192,1280]{1,0:T(8,128)(2,1)S(1)} %pad_maximum_fusion.4.refs_1_.refs_2_), channel_id=1, source_target_pairs={{0,4},{1,5},{2,6},{3,7},{4,0},{5,1},{6,2},{7,3},{8,12},{9,13},{10,... | collective-permute-start | bytes 1474568 | tf_op jit(solution)/shard_map/ppermute | solution.py:1125
  43.2 17.4 %collective-permute-start.5 = (bf16[192,1280]{1,0:T(8,128)(2,1)S(1)}, bf16[192,1280]{1,0:T(8,128)(2,1)S(1)}, u32[]{:S(2)}, u32[]{:S(2)}) collective-permute-start(bf16[192,1280]{1,0:T(8,128)(2,1)S(1)} %pad_maximum_fusion.4.refs_1_.refs_2_), channel_id=1, source_target_pairs={{0,2},{1,3},{2,0},{3,1},{4,6},{5,7},{6,4},{7,5},{8,10},{9,11},{10,... | collective-permute-start | bytes 1474568 | tf_op jit(solution)/shard_map/ppermute | solution.py:1125
  46.0 15.0 %collective-permute-start.17 = (bf16[48,1920]{1,0:T(8,128)(2,1)S(1)}, bf16[48,1920]{1,0:T(8,128)(2,1)S(1)}, u32[]{:S(2)}, u32[]{:S(2)}) collective-permute-start(bf16[48,1920]{1,0:T(8,128)(2,1)S(1)} %pad_maximum_fusion.7), channel_id=1, source_target_pairs={{0,24},{1,25},{2,26},{3,27},{4,28},{5,29},{6,30},{7,31},{8,0},{9,1... | collective-permute-start | bytes 552968 | tf_op jit(solution)/shard_map/ppermute | solution.py:1125
  48.6 20.2 %collective-permute-start.16 = (bf16[48,1920]{1,0:T(8,128)(2,1)S(1)}, bf16[48,1920]{1,0:T(8,128)(2,1)S(1)}, u32[]{:S(2)}, u32[]{:S(2)}) collective-permute-start(bf16[48,1920]{1,0:T(8,128)(2,1)S(1)} %pad_maximum_fusion.7), channel_id=1, source_target_pairs={{0,16},{1,17},{2,18},{3,19},{4,20},{5,21},{6,22},{7,23},{8,24},{9,... | collective-permute-start | bytes 552968 | tf_op jit(solution)/shard_map/ppermute | solution.py:1125
  48.6 20.2 %collective-permute-start.15 = (bf16[48,1920]{1,0:T(8,128)(2,1)S(1)}, bf16[48,1920]{1,0:T(8,128)(2,1)S(1)}, u32[]{:S(2)}, u32[]{:S(2)}) collective-permute-start(bf16[48,1920]{1,0:T(8,128)(2,1)S(1)} %pad_maximum_fusion.7), channel_id=1, source_target_pairs={{0,8},{1,9},{2,10},{3,11},{4,12},{5,13},{6,14},{7,15},{8,16},{9,17... | collective-permute-start | bytes 552968 | tf_op jit(solution)/shard_map/ppermute | solution.py:1125
  57.1 12.9 %collective-permute-start.8 = (bf16[192,640]{1,0:T(8,128)(2,1)S(1)}, bf16[192,640]{1,0:T(8,128)(2,1)S(1)}, u32[]{:S(2)}, u32[]{:S(2)}) collective-permute-start(bf16[192,640]{1,0:T(8,128)(2,1)S(1)} %slice.159), channel_id=1, source_target_pairs={{0,2},{1,3},{2,0},{3,1},{4,6},{5,7},{6,4},{7,5},{8,10},{9,11},{10,... | collective-permute-start | bytes 737288 | tf_op jit(solution)/shard_map/ppermute | solution.py:1125
  60.7 9.3 %collective-permute-start.7 = (bf16[192,640]{1,0:T(8,128)(2,1)S(1)}, bf16[192,640]{1,0:T(8,128)(2,1)S(1)}, u32[]{:S(2)}, u32[]{:S(2)}) collective-permute-start(bf16[192,640]{1,0:T(8,128)(2,1)S(1)} %slice.158), channel_id=1, source_target_pairs={{0,4},{1,5},{2,6},{3,7},{4,0},{5,1},{6,2},{7,3},{8,12},{9,13},{10,... | collective-permute-start | bytes 737288 | tf_op jit(solution)/shard_map/ppermute | solution.py:1125
  61.0 10.9 %collective-permute-start.9 = (bf16[192,1280]{1,0:T(8,128)(2,1)S(1)}, bf16[192,1280]{1,0:T(8,128)(2,1)S(1)}, u32[]{:S(2)}, u32[]{:S(2)}) collective-permute-start(bf16[192,1280]{1,0:T(8,128)(2,1)S(1)} %pad_maximum_fusion.4.refs_1_.refs_2_), channel_id=1, source_target_pairs={{0,1},{1,0},{2,3},{3,2},{4,5},{5,4},{6,7},{7,6},{8,9},{9,8},{10,11... | collective-permute-start | bytes 1474568 | tf_op jit(solution)/shard_map/ppermute | solution.py:1125
  68.8 4.0 collective-permute-start.10
  72.7 25.9 %collective-permute-start.20 = (bf16[192,1920]{1,0:T(8,128)(2,1)}, bf16[192,1920]{1,0:T(8,128)(2,1)}, u32[]{:S(2)}, u32[]{:S(2)}) collective-permute-start(bf16[192,1920]{1,0:T(8,128)(2,1)} %constant_dynamic-update-slice_fusion.refs_4_.refs_7_), channel_id=1, source_target_pairs={{0,1},{1,0},{2,3},{3,2},{4,5},{5,4},{6,7},{7,6},{8,9},{9,8},{10,11... | collective-permute-start | bytes 2211848 | tf_op jit(solution)/shard_map/ppermute | solution.py:1125
  72.9 25.7 %collective-permute-start.19 = (bf16[192,1920]{1,0:T(8,128)(2,1)}, bf16[192,1920]{1,0:T(8,128)(2,1)}, u32[]{:S(2)}, u32[]{:S(2)}) collective-permute-start(bf16[192,1920]{1,0:T(8,128)(2,1)} %constant_dynamic-update-slice_fusion.refs_4_.refs_7_), channel_id=1, source_target_pairs={{0,4},{1,5},{2,6},{3,7},{4,0},{5,1},{6,2},{7,3},{8,12},{9,13},{10,... | collective-permute-start | bytes 2211848 | tf_op jit(solution)/shard_map/ppermute | solution.py:1125
  74.4 24.2 %collective-permute-start.18 = (bf16[192,1920]{1,0:T(8,128)(2,1)}, bf16[192,1920]{1,0:T(8,128)(2,1)}, u32[]{:S(2)}, u32[]{:S(2)}) collective-permute-start(bf16[192,1920]{1,0:T(8,128)(2,1)} %constant_dynamic-update-slice_fusion.refs_4_.refs_7_), channel_id=1, source_target_pairs={{0,2},{1,3},{2,0},{3,1},{4,6},{5,7},{6,4},{7,5},{8,10},{9,11},{10,... | collective-permute-start | bytes 2211848 | tf_op jit(solution)/shard_map/ppermute | solution.py:1125
  99.7 9.9 %collective-permute-start.22 = (bf16[192,896]{1,0:T(8,128)(2,1)S(1)}, bf16[192,896]{1,0:T(8,128)(2,1)}, u32[]{:S(2)}, u32[]{:S(2)}) collective-permute-start(bf16[192,896]{1,0:T(8,128)(2,1)S(1)} %slice.122), channel_id=1, source_target_pairs={{0,2},{1,3},{2,0},{3,1},{4,6},{5,7},{6,4},{7,5},{8,10},{9,11},{10,... | collective-permute-start | bytes 1032200 | tf_op jit(solution)/shard_map/ppermute | solution.py:1125
  101.3 11.6 %collective-permute-start.21 = (bf16[192,1024]{1,0:T(8,128)(2,1)S(1)}, bf16[192,1024]{1,0:T(8,128)(2,1)S(1)}, u32[]{:S(2)}, u32[]{:S(2)}) collective-permute-start(bf16[192,1024]{1,0:T(8,128)(2,1)S(1)} %slice.121), channel_id=1, source_target_pairs={{0,4},{1,5},{2,6},{3,7},{4,0},{5,1},{6,2},{7,3},{8,12},{9,13},{10,... | collective-permute-start | bytes 1179656 | tf_op jit(solution)/shard_map/ppermute | solution.py:1125
  109.6 4.9 %collective-permute-start.26 = (bf16[192,896]{1,0:T(8,128)(2,1)}, bf16[192,896]{1,0:T(8,128)(2,1)}, u32[]{:S(2)}, u32[]{:S(2)}) collective-permute-start(bf16[192,896]{1,0:T(8,128)(2,1)} %collective-permute-done.22.refs_8_.refs_11_), channel_id=1, source_target_pairs={{0,1},{1,0},{2,3},{3,2},{4,5},{5,4},{6,7},{7,6},{8,9},{9,8},{10,11... | collective-permute-start | bytes 1032200 | tf_op jit(solution)/shard_map/ppermute | solution.py:1125
  110.9 34.5 %collective-permute-start.28 = (bf16[6,128,768]{2,1,0:T(8,128)(2,1)}, bf16[6,128,768]{2,1,0:T(8,128)(2,1)S(1)}, u32[]{:S(2)}, u32[]{:S(2)}) collective-permute-start(bf16[6,128,768]{2,1,0:T(8,128)(2,1)} %get-tuple-element.178), channel_id=1, source_target_pairs={{0,3},{1,0},{2,1},{3,2},{4,7},{5,4},{6,5},{7,6},{8,11},{9,8},{10,9... | collective-permute-start | bytes 3538952 | tf_op jit(solution)/shard_map/ppermute | solution.py:1313
  111.7 6.3 %collective-permute-start.23 = (bf16[192,1920]{1,0:T(8,128)(2,1)}, bf16[192,1920]{1,0:T(8,128)(2,1)S(1)}, u32[]{:S(2)}, u32[]{:S(2)}) collective-permute-start(bf16[192,1920]{1,0:T(8,128)(2,1)} %collective-permute-done.18.refs_5_.refs_8_), channel_id=1, source_target_pairs={{0,1},{1,0},{2,3},{3,2},{4,5},{5,4},{6,7},{7,6},{8,9},{9,8},{10,11... | collective-permute-start | bytes 2211848 | tf_op jit(solution)/shard_map/ppermute | solution.py:1125
  111.7 6.3 %collective-permute-start.24 = (bf16[192,1920]{1,0:T(8,128)(2,1)}, bf16[192,1920]{1,0:T(8,128)(2,1)}, u32[]{:S(2)}, u32[]{:S(2)}) collective-permute-start(bf16[192,1920]{1,0:T(8,128)(2,1)} %collective-permute-done.19.refs_6_.refs_9_), channel_id=1, source_target_pairs={{0,1},{1,0},{2,3},{3,2},{4,5},{5,4},{6,7},{7,6},{8,9},{9,8},{10,11... | collective-permute-start | bytes 2211848 | tf_op jit(solution)/shard_map/ppermute | solution.py:1125
  112.9 39.9 %collective-permute-start.27 = (bf16[6,128,768]{2,1,0:T(8,128)(2,1)}, bf16[6,128,768]{2,1,0:T(8,128)(2,1)S(1)}, u32[]{:S(2)}, u32[]{:S(2)}) collective-permute-start(bf16[6,128,768]{2,1,0:T(8,128)(2,1)} %get-tuple-element.177), channel_id=1, source_target_pairs={{0,2},{1,3},{2,0},{3,1},{4,6},{5,7},{6,4},{7,5},{8,10},{9,11},{10,... | collective-permute-start | bytes 3538952 | tf_op jit(solution)/shard_map/ppermute | solution.py:1313
  208.1 59.5 %collective-permute-start.29 = (bf16[6,128,768]{2,1,0:T(8,128)(2,1)}, bf16[6,128,768]{2,1,0:T(8,128)(2,1)S(1)}, u32[]{:S(2)}, u32[]{:S(2)}) collective-permute-start(bf16[6,128,768]{2,1,0:T(8,128)(2,1)} %get-tuple-element.199), channel_id=1, source_target_pairs={{0,1},{1,2},{2,3},{3,0},{4,5},{5,6},{6,7},{7,4},{8,9},{9,10},{10,1... | collective-permute-start | bytes 3538952 | tf_op jit(solution)/shard_map/ppermute | solution.py:1313
  208.2 59.5 %collective-permute-start.30 = (bf16[6,128,768]{2,1,0:T(8,128)(2,1)}, bf16[6,128,768]{2,1,0:T(8,128)(2,1)S(1)}, u32[]{:S(2)}, u32[]{:S(2)}) collective-permute-start(bf16[6,128,768]{2,1,0:T(8,128)(2,1)} %get-tuple-element.200), channel_id=1, source_target_pairs={{0,2},{1,3},{2,0},{3,1},{4,6},{5,7},{6,4},{7,5},{8,10},{9,11},{10,... | collective-permute-start | bytes 3538952 | tf_op jit(solution)/shard_map/ppermute | solution.py:1313
  208.9 58.7 %collective-permute-start.31 = (bf16[6,128,768]{2,1,0:T(8,128)(2,1)}, bf16[6,128,768]{2,1,0:T(8,128)(2,1)S(1)}, u32[]{:S(2)}, u32[]{:S(2)}) collective-permute-start(bf16[6,128,768]{2,1,0:T(8,128)(2,1)} %get-tuple-element.201), channel_id=1, source_target_pairs={{0,3},{1,0},{2,1},{3,2},{4,7},{5,4},{6,5},{7,6},{8,11},{9,8},{10,9... | collective-permute-start | bytes 3538952 | tf_op jit(solution)/shard_map/ppermute | solution.py:1313
  269.2 7.0 %collective-permute-start.33 = (bf16[768,1536]{1,0:T(8,128)(2,1)}, bf16[768,1536]{1,0:T(8,128)(2,1)S(1)}, u32[]{:S(2)}, u32[]{:S(2)}) collective-permute-start(bf16[768,1536]{1,0:T(8,128)(2,1)} %get-tuple-element.209), channel_id=1, source_target_pairs={{0,1},{1,0},{2,3},{3,2},{4,5},{5,4},{6,7},{7,6},{8,9},{9,8},{10,11... | collective-permute-start | bytes 7077896 | tf_op jit(solution)/shard_map/ppermute | solution.py:1125
  269.2 5.4 %collective-permute-start.32 = (bf16[768,384]{1,0:T(8,128)(2,1)}, bf16[768,384]{1,0:T(8,128)(2,1)}, u32[]{:S(2)}, u32[]{:S(2)}) collective-permute-start(bf16[768,384]{1,0:T(8,128)(2,1)} %get-tuple-element.207), channel_id=1, source_target_pairs={{0,1},{1,0},{2,3},{3,2},{4,5},{5,4},{6,7},{7,6},{8,9},{9,8},{10,11... | collective-permute-start | bytes 1769480 | tf_op jit(solution)/shard_map/ppermute | solution.py:1125
  310.8 28.9 %collective-permute-start.36 = (bf16[768,1152]{1,0:T(8,128)(2,1)}, bf16[768,1152]{1,0:T(8,128)(2,1)}, u32[]{:S(2)}, u32[]{:S(2)}) collective-permute-start(bf16[768,1152]{1,0:T(8,128)(2,1)} %get-tuple-element.223), channel_id=1, source_target_pairs={{0,1},{1,0},{2,3},{3,2},{4,5},{5,4},{6,7},{7,6},{8,9},{9,8},{10,11... | collective-permute-start | bytes 5308424 | tf_op jit(solution)/shard_map/ppermute | solution.py:1125
  310.8 20.1 %collective-permute-start.34 = (bf16[4,2,48,1024]{3,2,0,1:T(8,128)(2,1)S(1)}, bf16[4,2,48,1024]{3,2,0,1:T(8,128)(2,1)}, u32[]{:S(2)}, u32[]{:S(2)}) collective-permute-start(bf16[4,2,48,1024]{3,2,0,1:T(8,128)(2,1)S(1)} %fusion.4), channel_id=1, source_target_pairs={{0,4},{1,5},{2,6},{3,7},{4,0},{5,1},{6,2},{7,3},{8,12},{9,13},{10,... | collective-permute-start | bytes 2359304 | tf_op jit(solution)/shard_map/ppermute | solution.py:1125
  311.2 17.9 %collective-permute-start.35 = (bf16[2,4,48,896]{3,2,1,0:T(8,128)(2,1)}, bf16[2,4,48,896]{3,2,1,0:T(8,128)(2,1)}, u32[]{:S(2)}, u32[]{:S(2)}) collective-permute-start(bf16[2,4,48,896]{3,2,1,0:T(8,128)(2,1)} %fusion.5), channel_id=1, source_target_pairs={{0,2},{1,3},{2,0},{3,1},{4,6},{5,7},{6,4},{7,5},{8,10},{9,11},{10,... | collective-permute-start | bytes 2064392 | tf_op jit(solution)/shard_map/ppermute | solution.py:1125
  334.1 7.4 %collective-permute-start.37 = (bf16[768,128]{1,0:T(8,128)(2,1)}, bf16[768,128]{1,0:T(8,128)(2,1)S(1)}, u32[]{:S(2)}, u32[]{:S(2)}) collective-permute-start(bf16[768,128]{1,0:T(8,128)(2,1)} %get-tuple-element.233), channel_id=1, source_target_pairs={{0,1},{1,0},{2,3},{3,2},{4,5},{5,4},{6,7},{7,6},{8,9},{9,8},{10,11... | collective-permute-start | bytes 589832 | tf_op jit(solution)/shard_map/ppermute | solution.py:1125
  335.4 10.5 %collective-permute-start.39 = (bf16[4,48,896]{2,1,0:T(8,128)(2,1)S(1)}, bf16[4,48,896]{2,1,0:T(8,128)(2,1)S(1)}, u32[]{:S(2)}, u32[]{:S(2)}) collective-permute-start(bf16[4,48,896]{2,1,0:T(8,128)(2,1)S(1)} %fusion.16), channel_id=1, source_target_pairs={{0,4},{1,5},{2,6},{3,7},{4,0},{5,1},{6,2},{7,3},{8,12},{9,13},{10,... | collective-permute-start | bytes 1032200 | tf_op jit(solution)/shard_map/ppermute | solution.py:1125
  337.9 11.3 %collective-permute-start.38 = (bf16[4,48,1024]{2,1,0:T(8,128)(2,1)S(1)}, bf16[4,48,1024]{2,1,0:T(8,128)(2,1)S(1)}, u32[]{:S(2)}, u32[]{:S(2)}) collective-permute-start(bf16[4,48,1024]{2,1,0:T(8,128)(2,1)S(1)} %fusion.10), channel_id=1, source_target_pairs={{0,2},{1,3},{2,0},{3,1},{4,6},{5,7},{6,4},{7,5},{8,10},{9,11},{10,... | collective-permute-start | bytes 1179656 | tf_op jit(solution)/shard_map/ppermute | solution.py:1125
  349.4 22.6 %collective-permute-start.40 = (bf16[4,2,48,640]{3,2,0,1:T(8,128)(2,1)}, bf16[4,2,48,640]{3,2,0,1:T(8,128)(2,1)}, u32[]{:S(2)}, u32[]{:S(2)}) collective-permute-start(bf16[4,2,48,640]{3,2,0,1:T(8,128)(2,1)} %fusion.8), channel_id=1, source_target_pairs={{0,4},{1,5},{2,6},{3,7},{4,0},{5,1},{6,2},{7,3},{8,12},{9,13},{10,... | collective-permute-start | bytes 1474568 | tf_op jit(solution)/shard_map/ppermute | solution.py:1125
  351.1 21.0 %collective-permute-start.41 = (bf16[2,4,48,640]{3,2,1,0:T(8,128)(2,1)}, bf16[2,4,48,640]{3,2,1,0:T(8,128)(2,1)}, u32[]{:S(2)}, u32[]{:S(2)}) collective-permute-start(bf16[2,4,48,640]{3,2,1,0:T(8,128)(2,1)} %fusion.7), channel_id=1, source_target_pairs={{0,2},{1,3},{2,0},{3,1},{4,6},{5,7},{6,4},{7,5},{8,10},{9,11},{10,... | collective-permute-start | bytes 1474568 | tf_op jit(solution)/shard_map/ppermute | solution.py:1125
  353.4 18.6 %collective-permute-start.44 = (bf16[48,1920]{1,0:T(8,128)(2,1)}, bf16[48,1920]{1,0:T(8,128)(2,1)S(1)}, u32[]{:S(2)}, u32[]{:S(2)}) collective-permute-start(bf16[48,1920]{1,0:T(8,128)(2,1)} %get-tuple-element.281), channel_id=1, source_target_pairs={{0,24},{1,25},{2,26},{3,27},{4,28},{5,29},{6,30},{7,31},{8,0},{9,1... | collective-permute-start | bytes 552968 | tf_op jit(solution)/shard_map/ppermute | solution.py:1125
  354.2 17.8 %collective-permute-start.43 = (bf16[48,1920]{1,0:T(8,128)(2,1)}, bf16[48,1920]{1,0:T(8,128)(2,1)}, u32[]{:S(2)}, u32[]{:S(2)}) collective-permute-start(bf16[48,1920]{1,0:T(8,128)(2,1)} %get-tuple-element.282), channel_id=1, source_target_pairs={{0,16},{1,17},{2,18},{3,19},{4,20},{5,21},{6,22},{7,23},{8,24},{9,... | collective-permute-start | bytes 552968 | tf_op jit(solution)/shard_map/ppermute | solution.py:1125
  355.4 16.6 %collective-permute-start.42 = (bf16[48,1920]{1,0:T(8,128)(2,1)}, bf16[48,1920]{1,0:T(8,128)(2,1)}, u32[]{:S(2)}, u32[]{:S(2)}) collective-permute-start(bf16[48,1920]{1,0:T(8,128)(2,1)} %get-tuple-element.283), channel_id=1, source_target_pairs={{0,8},{1,9},{2,10},{3,11},{4,12},{5,13},{6,14},{7,15},{8,16},{9,17... | collective-permute-start | bytes 552968 | tf_op jit(solution)/shard_map/ppermute | solution.py:1125
  376.0 3.7 collective-permute-start.51
  377.4 8.3 %collective-permute-start.45 = (bf16[4,48,640]{2,1,0:T(8,128)(2,1)S(1)}, bf16[4,48,640]{2,1,0:T(8,128)(2,1)S(1)}, u32[]{:S(2)}, u32[]{:S(2)}) collective-permute-start(bf16[4,48,640]{2,1,0:T(8,128)(2,1)S(1)} %fusion.17), channel_id=1, source_target_pairs={{0,2},{1,3},{2,0},{3,1},{4,6},{5,7},{6,4},{7,5},{8,10},{9,11},{10,... | collective-permute-start | bytes 737288 | tf_op jit(solution)/shard_map/ppermute | solution.py:1125
  379.1 8.1 %collective-permute-start.46 = (bf16[4,48,640]{2,1,0:T(8,128)(2,1)S(1)}, bf16[4,48,640]{2,1,0:T(8,128)(2,1)S(1)}, u32[]{:S(2)}, u32[]{:S(2)}) collective-permute-start(bf16[4,48,640]{2,1,0:T(8,128)(2,1)S(1)} %fusion.18), channel_id=1, source_target_pairs={{0,4},{1,5},{2,6},{3,7},{4,0},{5,1},{6,2},{7,3},{8,12},{9,13},{10,... | collective-permute-start | bytes 737288 | tf_op jit(solution)/shard_map/ppermute | solution.py:1125
  387.3 8.1 %collective-permute-start.47 = (bf16[48,1280]{1,0:T(8,128)(2,1)S(1)}, bf16[48,1280]{1,0:T(8,128)(2,1)S(1)}, u32[]{:S(2)}, u32[]{:S(2)}) collective-permute-start(bf16[48,1280]{1,0:T(8,128)(2,1)S(1)} %get-tuple-element.284), channel_id=1, source_target_pairs={{0,8},{1,9},{2,10},{3,11},{4,12},{5,13},{6,14},{7,15},{8,16},{9,17... | collective-permute-start | bytes 368648 | tf_op jit(solution)/shard_map/ppermute | solution.py:1125
  387.4 8.0 %collective-permute-start.49 = (bf16[48,1280]{1,0:T(8,128)(2,1)S(1)}, bf16[48,1280]{1,0:T(8,128)(2,1)S(1)}, u32[]{:S(2)}, u32[]{:S(2)}) collective-permute-start(bf16[48,1280]{1,0:T(8,128)(2,1)S(1)} %get-tuple-element.285), channel_id=1, source_target_pairs={{0,24},{1,25},{2,26},{3,27},{4,28},{5,29},{6,30},{7,31},{8,0},{9,1... | collective-permute-start | bytes 368648 | tf_op jit(solution)/shard_map/ppermute | solution.py:1125
  391.2 9.2 %collective-permute-start.48 = (bf16[48,1280]{1,0:T(8,128)(2,1)S(1)}, bf16[48,1280]{1,0:T(8,128)(2,1)S(1)}, u32[]{:S(2)}, u32[]{:S(2)}) collective-permute-start(bf16[48,1280]{1,0:T(8,128)(2,1)S(1)} %get-tuple-element.286), channel_id=1, source_target_pairs={{0,16},{1,17},{2,18},{3,19},{4,20},{5,21},{6,22},{7,23},{8,24},{9,... | collective-permute-start | bytes 368648 | tf_op jit(solution)/shard_map/ppermute | solution.py:1125
  (45 other events, 543.1 us)
Sparse Core Ops, SparseCore 0:
  10.9 87.6 all-gather.1
  210.5 106.6 reduce-scatter.1

commit v4 on v2

--- a/solution.py
+++ b/solution.py
@@ -785,22 +785,32 @@
 
     for s in range(rows // seq):
         at = slice(s * seq, (s + 1) * seq)
-        for pair in range(width // 128):
-            low = pair * 128
-            q = split(qkv_ref[at, low : low + 128])
-            k = qkv_ref[at, width + low : width + low + 128]
-            v = qkv_ref[at, 2 * width + low : 2 * width + low + 128]
-            cot = split(mcot_ref[at, low : low + 128])
-            share = prob_ref[s, pair]
-            share_cot = dot_nt(v, cot)
-            pcot_ref[at, 2 * width + low : 2 * width + low + 128] = dot(share, cot).astype(BF16)
-            wide = share.astype(F32)
+        lows = range(0, width, 128)
+        cots = [split(mcot_ref[at, low : low + 128]) for low in lows]
+        share_cots = [
+            dot_nt(qkv_ref[at, 2 * width + low : 2 * width + low + 128], cot)
+            for low, cot in zip(lows, cots)
+        ]
+        values = [dot(prob_ref[s, n], cot) for n, cot in enumerate(cots)]
+        for low, value in zip(lows, values):
+            pcot_ref[at, 2 * width + low : 2 * width + low + 128] = value.astype(BF16)
+        score_cots = []
+        for n, share_cot in enumerate(share_cots):
+            wide = prob_ref[s, n].astype(F32)
             product = wide * share_cot
-            score_cot = (product - wide * column_sum(product)).astype(BF16)
-            pcot_ref[at, width + low : width + low + 128] = (dot(score_cot, q) * scale).astype(BF16)
-            query_cot = dot_tn(score_cot, k) * scale
+            score_cots.append((product - wide * column_sum(product)).astype(BF16))
+        keys = [
+            dot(score, split(qkv_ref[at, low : low + 128])) * scale
+            for low, score in zip(lows, score_cots)
+        ]
+        queries = [
+            dot_tn(score, qkv_ref[at, width + low : width + low + 128]) * scale
+            for low, score in zip(lows, score_cots)
+        ]
+        for low, key, query in zip(lows, keys, queries):
+            pcot_ref[at, width + low : width + low + 128] = key.astype(BF16)
             pcot_ref[at, low : low + 128] = jnp.where(
-                first_head, query_cot[:seq], query_cot[seq:]
+                first_head, query[:seq], query[seq:]
             ).astype(BF16)
     vgrad_ref[...] += stack_rows(
         [

time: 417 us -> 415 us (level)
  Pallas kernels: 234 us -> 225 us
  waiting for transfers between devices: 69.7 us -> 76.8 us
    pallas_call x1, Pallas kernels: 24.1 us -> 14.5 us  [attend_back(): pl.pallas_call(functools.partial(attend_back_kernel, seq=seq, width=width...]
    ppermute x46, waiting for transfers between devices: 61.3 us -> 68.4 us  [send(): return lax.ppermute(array, AXES, pairs)]
  transfers between devices with their start and end apart: 54 -> 54, of which waited for: 16 -> 18; matrix products, arithmetic and copies ran while one was open for 7% -> 7% of each run, Pallas kernels for 44% -> 42%
where the time goes in v4:
time: 415 us; the launch traced here: 408 us
  Pallas kernels  225 us (54%)
  waiting for transfers between devices  76.8 us (19%)
  starting transfers between devices  43.4 us (10%)
  other arithmetic  25.1 us (6%)
  local copies, waits for them, and re-layouts  22.5 us (5%)
  between operations  15.5 us (4%)
    ppermute x46, waiting for transfers between devices, send(): return lax.ppermute(array, AXES, pairs)  68.4 us
    pallas_call x1, Pallas kernels, up_back(): pl.pallas_call(functools.partial(up_back_kernel, copies=copies, size=size...  58.2 us
    pallas_call x1, Pallas kernels, down_part(): pl.pallas_call(functools.partial(down_kernel, seq=seq, steps=steps, tile=...  46.5 us
    ppermute x46, starting transfers between devices, send(): return lax.ppermute(array, AXES, pairs)  38.6 us
    pallas_call x1, Pallas kernels, up_part(): pl.pallas_call(functools.partial(up_kernel, copies=copies, size=size, chu...  26.5 us
    pallas_call x1, Pallas kernels, attend(): pl.pallas_call(functools.partial(attend_kernel, copies=copies, size=size,...  22.6 us
    pallas_call x1, Pallas kernels, token_part(): pl.pallas_call(functools.partial(token_kernel, copies=copies, size=size),...  16.1 us
    pallas_call x1, Pallas kernels, input_grad(): pl.pallas_call(functools.partial(input_grad_kernel, per=per), grid_spec=p...  15.6 us
  transfers between devices with their start and end apart: 54, of which 18 were waited for; matrix products, arithmetic and copies ran while one was open for 7% of the time, Pallas kernels for 42%

profile of v4, /device:TPU:0, one launch (start us, length us, event | category | flops | bytes accessed | tf_op | source)
XLA Modules:
  0.0 408.5 jit_solution(16845510732590564477)
XLA Ops:
  8.6 2.7 pack.1
  15.5 5.3 %pick.2 = (bf16[6,128,768]{2,1,0:T(8,128)(2,1)}, bf16[6,128,768]{2,1,0:T(8,128)(2,1)}, bf16[6,128,768]{2,1,0:T(8,128)(2,1)}) custom-call(s32[3,6]{1,0:T(4,128)} %select_reduce_fusion.4.table, bf16[16,128,768]{2,1,0:T(8,128)(2,1)} %refs_0_.3), custom_call_target="tpu_custom_call" | custom-call | bytes 2123366 | tf_op jit(solution)/shard_map/pick/pallas_call | solution.py:982
  21.0 2.8 collective-permute-start.1
  24.9 2.1 collective-permute-start.3
  28.0 2.1 collective-permute-done.1
  30.1 10.2 %collective-permute-done.2 = bf16[48,1280]{1,0:T(8,128)(2,1)S(1)} collective-permute-done((bf16[48,1280]{1,0:T(8,128)(2,1)S(1)}, bf16[48,1280]{1,0:T(8,128)(2,1)S(1)}, u32[]{:S(2)}, u32[]{:S(2)}) %collective-permute-start.2) | collective-permute-done | bytes 122912 | tf_op jit(solution)/shard_map/ppermute | solution.py:1104
  40.4 1.7 collective-permute-start.6
  46.7 9.0 %collective-permute-done.6.refs_3_.refs_4_ = bf16[192,1280]{1,0:T(8,128)(2,1)S(1)} collective-permute-done((bf16[192,1280]{1,0:T(8,128)(2,1)S(1)}, bf16[192,1280]{1,0:T(8,128)(2,1)S(1)}, u32[]{:S(2)}, u32[]{:S(2)}) %collective-permute-start.6) | collective-permute-done | bytes 491552 | tf_op jit(solution)/shard_map/ppermute | solution.py:1104
  55.7 1.5 collective-permute-start.8
  57.2 3.2 collective-permute-done.5.refs_2_.refs_3_
  60.6 6.1 %collective-permute-done.16 = bf16[48,1920]{1,0:T(8,128)(2,1)S(1)} collective-permute-done((bf16[48,1920]{1,0:T(8,128)(2,1)S(1)}, bf16[48,1920]{1,0:T(8,128)(2,1)S(1)}, u32[]{:S(2)}, u32[]{:S(2)}) %collective-permute-start.16) | collective-permute-done | bytes 184352 | tf_op jit(solution)/shard_map/ppermute | solution.py:1104
  72.4 1.4 collective-permute-start.18
  73.9 22.6 %attend.1 = (bf16[2048,2304]{1,0:T(8,128)(2,1)}, bf16[16,6,128,256]{3,2,1,0:T(8,128)(2,1)}, bf16[2048,768]{1,0:T(8,128)(2,1)}, bf16[768,2048]{1,0:T(8,128)(2,1)}...) custom-call(s32[16]{0:T(128)} %lens.3, ...), custom_call_target="tpu_custom_call" | custom-call | flops 4348654592 | bytes 9000000 | tf_op jit(solution)/shard_map/attend/pallas_call | solution.py:283
  98.8 7.5 %collective-permute-done.22.refs_8_.refs_13_ = bf16[192,896]{1,0:T(8,128)(2,1)} collective-permute-done((bf16[192,896]{1,0:T(8,128)(2,1)S(1)}, bf16[192,896]{1,0:T(8,128)(2,1)}, u32[]{:S(2)}, u32[]{:S(2)}) %collective-permute-start.22) | collective-permute-done | bytes 344096 | tf_op jit(solution)/shard_map/ppermute | solution.py:1104
  107.4 1.5 collective-permute-start.27
  113.4 26.5 %up_part.1 = (f32[2048,768]{1,0:T(8,128)}, f32[2048,128]{1,0:T(8,128)}, bf16[2048,768]{1,0:T(8,128)(2,1)}, bf16[2048,3072]{1,0:T(8,128)(2,1)}, bf16[2048,3072]{1,0:T(8,128)(2,1)}) custom-call(s32[4]{0:T(128)} %pad_add_fusion.here, bf16[2048,768]{1,0:T(8,128)(2,1)} %get-tuple-element.169.refs_0_.refs_6_, bf16[2048,768]{1,0:T(8,128)(2,1)} %bitcast.160, ...), custom_call_target="tpu_custom_call" | custom-call | flops 7247757312 | bytes 15000000 | tf_op jit(solution)/shard_map/up_part/pallas_call | solution.py:357
  139.9 7.7 %collective-permute-done.28.refs_3_ = bf16[6,128,768]{2,1,0:T(8,128)(2,1)} collective-permute-done((bf16[6,128,768]{2,1,0:T(8,128)(2,1)}, bf16[6,128,768]{2,1,0:T(8,128)(2,1)}, u32[]{:S(2)}, u32[]{:S(2)}) %collective-permute-start.28) | collective-permute-done | bytes 1179680 | tf_op jit(solution)/shard_map/ppermute | solution.py:1281
  147.7 3.8 place.2
  151.5 46.5 %down_part.1 = (bf16[2048,768]{1,0:T(8,128)(2,1)}, f32[2048,768]{1,0:T(8,128)}, bf16[2048,768]{1,0:T(8,128)(2,1)}, f32[32,128]{1,0:T(8,128)}, f32[8,768]{1,0:T(8...) custom-call(s32[16]{0:T(128)} %lens.3, ...), custom_call_target="tpu_custom_call" | custom-call | flops 11596411904 | bytes 18000000 | tf_op jit(solution)/shard_map/down_part/pallas_call | solution.py:530
  198.1 4.7 %pick.3 = (bf16[6,128,768]{2,1,0:T(8,128)(2,1)}, bf16[6,128,768]{2,1,0:T(8,128)(2,1)}, bf16[6,128,768]{2,1,0:T(8,128)(2,1)}) custom-call(s32[3,6]{1,0:T(4,128)} %select_reduce_fusion.3.table, bf16[16,128,768]{2,1,0:T(8,128)(2,1)} %bitcast.139), custom_call_target="tpu_custom_call" | custom-call | bytes 2123366 | tf_op jit(solution)/shard_map/pick/pallas_call | solution.py:982
  203.7 1.5 collective-permute-start.30
  205.4 58.2 %up_back.1 = (f32[2048,768]{1,0:T(8,128)}, bf16[2048,768]{1,0:T(8,128)(2,1)}, f32[8,768]{1,0:T(8,128)}, f32[8,3072]{1,0:T(8,128)}, bf16[768,1536]{1,0:T(8,128)(2...) custom-call(s32[4]{0:T(128)} %pad_add_fusion.here, ...), custom_call_target="tpu_custom_call" | custom-call | flops 11596411904 | bytes 18000000 | tf_op jit(solution)/shard_map/up_back/pallas_call | solution.py:671
  264.4 5.3 %collective-permute-done.32 = bf16[768,384]{1,0:T(8,128)(2,1)} collective-permute-done((bf16[768,384]{1,0:T(8,128)(2,1)}, bf16[768,384]{1,0:T(8,128)(2,1)}, u32[]{:S(2)}, u32[]{:S(2)}) %collective-permute-start.32) | collective-permute-done | bytes 589856 | tf_op jit(solution)/shard_map/ppermute | solution.py:1104
  269.6 1.4 convert_add_fusion.2
  271.0 2.4 convert_add_fusion
  275.2 1.4 copy-done
  278.5 14.5 %attend_back.1 = (bf16[2048,2304]{1,0:T(8,128)(2,1)}, f32[8,768]{1,0:T(8,128)}) custom-call(bf16[2048,768]{1,0:T(8,128)(2,1)} %get-tuple-element.209.mcot_ref, bf16[2048,2304]{1,0:T(8,128)(2,1)} %get-tuple-element.210.qkv_ref, bf16[16,6,128,256]{3,2,1,0:T(8,128)(2,1)} %get-tuple-element.211.prob_ref), custom_call_target="tpu_custom_call" | custom-call | flops 4348654592 | bytes 9000000 | tf_op jit(solution)/shard_map/attend_back/pallas_call | solution.py:827
  293.0 4.4 %collective-permute-done.35 = bf16[2,4,48,896]{3,2,1,0:T(8,128)(2,1)} collective-permute-done((bf16[2,4,48,896]{3,2,1,0:T(8,128)(2,1)}, bf16[2,4,48,896]{3,2,1,0:T(8,128)(2,1)}, u32[]{:S(2)}, u32[]{:S(2)}) %collective-permute-start.35) | collective-permute-done | bytes 688160 | tf_op jit(solution)/shard_map/ppermute | solution.py:1104
  297.4 3.5 collective-permute-done.34
  304.1 1.9 fusion
  308.6 3.3 small_pieces.1
  311.9 15.6 %input_grad.1 = (bf16[768,1152]{1,0:T(8,128)(2,1)}, bf16[768,1152]{1,0:T(8,128)(2,1)}) custom-call(s32[4]{0:T(128)} %pad_add_fusion.here, bf16[768,2048]{1,0:T(8,128)(2,1)} %get-tuple-element.217.turned_ref, bf16[2048,2304]{1,0:T(8,128)(2,1)} %get-tuple-element.243.pcot_ref.refs_0_), custom_call_target="tpu_custom_call" | custom-call | flops 2174327296 | bytes 6000000 | tf_op jit(solution)/shard_map/input_grad/pallas_call | solution.py:756
  330.7 1.6 convert_element_type.201
  332.3 4.0 place.3
  338.5 1.8 convert_add_fusion.1
  343.7 1.4 collective-permute-start.40
  346.8 2.9 collective-permute-start.44
  350.1 1.7 collective-permute-start.42
  351.7 16.1 %token_part.1 = f32[2048,768]{1,0:T(8,128)} custom-call(s32[4]{0:T(128)} %pad_add_fusion.here, bf16[2048,2304]{1,0:T(8,128)(2,1)} %get-tuple-element.243.pcot_ref.refs_0_, f32[2048,768]{1,0:T(8,128)} %get-tuple-element.244.refs_1_, bf16[192,1280]{1,0:T(8,128)(2,1)} %copy-done.18, bf16[192,1280]{1,0:T(8,128)(2,1)} %copy-done.16, ...), custom_call_target="tpu_custom_call" | custom-call | flops 2174327296 | bytes 7500000 | tf_op jit(solution)/shard_map/token_part/pallas_call | solution.py:871
  367.9 1.5 bitcast_add_fusion.1
  371.8 1.5 collective-permute-start.46
  374.5 5.8 %collective-permute-done.46 = bf16[4,48,640]{2,1,0:T(8,128)(2,1)S(1)} collective-permute-done((bf16[4,48,640]{2,1,0:T(8,128)(2,1)S(1)}, bf16[4,48,640]{2,1,0:T(8,128)(2,1)S(1)}, u32[]{:S(2)}, u32[]{:S(2)}) %collective-permute-start.46) | collective-permute-done | bytes 245792 | tf_op jit(solution)/shard_map/ppermute | solution.py:1104
  381.6 1.5 collective-permute-start.47
  383.1 2.4 collective-permute-start.49
  386.2 3.5 collective-permute-done.47
  390.6 4.5 %collective-permute-done.48 = bf16[48,1280]{1,0:T(8,128)(2,1)S(1)} collective-permute-done((bf16[48,1280]{1,0:T(8,128)(2,1)S(1)}, bf16[48,1280]{1,0:T(8,128)(2,1)S(1)}, u32[]{:S(2)}, u32[]{:S(2)}) %collective-permute-start.48) | collective-permute-done | bytes 122912 | tf_op jit(solution)/shard_map/ppermute | solution.py:1104
  397.8 1.4 finish.1
  399.9 1.3 pad_maximum_fusion.9
  (247 shorter events, 58.0 us)
Async XLA Ops:
  7.2 144.3 %all-gather.2.cloned.1.call-start = ((), (), s32[]{:S(2)}) async-start(), calls=%async_computation.1 | async-start | bytes 4866048 | tf_op jit(solution)/shard_map/all_gather | solution.py:1355
  7.9 319.7 %reduce-scatter.2.cloned.1.call-start = ((), (), s32[]{:S(2)}) async-start(), calls=%async_computation.2 | async-start | bytes 4866048 | tf_op jit(solution)/shard_map/reduce_scatter | solution.py:1412
  11.3 9.7 %collective-permute-start = (bf16[24,1280]{1,0:T(8,128)(2,1)}, bf16[24,1280]{1,0:T(8,128)(2,1)S(1)}, u32[]{:S(2)}, u32[]{:S(2)}) collective-permute-start(bf16[24,1280]{1,0:T(8,128)(2,1)} %get-tuple-element.148), channel_id=1, source_target_pairs={{0,1},{1,0},{2,3},{3,2},{4,5},{5,4},{6,7},{7,6},{8,9},{9,8},{10,11... | collective-permute-start | bytes 184328 | tf_op jit(solution)/shard_map/ppermute | solution.py:1104
  20.8 19.5 %collective-permute-start.4 = (bf16[6,128,768]{2,1,0:T(8,128)(2,1)}, bf16[6,128,768]{2,1,0:T(8,128)(2,1)S(1)}, u32[]{:S(2)}, u32[]{:S(2)}) collective-permute-start(bf16[6,128,768]{2,1,0:T(8,128)(2,1)} %get-tuple-element.151), channel_id=1, source_target_pairs={{0,1},{1,2},{2,3},{3,0},{4,5},{5,6},{6,7},{7,4},{8,9},{9,10},{10,1... | collective-permute-start | bytes 3538952 | tf_op jit(solution)/shard_map/ppermute | solution.py:1281
  21.0 9.1 %collective-permute-start.1 = (bf16[48,1280]{1,0:T(8,128)(2,1)S(1)}, bf16[48,1280]{1,0:T(8,128)(2,1)S(1)}, u32[]{:S(2)}, u32[]{:S(2)}) collective-permute-start(bf16[48,1280]{1,0:T(8,128)(2,1)S(1)} %pad_maximum_fusion.7), channel_id=1, source_target_pairs={{0,8},{1,9},{2,10},{3,11},{4,12},{5,13},{6,14},{7,15},{8,16},{9,17... | collective-permute-start | bytes 368648 | tf_op jit(solution)/shard_map/ppermute | solution.py:1104
  23.9 19.4 %collective-permute-start.14 = (bf16[24,1920]{1,0:T(8,128)(2,1)S(1)}, bf16[24,1920]{1,0:T(8,128)(2,1)S(1)}, u32[]{:S(2)}, u32[]{:S(2)}) collective-permute-start(bf16[24,1920]{1,0:T(8,128)(2,1)S(1)} %copy-done.33), channel_id=1, source_target_pairs={{0,1},{1,0},{2,3},{3,2},{4,5},{5,4},{6,7},{7,6},{8,9},{9,8},{10,11... | collective-permute-start | bytes 276488 | tf_op jit(solution)/shard_map/ppermute | solution.py:1104
  24.9 15.4 %collective-permute-start.3 = (bf16[48,1280]{1,0:T(8,128)(2,1)S(1)}, bf16[48,1280]{1,0:T(8,128)(2,1)S(1)}, u32[]{:S(2)}, u32[]{:S(2)}) collective-permute-start(bf16[48,1280]{1,0:T(8,128)(2,1)S(1)} %pad_maximum_fusion.7), channel_id=1, source_target_pairs={{0,24},{1,25},{2,26},{3,27},{4,28},{5,29},{6,30},{7,31},{8,0},{9,1... | collective-permute-start | bytes 368648 | tf_op jit(solution)/shard_map/ppermute | solution.py:1104
  27.0 13.3 %collective-permute-start.2 = (bf16[48,1280]{1,0:T(8,128)(2,1)S(1)}, bf16[48,1280]{1,0:T(8,128)(2,1)S(1)}, u32[]{:S(2)}, u32[]{:S(2)}) collective-permute-start(bf16[48,1280]{1,0:T(8,128)(2,1)S(1)} %pad_maximum_fusion.7), channel_id=1, source_target_pairs={{0,16},{1,17},{2,18},{3,19},{4,20},{5,21},{6,22},{7,23},{8,24},{9,... | collective-permute-start | bytes 368648 | tf_op jit(solution)/shard_map/ppermute | solution.py:1104
  40.4 15.3 %collective-permute-start.6 = (bf16[192,1280]{1,0:T(8,128)(2,1)S(1)}, bf16[192,1280]{1,0:T(8,128)(2,1)S(1)}, u32[]{:S(2)}, u32[]{:S(2)}) collective-permute-start(bf16[192,1280]{1,0:T(8,128)(2,1)S(1)} %constant_dynamic-update-slice_fusion.refs_1_.refs_2_), channel_id=1, source_target_pairs={{0,4},{1,5},{2,6},{3,7},{4,0},{5,1},{6,2},{7,3},{8,12},{9,13},{10,... | collective-permute-start | bytes 1474568 | tf_op jit(solution)/shard_map/ppermute | solution.py:1104
  42.0 18.3 %collective-permute-start.5 = (bf16[192,1280]{1,0:T(8,128)(2,1)S(1)}, bf16[192,1280]{1,0:T(8,128)(2,1)S(1)}, u32[]{:S(2)}, u32[]{:S(2)}) collective-permute-start(bf16[192,1280]{1,0:T(8,128)(2,1)S(1)} %constant_dynamic-update-slice_fusion.refs_1_.refs_2_), channel_id=1, source_target_pairs={{0,2},{1,3},{2,0},{3,1},{4,6},{5,7},{6,4},{7,5},{8,10},{9,11},{10,... | collective-permute-start | bytes 1474568 | tf_op jit(solution)/shard_map/ppermute | solution.py:1104
  44.6 15.9 %collective-permute-start.17 = (bf16[48,1920]{1,0:T(8,128)(2,1)S(1)}, bf16[48,1920]{1,0:T(8,128)(2,1)S(1)}, u32[]{:S(2)}, u32[]{:S(2)}) collective-permute-start(bf16[48,1920]{1,0:T(8,128)(2,1)S(1)} %pad_maximum_fusion.6), channel_id=1, source_target_pairs={{0,24},{1,25},{2,26},{3,27},{4,28},{5,29},{6,30},{7,31},{8,0},{9,1... | collective-permute-start | bytes 552968 | tf_op jit(solution)/shard_map/ppermute | solution.py:1104
  45.9 20.8 %collective-permute-start.16 = (bf16[48,1920]{1,0:T(8,128)(2,1)S(1)}, bf16[48,1920]{1,0:T(8,128)(2,1)S(1)}, u32[]{:S(2)}, u32[]{:S(2)}) collective-permute-start(bf16[48,1920]{1,0:T(8,128)(2,1)S(1)} %pad_maximum_fusion.6), channel_id=1, source_target_pairs={{0,16},{1,17},{2,18},{3,19},{4,20},{5,21},{6,22},{7,23},{8,24},{9,... | collective-permute-start | bytes 552968 | tf_op jit(solution)/shard_map/ppermute | solution.py:1104
  45.9 20.8 %collective-permute-start.15 = (bf16[48,1920]{1,0:T(8,128)(2,1)S(1)}, bf16[48,1920]{1,0:T(8,128)(2,1)S(1)}, u32[]{:S(2)}, u32[]{:S(2)}) collective-permute-start(bf16[48,1920]{1,0:T(8,128)(2,1)S(1)} %pad_maximum_fusion.6), channel_id=1, source_target_pairs={{0,8},{1,9},{2,10},{3,11},{4,12},{5,13},{6,14},{7,15},{8,16},{9,17... | collective-permute-start | bytes 552968 | tf_op jit(solution)/shard_map/ppermute | solution.py:1104
  55.7 12.2 %collective-permute-start.8 = (bf16[192,640]{1,0:T(8,128)(2,1)S(1)}, bf16[192,640]{1,0:T(8,128)(2,1)S(1)}, u32[]{:S(2)}, u32[]{:S(2)}) collective-permute-start(bf16[192,640]{1,0:T(8,128)(2,1)S(1)} %slice.159), channel_id=1, source_target_pairs={{0,2},{1,3},{2,0},{3,1},{4,6},{5,7},{6,4},{7,5},{8,10},{9,11},{10,... | collective-permute-start | bytes 737288 | tf_op jit(solution)/shard_map/ppermute | solution.py:1104
  60.4 7.5 %collective-permute-start.7 = (bf16[192,640]{1,0:T(8,128)(2,1)S(1)}, bf16[192,640]{1,0:T(8,128)(2,1)S(1)}, u32[]{:S(2)}, u32[]{:S(2)}) collective-permute-start(bf16[192,640]{1,0:T(8,128)(2,1)S(1)} %slice.158), channel_id=1, source_target_pairs={{0,4},{1,5},{2,6},{3,7},{4,0},{5,1},{6,2},{7,3},{8,12},{9,13},{10,... | collective-permute-start | bytes 737288 | tf_op jit(solution)/shard_map/ppermute | solution.py:1104
  60.5 9.3 %collective-permute-start.9 = (bf16[192,1280]{1,0:T(8,128)(2,1)S(1)}, bf16[192,1280]{1,0:T(8,128)(2,1)S(1)}, u32[]{:S(2)}, u32[]{:S(2)}) collective-permute-start(bf16[192,1280]{1,0:T(8,128)(2,1)S(1)} %constant_dynamic-update-slice_fusion.refs_1_.refs_2_), channel_id=1, source_target_pairs={{0,1},{1,0},{2,3},{3,2},{4,5},{5,4},{6,7},{7,6},{8,9},{9,8},{10,11... | collective-permute-start | bytes 1474568 | tf_op jit(solution)/shard_map/ppermute | solution.py:1104
  66.7 3.3 collective-permute-start.11
  71.0 25.5 %collective-permute-start.20 = (bf16[192,1920]{1,0:T(8,128)(2,1)}, bf16[192,1920]{1,0:T(8,128)(2,1)}, u32[]{:S(2)}, u32[]{:S(2)}) collective-permute-start(bf16[192,1920]{1,0:T(8,128)(2,1)} %constant_dynamic-update-slice_fusion.5.refs_4_.refs_9_), channel_id=1, source_target_pairs={{0,1},{1,0},{2,3},{3,2},{4,5},{5,4},{6,7},{7,6},{8,9},{9,8},{10,11... | collective-permute-start | bytes 2211848 | tf_op jit(solution)/shard_map/ppermute | solution.py:1104
  71.8 24.8 %collective-permute-start.19 = (bf16[192,1920]{1,0:T(8,128)(2,1)}, bf16[192,1920]{1,0:T(8,128)(2,1)S(1)}, u32[]{:S(2)}, u32[]{:S(2)}) collective-permute-start(bf16[192,1920]{1,0:T(8,128)(2,1)} %constant_dynamic-update-slice_fusion.5.refs_4_.refs_9_), channel_id=1, source_target_pairs={{0,4},{1,5},{2,6},{3,7},{4,0},{5,1},{6,2},{7,3},{8,12},{9,13},{10,... | collective-permute-start | bytes 2211848 | tf_op jit(solution)/shard_map/ppermute | solution.py:1104
  72.4 24.1 %collective-permute-start.18 = (bf16[192,1920]{1,0:T(8,128)(2,1)}, bf16[192,1920]{1,0:T(8,128)(2,1)S(1)}, u32[]{:S(2)}, u32[]{:S(2)}) collective-permute-start(bf16[192,1920]{1,0:T(8,128)(2,1)} %constant_dynamic-update-slice_fusion.5.refs_4_.refs_9_), channel_id=1, source_target_pairs={{0,2},{1,3},{2,0},{3,1},{4,6},{5,7},{6,4},{7,5},{8,10},{9,11},{10,... | collective-permute-start | bytes 2211848 | tf_op jit(solution)/shard_map/ppermute | solution.py:1104
  96.6 9.7 %collective-permute-start.22 = (bf16[192,896]{1,0:T(8,128)(2,1)S(1)}, bf16[192,896]{1,0:T(8,128)(2,1)}, u32[]{:S(2)}, u32[]{:S(2)}) collective-permute-start(bf16[192,896]{1,0:T(8,128)(2,1)S(1)} %slice.122), channel_id=1, source_target_pairs={{0,2},{1,3},{2,0},{3,1},{4,6},{5,7},{6,4},{7,5},{8,10},{9,11},{10,... | collective-permute-start | bytes 1032200 | tf_op jit(solution)/shard_map/ppermute | solution.py:1104
  97.9 11.0 %collective-permute-start.21 = (bf16[192,1024]{1,0:T(8,128)(2,1)S(1)}, bf16[192,1024]{1,0:T(8,128)(2,1)}, u32[]{:S(2)}, u32[]{:S(2)}) collective-permute-start(bf16[192,1024]{1,0:T(8,128)(2,1)S(1)} %slice.121), channel_id=1, source_target_pairs={{0,4},{1,5},{2,6},{3,7},{4,0},{5,1},{6,2},{7,3},{8,12},{9,13},{10,... | collective-permute-start | bytes 1179656 | tf_op jit(solution)/shard_map/ppermute | solution.py:1104
  106.3 6.0 %collective-permute-start.23 = (bf16[192,1920]{1,0:T(8,128)(2,1)S(1)}, bf16[192,1920]{1,0:T(8,128)(2,1)S(1)}, u32[]{:S(2)}, u32[]{:S(2)}) collective-permute-start(bf16[192,1920]{1,0:T(8,128)(2,1)S(1)} %collective-permute-done.18.refs_5_.refs_10_), channel_id=1, source_target_pairs={{0,1},{1,0},{2,3},{3,2},{4,5},{5,4},{6,7},{7,6},{8,9},{9,8},{10,11... | collective-permute-start | bytes 2211848 | tf_op jit(solution)/shard_map/ppermute | solution.py:1104
  106.8 5.5 %collective-permute-start.24 = (bf16[192,1920]{1,0:T(8,128)(2,1)S(1)}, bf16[192,1920]{1,0:T(8,128)(2,1)}, u32[]{:S(2)}, u32[]{:S(2)}) collective-permute-start(bf16[192,1920]{1,0:T(8,128)(2,1)S(1)} %collective-permute-done.19.refs_6_.refs_11_), channel_id=1, source_target_pairs={{0,1},{1,0},{2,3},{3,2},{4,5},{5,4},{6,7},{7,6},{8,9},{9,8},{10,11... | collective-permute-start | bytes 2211848 | tf_op jit(solution)/shard_map/ppermute | solution.py:1104
  107.4 32.5 %collective-permute-start.27 = (bf16[6,128,768]{2,1,0:T(8,128)(2,1)}, bf16[6,128,768]{2,1,0:T(8,128)(2,1)S(1)}, u32[]{:S(2)}, u32[]{:S(2)}) collective-permute-start(bf16[6,128,768]{2,1,0:T(8,128)(2,1)} %get-tuple-element.177), channel_id=1, source_target_pairs={{0,2},{1,3},{2,0},{3,1},{4,6},{5,7},{6,4},{7,5},{8,10},{9,11},{10,... | collective-permute-start | bytes 3538952 | tf_op jit(solution)/shard_map/ppermute | solution.py:1281
  108.9 38.8 %collective-permute-start.28 = (bf16[6,128,768]{2,1,0:T(8,128)(2,1)}, bf16[6,128,768]{2,1,0:T(8,128)(2,1)}, u32[]{:S(2)}, u32[]{:S(2)}) collective-permute-start(bf16[6,128,768]{2,1,0:T(8,128)(2,1)} %get-tuple-element.178), channel_id=1, source_target_pairs={{0,3},{1,0},{2,1},{3,2},{4,7},{5,4},{6,5},{7,6},{8,11},{9,8},{10,9... | collective-permute-start | bytes 3538952 | tf_op jit(solution)/shard_map/ppermute | solution.py:1281
  109.4 3.4 collective-permute-start.25
  202.8 60.9 %collective-permute-start.29 = (bf16[6,128,768]{2,1,0:T(8,128)(2,1)}, bf16[6,128,768]{2,1,0:T(8,128)(2,1)S(1)}, u32[]{:S(2)}, u32[]{:S(2)}) collective-permute-start(bf16[6,128,768]{2,1,0:T(8,128)(2,1)} %get-tuple-element.201), channel_id=1, source_target_pairs={{0,1},{1,2},{2,3},{3,0},{4,5},{5,6},{6,7},{7,4},{8,9},{9,10},{10,1... | collective-permute-start | bytes 3538952 | tf_op jit(solution)/shard_map/ppermute | solution.py:1281
  203.7 60.0 %collective-permute-start.30 = (bf16[6,128,768]{2,1,0:T(8,128)(2,1)}, bf16[6,128,768]{2,1,0:T(8,128)(2,1)}, u32[]{:S(2)}, u32[]{:S(2)}) collective-permute-start(bf16[6,128,768]{2,1,0:T(8,128)(2,1)} %get-tuple-element.202), channel_id=1, source_target_pairs={{0,2},{1,3},{2,0},{3,1},{4,6},{5,7},{6,4},{7,5},{8,10},{9,11},{10,... | collective-permute-start | bytes 3538952 | tf_op jit(solution)/shard_map/ppermute | solution.py:1281
  205.2 58.5 %collective-permute-start.31 = (bf16[6,128,768]{2,1,0:T(8,128)(2,1)}, bf16[6,128,768]{2,1,0:T(8,128)(2,1)}, u32[]{:S(2)}, u32[]{:S(2)}) collective-permute-start(bf16[6,128,768]{2,1,0:T(8,128)(2,1)} %get-tuple-element.203), channel_id=1, source_target_pairs={{0,3},{1,0},{2,1},{3,2},{4,7},{5,4},{6,5},{7,6},{8,11},{9,8},{10,9... | collective-permute-start | bytes 3538952 | tf_op jit(solution)/shard_map/ppermute | solution.py:1281
  263.7 7.3 %collective-permute-start.33 = (bf16[768,1536]{1,0:T(8,128)(2,1)}, bf16[768,1536]{1,0:T(8,128)(2,1)}, u32[]{:S(2)}, u32[]{:S(2)}) collective-permute-start(bf16[768,1536]{1,0:T(8,128)(2,1)} %get-tuple-element.208), channel_id=1, source_target_pairs={{0,1},{1,0},{2,3},{3,2},{4,5},{5,4},{6,7},{7,6},{8,9},{9,8},{10,11... | collective-permute-start | bytes 7077896 | tf_op jit(solution)/shard_map/ppermute | solution.py:1104
  264.3 5.3 %collective-permute-start.32 = (bf16[768,384]{1,0:T(8,128)(2,1)}, bf16[768,384]{1,0:T(8,128)(2,1)}, u32[]{:S(2)}, u32[]{:S(2)}) collective-permute-start(bf16[768,384]{1,0:T(8,128)(2,1)} %get-tuple-element.206), channel_id=1, source_target_pairs={{0,1},{1,0},{2,3},{3,2},{4,5},{5,4},{6,7},{7,6},{8,9},{9,8},{10,11... | collective-permute-start | bytes 1769480 | tf_op jit(solution)/shard_map/ppermute | solution.py:1104
  276.7 24.2 %collective-permute-start.34 = (bf16[4,2,48,1024]{3,2,0,1:T(8,128)(2,1)S(1)}, bf16[4,2,48,1024]{3,2,0,1:T(8,128)(2,1)}, u32[]{:S(2)}, u32[]{:S(2)}) collective-permute-start(bf16[4,2,48,1024]{3,2,0,1:T(8,128)(2,1)S(1)} %fusion.4), channel_id=1, source_target_pairs={{0,4},{1,5},{2,6},{3,7},{4,0},{5,1},{6,2},{7,3},{8,12},{9,13},{10,... | collective-permute-start | bytes 2359304 | tf_op jit(solution)/shard_map/ppermute | solution.py:1104
  277.8 19.6 %collective-permute-start.35 = (bf16[2,4,48,896]{3,2,1,0:T(8,128)(2,1)}, bf16[2,4,48,896]{3,2,1,0:T(8,128)(2,1)}, u32[]{:S(2)}, u32[]{:S(2)}) collective-permute-start(bf16[2,4,48,896]{3,2,1,0:T(8,128)(2,1)} %fusion.5), channel_id=1, source_target_pairs={{0,2},{1,3},{2,0},{3,1},{4,6},{5,7},{6,4},{7,5},{8,10},{9,11},{10,... | collective-permute-start | bytes 2064392 | tf_op jit(solution)/shard_map/ppermute | solution.py:1104
  303.3 24.3 %collective-permute-start.37 = (bf16[4,48,896]{2,1,0:T(8,128)(2,1)S(1)}, bf16[4,48,896]{2,1,0:T(8,128)(2,1)S(1)}, u32[]{:S(2)}, u32[]{:S(2)}) collective-permute-start(bf16[4,48,896]{2,1,0:T(8,128)(2,1)S(1)} %fusion.16), channel_id=1, source_target_pairs={{0,4},{1,5},{2,6},{3,7},{4,0},{5,1},{6,2},{7,3},{8,12},{9,13},{10,... | collective-permute-start | bytes 1032200 | tf_op jit(solution)/shard_map/ppermute | solution.py:1104
  306.1 21.5 %collective-permute-start.36 = (bf16[4,48,1024]{2,1,0:T(8,128)(2,1)S(1)}, bf16[4,48,1024]{2,1,0:T(8,128)(2,1)S(1)}, u32[]{:S(2)}, u32[]{:S(2)}) collective-permute-start(bf16[4,48,1024]{2,1,0:T(8,128)(2,1)S(1)} %fusion.10), channel_id=1, source_target_pairs={{0,2},{1,3},{2,0},{3,1},{4,6},{5,7},{6,4},{7,5},{8,10},{9,11},{10,... | collective-permute-start | bytes 1179656 | tf_op jit(solution)/shard_map/ppermute | solution.py:1104
  327.6 9.7 %collective-permute-start.38 = (bf16[768,1152]{1,0:T(8,128)(2,1)}, bf16[768,1152]{1,0:T(8,128)(2,1)}, u32[]{:S(2)}, u32[]{:S(2)}) collective-permute-start(bf16[768,1152]{1,0:T(8,128)(2,1)} %get-tuple-element.238), channel_id=1, source_target_pairs={{0,1},{1,0},{2,3},{3,2},{4,5},{5,4},{6,7},{7,6},{8,9},{9,8},{10,11... | collective-permute-start | bytes 5308424 | tf_op jit(solution)/shard_map/ppermute | solution.py:1104
  330.2 6.4 %collective-permute-start.39 = (bf16[768,128]{1,0:T(8,128)(2,1)}, bf16[768,128]{1,0:T(8,128)(2,1)S(1)}, u32[]{:S(2)}, u32[]{:S(2)}) collective-permute-start(bf16[768,128]{1,0:T(8,128)(2,1)} %get-tuple-element.240), channel_id=1, source_target_pairs={{0,1},{1,0},{2,3},{3,2},{4,5},{5,4},{6,7},{7,6},{8,9},{9,8},{10,11... | collective-permute-start | bytes 589832 | tf_op jit(solution)/shard_map/ppermute | solution.py:1104
  343.7 24.2 %collective-permute-start.40 = (bf16[4,2,48,640]{3,2,0,1:T(8,128)(2,1)}, bf16[4,2,48,640]{3,2,0,1:T(8,128)(2,1)}, u32[]{:S(2)}, u32[]{:S(2)}) collective-permute-start(bf16[4,2,48,640]{3,2,0,1:T(8,128)(2,1)} %fusion.8), channel_id=1, source_target_pairs={{0,4},{1,5},{2,6},{3,7},{4,0},{5,1},{6,2},{7,3},{8,12},{9,13},{10,... | collective-permute-start | bytes 1474568 | tf_op jit(solution)/shard_map/ppermute | solution.py:1104
  345.1 22.8 %collective-permute-start.41 = (bf16[2,4,48,640]{3,2,1,0:T(8,128)(2,1)}, bf16[2,4,48,640]{3,2,1,0:T(8,128)(2,1)}, u32[]{:S(2)}, u32[]{:S(2)}) collective-permute-start(bf16[2,4,48,640]{3,2,1,0:T(8,128)(2,1)} %fusion.7), channel_id=1, source_target_pairs={{0,2},{1,3},{2,0},{3,1},{4,6},{5,7},{6,4},{7,5},{8,10},{9,11},{10,... | collective-permute-start | bytes 1474568 | tf_op jit(solution)/shard_map/ppermute | solution.py:1104
  346.8 21.0 %collective-permute-start.44 = (bf16[48,1920]{1,0:T(8,128)(2,1)}, bf16[48,1920]{1,0:T(8,128)(2,1)S(1)}, u32[]{:S(2)}, u32[]{:S(2)}) collective-permute-start(bf16[48,1920]{1,0:T(8,128)(2,1)} %get-tuple-element.287), channel_id=1, source_target_pairs={{0,24},{1,25},{2,26},{3,27},{4,28},{5,29},{6,30},{7,31},{8,0},{9,1... | collective-permute-start | bytes 552968 | tf_op jit(solution)/shard_map/ppermute | solution.py:1104
  349.7 18.2 %collective-permute-start.43 = (bf16[48,1920]{1,0:T(8,128)(2,1)}, bf16[48,1920]{1,0:T(8,128)(2,1)}, u32[]{:S(2)}, u32[]{:S(2)}) collective-permute-start(bf16[48,1920]{1,0:T(8,128)(2,1)} %get-tuple-element.288), channel_id=1, source_target_pairs={{0,16},{1,17},{2,18},{3,19},{4,20},{5,21},{6,22},{7,23},{8,24},{9,... | collective-permute-start | bytes 552968 | tf_op jit(solution)/shard_map/ppermute | solution.py:1104
  350.1 17.8 %collective-permute-start.42 = (bf16[48,1920]{1,0:T(8,128)(2,1)}, bf16[48,1920]{1,0:T(8,128)(2,1)}, u32[]{:S(2)}, u32[]{:S(2)}) collective-permute-start(bf16[48,1920]{1,0:T(8,128)(2,1)} %get-tuple-element.289), channel_id=1, source_target_pairs={{0,8},{1,9},{2,10},{3,11},{4,12},{5,13},{6,14},{7,15},{8,16},{9,17... | collective-permute-start | bytes 552968 | tf_op jit(solution)/shard_map/ppermute | solution.py:1104
  371.8 8.4 %collective-permute-start.46 = (bf16[4,48,640]{2,1,0:T(8,128)(2,1)S(1)}, bf16[4,48,640]{2,1,0:T(8,128)(2,1)S(1)}, u32[]{:S(2)}, u32[]{:S(2)}) collective-permute-start(bf16[4,48,640]{2,1,0:T(8,128)(2,1)S(1)} %fusion.18), channel_id=1, source_target_pairs={{0,4},{1,5},{2,6},{3,7},{4,0},{5,1},{6,2},{7,3},{8,12},{9,13},{10,... | collective-permute-start | bytes 737288 | tf_op jit(solution)/shard_map/ppermute | solution.py:1104
  373.3 8.1 %collective-permute-start.45 = (bf16[4,48,640]{2,1,0:T(8,128)(2,1)S(1)}, bf16[4,48,640]{2,1,0:T(8,128)(2,1)S(1)}, u32[]{:S(2)}, u32[]{:S(2)}) collective-permute-start(bf16[4,48,640]{2,1,0:T(8,128)(2,1)S(1)} %fusion.17), channel_id=1, source_target_pairs={{0,2},{1,3},{2,0},{3,1},{4,6},{5,7},{6,4},{7,5},{8,10},{9,11},{10,... | collective-permute-start | bytes 737288 | tf_op jit(solution)/shard_map/ppermute | solution.py:1104
  381.6 8.1 %collective-permute-start.47 = (bf16[48,1280]{1,0:T(8,128)(2,1)S(1)}, bf16[48,1280]{1,0:T(8,128)(2,1)S(1)}, u32[]{:S(2)}, u32[]{:S(2)}) collective-permute-start(bf16[48,1280]{1,0:T(8,128)(2,1)S(1)} %get-tuple-element.290), channel_id=1, source_target_pairs={{0,8},{1,9},{2,10},{3,11},{4,12},{5,13},{6,14},{7,15},{8,16},{9,17... | collective-permute-start | bytes 368648 | tf_op jit(solution)/shard_map/ppermute | solution.py:1104
  383.1 7.5 %collective-permute-start.49 = (bf16[48,1280]{1,0:T(8,128)(2,1)S(1)}, bf16[48,1280]{1,0:T(8,128)(2,1)S(1)}, u32[]{:S(2)}, u32[]{:S(2)}) collective-permute-start(bf16[48,1280]{1,0:T(8,128)(2,1)S(1)} %get-tuple-element.291), channel_id=1, source_target_pairs={{0,24},{1,25},{2,26},{3,27},{4,28},{5,29},{6,30},{7,31},{8,0},{9,1... | collective-permute-start | bytes 368648 | tf_op jit(solution)/shard_map/ppermute | solution.py:1104
  385.5 9.6 %collective-permute-start.48 = (bf16[48,1280]{1,0:T(8,128)(2,1)S(1)}, bf16[48,1280]{1,0:T(8,128)(2,1)S(1)}, u32[]{:S(2)}, u32[]{:S(2)}) collective-permute-start(bf16[48,1280]{1,0:T(8,128)(2,1)S(1)} %get-tuple-element.292), channel_id=1, source_target_pairs={{0,16},{1,17},{2,18},{3,19},{4,20},{5,21},{6,22},{7,23},{8,24},{9,... | collective-permute-start | bytes 368648 | tf_op jit(solution)/shard_map/ppermute | solution.py:1104
  (42 other events, 391.6 us)
Sparse Core Ops, SparseCore 0:
  10.9 84.1 all-gather.1
  205.6 112.6 reduce-scatter.1
